TPU v7x, 32 devices: a whole 2x2x4 slice. The times are simulated.
32 devices in a mesh: row: 4 (over z), col: 8 (over y, x, core).
Axes of the slice: x: 2, y: 2, z: 4, core: 2. Of those that a mesh axis runs over, the one named last changes fastest.
Arguments:
- ancestor_inverse: float32 [16384, 16384], P('row', 'col'), may hold values from -6 to 6
- panel_one: bfloat16 [16384, 256], P(('row', 'col')), may hold values from -0.046875 to 0.046875
- panel_two: bfloat16 [16384, 256], P(('row', 'col')), may hold values from -0.046875 to 0.046875
- panel_three: bfloat16 [16384, 256], P(('row', 'col')), may hold values from -0.046875 to 0.046875
- couplings: bfloat16 [3, 256, 256], replicated, may hold values from -0.375 to 0.375
- diag_terms: float32 [3, 256, 256], replicated, may hold values from -6 to 6
- list_two: int32 [60], replicated, may hold values from 0 to 63, as said below
- list_three: int32 [56], replicated, may hold values from 0 to 63, as said below
Outputs:
- inverse_one: float32 [16384, 256], P(('row', 'col'))
- inverse_two: float32 [16384, 256], P(('row', 'col'))
- inverse_three: float32 [16384, 256], P(('row', 'col'))
- small_blocks: float32 [6, 256, 256], P(None, 'row', 'col')
Inputs may be any that keep to these rules, and one draw needn't show every extreme that they name: `list_two`: 60 distinct block indices in increasing order, always including 0 and 63. `list_three`: 56 distinct entries of list_two in increasing order, always including 0 and 63.
All inputs are finite; a program needn't handle non-finite values.
Results may differ from a plain program's by a relative error of at most 0.0003.
Values may be sent and summed in bfloat16 or wider, within the bound.
No kernel may reach another device: no remote copies, remote signals or barrier semaphores. Data moves between devices by JAX's collectives and lax.ppermute only.
A program may use at most 128 MiB of HBM per device.

v0:
```python
import jax
import jax.numpy as jnp
from jax import lax
from jax.sharding import PartitionSpec as P


def from_root(value, axis, source):
    kept = jnp.where(lax.axis_index(axis) == source, value, 0).astype(value.dtype)
    return lax.psum(kept, axis)


def product(former, latter):
    return jnp.dot(
        former, latter, precision=lax.Precision.HIGHEST, preferred_element_type=jnp.float32
    )


def inner_product(former, latter):
    return lax.dot_general(
        former,
        latter,
        (((0,), (0,)), ((), ())),
        precision=lax.Precision.HIGHEST,
        preferred_element_type=jnp.float32,
    )


def piece_keep(listed, start_row, slab_rows, block_width):
    rows_here = start_row + jnp.arange(slab_rows, dtype=jnp.int32)
    matches = (rows_here // block_width)[:, None] == listed[None, :]
    return jnp.any(matches, axis=1).astype(jnp.float32)[:, None]


def spread_joint(own_piece, local_cols):
    rows_all = lax.all_gather(own_piece, "col", axis=0, tiled=True)
    col_ratio = lax.axis_size("col") // lax.axis_size("row")
    col_id = lax.axis_index("col")
    own_part = lax.dynamic_slice_in_dim(rows_all, col_id % col_ratio * local_cols, local_cols, 0)
    return from_root(own_part, "row", col_id // col_ratio)


def body(
    ancestor_inverse, panel_one, panel_two, panel_three, couplings, diag_terms, list_two, list_three
):
    block_width = couplings.shape[1]
    slab_rows = panel_one.shape[0]
    local_cols = ancestor_inverse.shape[1]
    start_row = (lax.axis_index("row") * lax.axis_size("col") + lax.axis_index("col")) * slab_rows
    keep_two = piece_keep(list_two, start_row, slab_rows, block_width)
    keep_three = piece_keep(list_three, start_row, slab_rows, block_width)
    own_two = jnp.where(keep_two > 0.5, panel_two, jnp.zeros_like(panel_two))
    own_three = jnp.where(keep_three > 0.5, panel_three, jnp.zeros_like(panel_three))
    factor_one = panel_one.astype(jnp.float32)
    factor_two = own_two.astype(jnp.float32)
    factor_three = own_three.astype(jnp.float32)
    coupled = couplings.astype(jnp.float32)
    own_all = jnp.concatenate([panel_one, own_two, own_three], axis=1)
    cols_all = spread_joint(own_all, local_cols)
    partial_all = product(ancestor_inverse, cols_all.astype(jnp.float32))
    summed = lax.psum_scatter(partial_all, "col", scatter_dimension=0, tiled=True)
    sum_one = summed[:, :block_width]
    sum_two = summed[:, block_width : 2 * block_width]
    sum_three = summed[:, 2 * block_width :]
    blocks = (
        inner_product(factor_one, sum_one),
        inner_product(factor_two, sum_one),
        inner_product(factor_two, sum_two),
        inner_product(factor_three, sum_one),
        inner_product(factor_three, sum_two),
        inner_product(factor_three, sum_three),
    )
    m_oneone, m_twoone, m_twotwo, m_threeone, m_threetwo, m_threethree = lax.psum(
        (blocks[0], blocks[1], blocks[2], blocks[3], blocks[4], blocks[5]), ("row", "col")
    )
    inverse_one = -sum_one
    inverse_two = -(sum_two - product(sum_one, coupled[0])) * keep_two
    inverse_three = (
        -(sum_three + product(inverse_one, coupled[1]) + product(inverse_two, coupled[2]))
        * keep_three
    )
    diag_one = diag_terms[0] + m_oneone
    cross_two = m_twoone.T - product(diag_one, coupled[0])
    diag_two = (
        diag_terms[1]
        + m_twotwo
        - product(m_twoone, coupled[0])
        - inner_product(coupled[0], cross_two)
    )
    second_three = m_threetwo - product(m_threeone, coupled[0])
    cross_first = -(-m_threeone.T + product(diag_one, coupled[1]) + product(cross_two, coupled[2]))
    cross_second = -(
        -second_three.T + inner_product(cross_two, coupled[1]) + product(diag_two, coupled[2])
    )
    diag_three = (
        diag_terms[2]
        + m_threethree
        - product(m_threeone, coupled[1])
        - product(second_three, coupled[2])
        - inner_product(coupled[1], cross_first)
        - inner_product(coupled[2], cross_second)
    )
    stacked = jnp.stack([diag_one, diag_two, diag_three, cross_two, cross_first, cross_second])
    tile_rows = block_width // lax.axis_size("row")
    tile_cols = block_width // lax.axis_size("col")
    own_tile = lax.dynamic_slice(
        stacked,
        (0, lax.axis_index("row") * tile_rows, lax.axis_index("col") * tile_cols),
        (6, tile_rows, tile_cols),
    )
    return (inverse_one, inverse_two, inverse_three, own_tile)


def solution(mesh):
    in_specs = (
        P("row", "col"),
        P(("row", "col"), None),
        P(("row", "col"), None),
        P(("row", "col"), None),
        P(),
        P(),
        P(),
        P(),
    )
    out_specs = (
        P(("row", "col"), None),
        P(("row", "col"), None),
        P(("row", "col"), None),
        P(None, "row", "col"),
    )
    return jax.shard_map(body, mesh=mesh, in_specs=in_specs, out_specs=out_specs, check_vma=False)
```

profile of v0, /device:TPU:0, one launch (start us, length us, event | category | flops | bytes accessed | tf_op | source)
XLA Modules:
  0.0 484.6 jit_solution(16087073610636308880)
XLA Ops:
  7.2 0.8 compare_reduce_fusion.1
  8.0 0.8 compare_reduce_fusion
  8.8 1.2 broadcast_select_fusion
  10.0 1.9 pad_maximum_fusion
  12.0 48.3 %all-gather.2.cloned.1.call-done = bf16[4096,768]{1,0:T(8,128)(2,1)} async-done(((bf16[512,768]{1,0:T(8,128)(2,1)}), bf16[4096,768]{1,0:T(8,128)(2,1)}) %all-gather.2.cloned.1.call-update) | async-done | bytes 6291472 | tf_op jit(solution)/shard_map/all_gather | solution.py:35
  60.3 4.1 dynamic-slice_select_fusion
  64.5 121.2 %all-reduce.4.cloned.1.call-done = bf16[2048,768]{1,0:T(8,128)(2,1)} async-done(((bf16[2048,768]{1,0:T(8,128)(2,1)}), bf16[2048,768]{1,0:T(8,128)(2,1)}) %all-reduce.4.cloned.1.call-update) | async-done | bytes 3145744 | tf_op jit(solution)/shard_map/psum | solution.py:9
  185.7 50.6 %convolution_bitcast_fusion = f32[4096,768]{0,1:T(8,128)} fusion(bf16[2048,768]{1,0:T(8,128)(2,1)} %all-reduce.4.cloned.1.call-done, f32[4096,2048]{1,0:T(8,128)} %param.8), kind=kOutput, calls=%fused_computation | convolution fusion | flops 77309411328 | bytes 49283072 | tf_op jit(solution)/shard_map/dot_general | solution.py:13
  236.6 0.9 copy-done.8
  237.7 0.8 copy.40
  238.5 0.8 copy.41
  239.4 88.6 %reduce-scatter.2.cloned.1.call-done = f32[512,768]{0,1:T(8,128)} async-done(((f32[4096,768]{0,1:T(8,128)}), f32[512,768]{0,1:T(8,128)}) %reduce-scatter.2.cloned.1.call-update) | async-done | bytes 1572880 | tf_op jit(solution)/shard_map/reduce_scatter | solution.py:60
  328.0 2.3 fusion.11
  330.2 2.2 fusion.13
  332.4 1.1 fusion.15
  333.6 1.2 fusion.17
  334.8 1.2 fusion.19
  335.9 1.1 convolution_bitcast_fusion.4
  337.6 1.0 copy.32
  339.5 1.0 copy.33
  340.6 1.0 copy.31
  341.6 129.6 %all-reduce.6.cloned.1.call-done = (f32[256,256]{0,1:T(8,128)}, f32[256,256]{1,0:T(8,128)}, f32[256,256]{0,1:T(8,128)}, f32[256,256]{1,0:T(8,128)}, f32[256,256]{0,1:T(8,128)}, /*index=5*/f32[256,256]{1,0:T(8,128)}) async-done(((f32[256,256]{0,1:T(8,128)}, f32[256,256]{1,0:T(8,128)}, f32[256,256]{0,1:T(8,128)}, f32[256,256]{1,0:T(8,128)}, f32[256,256]{0,1:T(8,128)}, /*index=5*/f32[256,256]{1,0:T(8,128)}), ...) | async-done | bytes 1572880 | tf_op jit(solution)/shard_map/psum | solution.py:72
  471.2 1.1 bitcast_dynamic-update-slice_fusion.4
  472.3 1.4 convolution_add_fusion.5
  (55 shorter events, 6.3 us)
Async XLA Ops:
  7.2 53.2 %all-gather.2.cloned.1.call-start = ((), (), s32[]{:S(2)}) async-start(), calls=%async_computation.1 | async-start | bytes 7077888 | tf_op jit(solution)/shard_map/all_gather | solution.py:35
  11.9 173.8 %all-reduce.4.cloned.1.call-start = ((), (), s32[]{:S(2)}) async-start(), calls=%async_computation.2 | async-start | bytes 6291456 | tf_op jit(solution)/shard_map/psum | solution.py:9
  64.5 263.5 %reduce-scatter.2.cloned.1.call-start = ((), (), s32[]{:S(2)}) async-start(), calls=%async_computation.3 | async-start | bytes 14155776 | tf_op jit(solution)/shard_map/reduce_scatter | solution.py:60
  236.4 1.1 copy-start.8
  236.4 234.8 %all-reduce.6.cloned.1.call-start = ((), (), s32[]{:S(2)}) async-start(), calls=%async_computation.4 | async-start | bytes 3145728 | tf_op jit(solution)/shard_map/psum | solution.py:72
  328.0 4.5 copy-start
  332.4 3.5 copy-start.6
  335.9 1.1 copy-start.1
  471.2 2.5 copy-start.2
  471.2 2.5 copy-start.9
  471.2 2.8 copy-start.3
  471.2 2.8 copy-start.7
  473.9 1.1 copy-start.5
  473.9 1.1 copy-start.11
  474.6 1.0 copy-start.4
  474.6 1.1 copy-start.10
Sparse Core Ops, SparseCore 0:
  12.1 48.2 all-gather.1
  64.6 121.0 all-reduce.3
  236.5 91.4 reduce-scatter.1
  337.2 133.9 all-reduce.5
where the time goes:
time: 485 us
  waiting for transfers between devices  388 us (80%)
  matrix products  65.9 us (14%)
  between operations  14.1 us (3%)
  other arithmetic  9.95 us (2%)
  local copies, waits for them, and re-layouts  6.59 us (1%)
    psum x1, waiting for transfers between devices, body(): lax.psum((blocks[0], blocks[1], blocks[2], blocks[3], blocks[4], blocks[5...  130 us
    psum x1, waiting for transfers between devices, from_root(): return lax.psum(kept, axis)  121 us
    reduce_scatter x1, waiting for transfers between devices, body(): lax.psum_scatter(partial_all, 'col', scatter_dimension=0, tiled=True)  88.6 us
    dot_general x12, matrix products, product(): jnp.dot(former, latter, precision=lax.Precision.HIGHEST, preferred_elemen...  55.6 us
    all_gather x1, waiting for transfers between devices, spread_joint(): rows_all = lax.all_gather(own_piece, 'col', axis=0, tiled=True)  48.3 us
    dot_general x10, matrix products, inner_product(): lax.dot_general(former, latter, (((0,), (0,)), ((), ())), precision=lax.P...  10.2 us
  transfers between devices with their start and end apart: 4, of which 4 were waited for; matrix products, arithmetic and copies ran while one was open for 1% of the time, Pallas kernels for 0%

commit v1 on v0

v1 whole, which is shorter than its diff:
```python
import functools

import jax
import jax.numpy as jnp
from jax import lax
from jax.experimental import pallas as pl
from jax.experimental.pallas import tpu as pltpu
from jax.sharding import PartitionSpec as P

F32 = jnp.float32
BF16 = jnp.bfloat16


def product(former, latter):
    return jnp.dot(
        former, latter, precision=lax.Precision.HIGHEST, preferred_element_type=F32
    )


def inner_product(former, latter):
    return lax.dot_general(
        former,
        latter,
        (((0,), (0,)), ((), ())),
        precision=lax.Precision.HIGHEST,
        preferred_element_type=F32,
    )


def piece_keep(listed, start_row, slab_rows, block_width):
    rows_here = start_row + jnp.arange(slab_rows, dtype=jnp.int32)
    matches = (rows_here // block_width)[:, None] == listed[None, :]
    return jnp.any(matches, axis=1).astype(F32)[:, None]


def spread_panel(own, rows, cols):
    ratio = cols // rows
    received = []
    for step in range(rows):
        pairs = []
        for plane in range(rows):
            for place in range(cols):
                target = ((place % rows) ^ step) * cols + plane * ratio + place // rows
                pairs.append((plane * cols + place, target))
        received.append(lax.ppermute(own, ("row", "col"), pairs))
    return received


def multiply_kernel(where, s_ref, *refs):
    pieces, out_ref, panel = refs[:-2], refs[-2], refs[-1]
    depth = pieces[0].shape[0]

    @pl.when((pl.program_id(0) == 0) & (pl.program_id(1) == 0))
    def _():
        for step, piece in enumerate(pieces):
            begin = pl.multiple_of((where[0] ^ step) * depth, depth)
            panel[pl.ds(begin, depth), :] = piece[...]

    whole = s_ref[...]
    high = whole.astype(BF16)
    low = (whole - high.astype(F32)).astype(BF16)
    factor = panel[...]
    out_ref[0] = jnp.dot(high, factor, preferred_element_type=F32) + jnp.dot(
        low, factor, preferred_element_type=F32
    )


def multiply(where, ancestor, pieces, slab_rows):
    local_rows, local_cols = ancestor.shape
    width = pieces[0].shape[1]
    chips = local_rows // slab_rows // 2
    tile = min(256, slab_rows)
    tiles = slab_rows // tile
    grid_spec = pltpu.PrefetchScalarGridSpec(
        num_scalar_prefetch=1,
        grid=(chips, tiles),
        in_specs=[
            pl.BlockSpec(
                (tile, local_cols), lambda i, j, where: ((2 * i + where[1]) * tiles + j, 0)
            )
        ]
        + [pl.BlockSpec(piece.shape, lambda i, j, where: (0, 0)) for piece in pieces],
        out_specs=pl.BlockSpec((1, tile, width), lambda i, j, where: (i, j, 0)),
        scratch_shapes=[pltpu.VMEM((local_cols, width), BF16)],
    )
    flops = 2 * 2 * chips * slab_rows * local_cols * width
    return pl.pallas_call(
        multiply_kernel,
        grid_spec=grid_spec,
        out_shape=jax.ShapeDtypeStruct((chips, slab_rows, width), F32),
        compiler_params=pltpu.CompilerParams(vmem_limit_bytes=28 * 1024 * 1024),
        cost_estimate=pl.CostEstimate(
            flops=flops,
            bytes_accessed=4 * chips * slab_rows * (local_cols + width),
            transcendentals=0,
        ),
    )(where, ancestor, *pieces)


def sibling(value, cols):
    return lax.ppermute(value, "col", [(c, c ^ 1) for c in range(cols)])


def to_chip(value, step, cols):
    return lax.ppermute(value, "col", [(c, c ^ (2 * step)) for c in range(cols)])


def take(pieces, index):
    return lax.dynamic_index_in_dim(pieces, index, 0, keepdims=False)


def chip_scatter(summed, cols):
    chip = lax.axis_index("col") // 2
    total = take(summed, chip)
    arrived = [to_chip(take(summed, chip ^ step), step, cols) for step in range(1, cols // 2)]
    for piece in arrived:
        total = total + piece
    return total


def panel_sum(where, other_where, ancestor, pieces, slab_rows, cols):
    theirs = multiply(other_where, ancestor, pieces, slab_rows)
    handed = sibling(theirs, cols)
    mine = multiply(where, ancestor, pieces, slab_rows)
    return chip_scatter(mine + handed, cols)


def tile_scatter(blocks, rows, cols):
    count, width = blocks.shape[0], blocks.shape[1]
    part = width // cols
    core = lax.axis_index("col") % 2
    split = blocks.reshape(count, cols // 2, 2, part, width)
    split = jnp.moveaxis(split, 0, 2)
    split = jnp.moveaxis(split, 1, 0)
    mine = take(split, core)
    handed = sibling(take(split, 1 - core), cols)
    strip = chip_scatter(mine + handed, cols)
    row = lax.axis_index("row")
    high = width // rows

    def rows_of(index):
        return lax.dynamic_slice_in_dim(strip, index * high, high, 2)

    total = rows_of(row)
    for step in range(1, rows):
        pairs = [(r, r ^ step) for r in range(rows)]
        total = total + lax.ppermute(rows_of(row ^ step), "row", pairs)
    return jnp.swapaxes(total, 1, 2)


def body(
    rows,
    cols,
    ancestor,
    panel_one,
    panel_two,
    panel_three,
    couplings,
    diag_terms,
    list_two,
    list_three,
):
    block_width = couplings.shape[1]
    slab_rows = panel_one.shape[0]
    row_id, col_id = lax.axis_index("row"), lax.axis_index("col")
    device = row_id * cols + col_id
    where = jnp.stack([row_id, col_id % 2]).astype(jnp.int32)
    other_where = jnp.stack([row_id, 1 - col_id % 2]).astype(jnp.int32)
    spread_one = spread_panel(panel_one, rows, cols)
    keep_two = piece_keep(list_two, device * slab_rows, slab_rows, block_width)
    keep_three = piece_keep(list_three, device * slab_rows, slab_rows, block_width)
    own_two = jnp.where(keep_two > 0.5, panel_two, jnp.zeros_like(panel_two))
    own_three = jnp.where(keep_three > 0.5, panel_three, jnp.zeros_like(panel_three))
    spread_two = spread_panel(own_two, rows, cols)
    spread_three = spread_panel(own_three, rows, cols)
    coupled = couplings.astype(F32)
    ends = jnp.where(device == 0, diag_terms, jnp.zeros_like(diag_terms))
    factors = [panel_one.astype(F32), own_two.astype(F32), own_three.astype(F32)]

    scatter = functools.partial(
        panel_sum, where, other_where, ancestor, slab_rows=slab_rows, cols=cols
    )
    sum_one = scatter(spread_one)
    m_oneone = inner_product(factors[0], sum_one)
    m_twoone = inner_product(factors[1], sum_one)
    m_threeone = inner_product(factors[2], sum_one)
    inverse_one = -sum_one

    sum_two = scatter(spread_two)
    m_twotwo = inner_product(factors[1], sum_two)
    m_threetwo = inner_product(factors[2], sum_two)
    inverse_two = -(sum_two - product(sum_one, coupled[0])) * keep_two

    diag_one = ends[0] + m_oneone
    cross_two = m_twoone.T - product(diag_one, coupled[0])
    diag_two = (
        ends[1] + m_twotwo - product(m_twoone, coupled[0]) - inner_product(coupled[0], cross_two)
    )
    second_three = m_threetwo - product(m_threeone, coupled[0])
    cross_first = m_threeone.T - product(diag_one, coupled[1]) - product(cross_two, coupled[2])
    cross_second = (
        second_three.T - inner_product(cross_two, coupled[1]) - product(diag_two, coupled[2])
    )
    most_three = (
        ends[2]
        - product(m_threeone, coupled[1])
        - product(second_three, coupled[2])
        - inner_product(coupled[1], cross_first)
        - inner_product(coupled[2], cross_second)
    )
    early = jnp.stack(
        [diag_one.T, diag_two.T, most_three.T, cross_two.T, cross_first.T, cross_second.T]
    )
    early_tile = tile_scatter(early, rows, cols)

    sum_three = scatter(spread_three)
    m_threethree = inner_product(sum_three, factors[2])
    late_tile = tile_scatter(m_threethree[None], rows, cols)
    inverse_three = (
        -(sum_three - product(sum_one, coupled[1]) + product(inverse_two, coupled[2]))
        * keep_three
    )
    own_tile = early_tile.at[2].add(late_tile[0])
    return (inverse_one, inverse_two, inverse_three, own_tile)


def solution(mesh):
    in_specs = (
        P("row", "col"),
        P(("row", "col"), None),
        P(("row", "col"), None),
        P(("row", "col"), None),
        P(),
        P(),
        P(),
        P(),
    )
    out_specs = (
        P(("row", "col"), None),
        P(("row", "col"), None),
        P(("row", "col"), None),
        P(None, "row", "col"),
    )
    local = functools.partial(body, mesh.shape["row"], mesh.shape["col"])
    return jax.shard_map(local, mesh=mesh, in_specs=in_specs, out_specs=out_specs, check_vma=False)
```

time: 485 us -> 233 us (0.48)
  waiting for transfers between devices: 388 us -> 43.9 us
  starting transfers between devices: 0.34 us -> 92.6 us
  Pallas kernels: 0 us -> 68.9 us
  matrix products: 65.9 us -> 8.84 us
  between operations: 14.1 us -> 1.47 us
    psum x2 -> x0, waiting for transfers between devices: 251 us -> none  [the longest x1 130 us: body(): lax.psum((blocks[0], blocks[1], blocks[2], blocks[3], blocks[4], blocks[5...]
    ppermute x0 -> x38, starting transfers between devices: none -> 92.6 us  [the longest x12 52.7 us: spread_panel(): received.append(lax.ppermute(own, ('row', 'col'), pairs))]
    reduce_scatter x1 -> x0, waiting for transfers between devices: 88.6 us -> none  [body(): lax.psum_scatter(partial_all, 'col', scatter_dimension=0, tiled=True)]
    pallas_call x0 -> x6, Pallas kernels: none -> 68.9 us  [multiply(): pl.pallas_call(multiply_kernel, grid_spec=grid_spec, out_shape=jax.ShapeD...]
    dot_general x12 -> x11, matrix products: 55.6 us -> 4.47 us  [product(): jnp.dot(former, latter, precision=lax.Precision.HIGHEST, preferred_elemen...]
    all_gather x1 -> x0, waiting for transfers between devices: 48.3 us -> none  [spread_joint(): rows_all = lax.all_gather(own_piece, 'col', axis=0, tiled=True)]
    ppermute x0 -> x38, waiting for transfers between devices: none -> 43.9 us  [the longest x15 41.1 us: to_chip(): return lax.ppermute(value, 'col', [(c, c ^ 2 * step) for c in range(cols)])]
    add x0 -> x10, other arithmetic: none -> 6.23 us  [the longest x3 5.59 us: panel_sum(): return chip_scatter(mine + handed, cols)]
  transfers between devices with their start and end apart: 4 -> 38, of which waited for: 4 -> 13; matrix products, arithmetic and copies ran while one was open for 1% -> 10% of each run, Pallas kernels for 0% -> 30%
where the time goes in v1:
time: 233 us; the launch traced here: 232 us
  starting transfers between devices  92.6 us (40%)
  Pallas kernels  68.9 us (30%)
  waiting for transfers between devices  43.9 us (19%)
  other arithmetic  12.3 us (5%)
  matrix products  8.84 us (4%)
  local copies, waits for them, and re-layouts  3.9 us (2%)
    pallas_call x6, Pallas kernels, multiply(): pl.pallas_call(multiply_kernel, grid_spec=grid_spec, out_shape=jax.ShapeD...  68.9 us
    ppermute x12, starting transfers between devices, spread_panel(): received.append(lax.ppermute(own, ('row', 'col'), pairs))  52.7 us
    ppermute x15, waiting for transfers between devices, to_chip(): return lax.ppermute(value, 'col', [(c, c ^ 2 * step) for c in range(cols)])  41.1 us
    ppermute x15, starting transfers between devices, to_chip(): return lax.ppermute(value, 'col', [(c, c ^ 2 * step) for c in range(cols)])  29.3 us
    ppermute x6, starting transfers between devices, tile_scatter(): total = total + lax.ppermute(rows_of(row ^ step), 'row', pairs)  9.68 us
    add x3, other arithmetic, panel_sum(): return chip_scatter(mine + handed, cols)  5.59 us
  transfers between devices with their start and end apart: 38, of which 13 were waited for; matrix products, arithmetic and copies ran while one was open for 10% of the time, Pallas kernels for 30%

profile of v1, /device:TPU:0, one launch (start us, length us, event | category | flops | bytes accessed | tf_op | source)
XLA Modules:
  0.0 231.9 jit_solution(11808751358960188707)
XLA Ops:
  2.2 4.8 %collective-permute-start.1 = (bf16[512,256]{1,0:T(8,128)(2,1)}, bf16[512,256]{1,0:T(8,128)(2,1)S(1)}, u32[]{:S(2)}, u32[]{:S(2)}) collective-permute-start(bf16[512,256]{1,0:T(8,128)(2,1)} %param.11), channel_id=1, source_target_pairs={{0,8},{1,0},{2,24},{3,16},{4,9},{5,1},{6,25},{7,17},{8,10},{9,2},{... | collective-permute-start | bytes 786440 | tf_op jit(solution)/shard_map/ppermute | solution.py:45
  8.8 5.0 %collective-permute-start.3 = (bf16[512,256]{1,0:T(8,128)(2,1)}, bf16[512,256]{1,0:T(8,128)(2,1)S(1)}, u32[]{:S(2)}, u32[]{:S(2)}) collective-permute-start(bf16[512,256]{1,0:T(8,128)(2,1)} %param.11), channel_id=1, source_target_pairs={{0,24},{1,16},{2,8},{3,0},{4,25},{5,17},{6,9},{7,1},{8,26},{9,18},... | collective-permute-start | bytes 786440 | tf_op jit(solution)/shard_map/ppermute | solution.py:45
  18.4 5.1 %collective-permute-start.9 = (bf16[512,256]{1,0:T(8,128)(2,1)S(1)}, bf16[512,256]{1,0:T(8,128)(2,1)S(1)}, u32[]{:S(2)}, u32[]{:S(2)}) collective-permute-start(bf16[512,256]{1,0:T(8,128)(2,1)S(1)} %broadcast_select_fusion.2), channel_id=1, source_target_pairs={{0,8},{1,0},{2,24},{3,16},{4,9},{5,1},{6,25},{7,17},{8,10},{9,2},{... | collective-permute-start | bytes 786440 | tf_op jit(solution)/shard_map/ppermute | solution.py:45
  23.5 19.3 %collective-permute-start.10 = (bf16[512,256]{1,0:T(8,128)(2,1)S(1)}, bf16[512,256]{1,0:T(8,128)(2,1)S(1)}, u32[]{:S(2)}, u32[]{:S(2)}) collective-permute-start(bf16[512,256]{1,0:T(8,128)(2,1)S(1)} %broadcast_select_fusion.2), channel_id=1, source_target_pairs={{0,16},{1,24},{2,0},{3,8},{4,17},{5,25},{6,1},{7,9},{8,18},{9,26},... | collective-permute-start | bytes 786440 | tf_op jit(solution)/shard_map/ppermute | solution.py:45
  42.9 1.9 collective-permute-start.11
  45.5 12.1 %shard_map.112 = f32[4,512,256]{2,1,0:T(8,128)} custom-call(s32[2]{0:T(128)S(1)} %pad_add_fusion.1.where, f32[4096,2048]{1,0:T(8,128)} %s_ref.11, bf16[512,256]{1,0:T(8,128)(2,1)S(1)} %collective-permute-done.refs_0_, bf16[512,256]{1,0:T(8,128)(2,1)S(1)} %collective-permute-done.1.refs_1_, bf16[512,256]{1,0:T(8,128)(2,1)S(1)} %collective-permute-done.2.refs_2_, ...), custom_call_target="tpu_custom_call" | custom-call | flops 4294967296 | bytes 18874368 | tf_op jit(solution)/shard_map/pallas_call | solution.py:87
  57.6 7.2 %collective-permute-start.17 = (bf16[512,256]{1,0:T(8,128)(2,1)S(1)}, bf16[512,256]{1,0:T(8,128)(2,1)S(1)}, u32[]{:S(2)}, u32[]{:S(2)}) collective-permute-start(bf16[512,256]{1,0:T(8,128)(2,1)S(1)} %broadcast_select_fusion.1), channel_id=1, source_target_pairs={{0,8},{1,0},{2,24},{3,16},{4,9},{5,1},{6,25},{7,17},{8,10},{9,2},{... | collective-permute-start | bytes 786440 | tf_op jit(solution)/shard_map/ppermute | solution.py:45
  64.8 4.6 %collective-permute-start.19 = (bf16[512,256]{1,0:T(8,128)(2,1)S(1)}, bf16[512,256]{1,0:T(8,128)(2,1)S(1)}, u32[]{:S(2)}, u32[]{:S(2)}) collective-permute-start(bf16[512,256]{1,0:T(8,128)(2,1)S(1)} %broadcast_select_fusion.1), channel_id=1, source_target_pairs={{0,24},{1,16},{2,8},{3,0},{4,25},{5,17},{6,9},{7,1},{8,26},{9,18},... | collective-permute-start | bytes 786440 | tf_op jit(solution)/shard_map/ppermute | solution.py:45
  69.6 11.1 %shard_map.114 = f32[4,512,256]{2,1,0:T(8,128)S(1)} custom-call(s32[2]{0:T(128)S(1)} %pad_add_fusion.1.where, f32[4096,2048]{1,0:T(8,128)} %s_ref.11, bf16[512,256]{1,0:T(8,128)(2,1)S(1)} %collective-permute-done.8.refs_0_, bf16[512,256]{1,0:T(8,128)(2,1)S(1)} %collective-permute-done.9.refs_1_, bf16[512,256]{1,0:T(8,128)(2,1)S(1)} %collective-permute-done.10.refs_2_, ...), custom_call_target="tpu_custom_call" | custom-call | flops 4294967296 | bytes 18874368 | tf_op jit(solution)/shard_map/pallas_call | solution.py:87
  81.4 12.2 %shard_map.116 = f32[4,512,256]{2,1,0:T(8,128)} custom-call(s32[2]{0:T(128)S(1)} %pad_add_fusion.1.where, f32[4096,2048]{1,0:T(8,128)} %s_ref.11, bf16[512,256]{1,0:T(8,128)(2,1)S(1)} %collective-permute-done.16.refs_0_, bf16[512,256]{1,0:T(8,128)(2,1)S(1)} %collective-permute-done.17.refs_1_, bf16[512,256]{1,0:T(8,128)(2,1)S(1)} %collective-permute-done.18.refs_2_, ...), custom_call_target="tpu_custom_call" | custom-call | flops 4294967296 | bytes 18874368 | tf_op jit(solution)/shard_map/pallas_call | solution.py:87
  93.7 2.3 copy.14
  97.3 11.1 %shard_map.111 = f32[4,512,256]{2,1,0:T(8,128)S(1)} custom-call(s32[2]{0:T(128)S(1)} %pad_add_fusion.where, f32[4096,2048]{1,0:T(8,128)} %s_ref.11, bf16[512,256]{1,0:T(8,128)(2,1)S(1)} %collective-permute-done.refs_0_, bf16[512,256]{1,0:T(8,128)(2,1)S(1)} %collective-permute-done.1.refs_1_, bf16[512,256]{1,0:T(8,128)(2,1)S(1)} %collective-permute-done.2.refs_2_, ...), custom_call_target="tpu_custom_call" | custom-call | flops 4294967296 | bytes 18874368 | tf_op jit(solution)/shard_map/pallas_call | solution.py:87
  108.4 11.1 %shard_map.113 = f32[4,512,256]{2,1,0:T(8,128)S(1)} custom-call(s32[2]{0:T(128)S(1)} %pad_add_fusion.where, f32[4096,2048]{1,0:T(8,128)} %s_ref.11, bf16[512,256]{1,0:T(8,128)(2,1)S(1)} %collective-permute-done.8.refs_0_, bf16[512,256]{1,0:T(8,128)(2,1)S(1)} %copy-done.3, bf16[512,256]{1,0:T(8,128)(2,1)S(1)} %copy-done.7, bf16[512,256]{1,0:T(8,128)(2,1)S(1)} %copy-done.11), custom_call_target="tpu_custom_call" | custom-call | flops 4294967296 | bytes 18874368 | tf_op jit(solution)/shard_map/pallas_call | solution.py:87
  123.2 8.2 %collective-permute-start.6 = (f32[512,256]{1,0:T(8,128)S(1)}, f32[512,256]{1,0:T(8,128)S(1)}, u32[]{:S(2)}, u32[]{:S(2)}) collective-permute-start(f32[512,256]{1,0:T(8,128)S(1)} %get-tuple-element.26), channel_id=1, source_target_pairs={{0,4},{1,5},{2,6},{3,7},{4,0},{5,1},{6,2},{7,3},{8,12},{9,13},{10,... | collective-permute-start | bytes 1572872 | tf_op jit(solution)/shard_map/ppermute | solution.py:105
  132.8 11.3 %shard_map.115 = f32[4,512,256]{2,1,0:T(8,128)S(1)} custom-call(s32[2]{0:T(128)S(1)} %pad_add_fusion.where, f32[4096,2048]{1,0:T(8,128)} %s_ref.11, bf16[512,256]{1,0:T(8,128)(2,1)S(1)} %copy-done.1, bf16[512,256]{1,0:T(8,128)(2,1)S(1)} %copy-done.5, bf16[512,256]{1,0:T(8,128)(2,1)S(1)} %copy-done.9, bf16[512,256]{1,0:T(8,128)(2,1)S(1)} %copy-done.13), custom_call_target="tpu_custom_call" | custom-call | flops 4294967296 | bytes 18874368 | tf_op jit(solution)/shard_map/pallas_call | solution.py:87
  151.7 3.3 %collective-permute-done.6 = f32[512,256]{1,0:T(8,128)S(1)} collective-permute-done((f32[512,256]{1,0:T(8,128)S(1)}, f32[512,256]{1,0:T(8,128)S(1)}, u32[]{:S(2)}, u32[]{:S(2)}) %collective-permute-start.6) | collective-permute-done | bytes 524320 | tf_op jit(solution)/shard_map/ppermute | solution.py:105
  162.8 5.3 %collective-permute-start.21 = (f32[512,256]{1,0:T(8,128)S(1)}, f32[512,256]{1,0:T(8,128)S(1)}, u32[]{:S(2)}, u32[]{:S(2)}) collective-permute-start(f32[512,256]{1,0:T(8,128)S(1)} %get-tuple-element.18), channel_id=1, source_target_pairs={{0,2},{1,3},{2,0},{3,1},{4,6},{5,7},{6,4},{7,5},{8,10},{9,11},{10,... | collective-permute-start | bytes 1572872 | tf_op jit(solution)/shard_map/ppermute | solution.py:105
  168.1 9.2 %collective-permute-done.14 = f32[512,256]{1,0:T(8,128)S(1)} collective-permute-done((f32[512,256]{1,0:T(8,128)S(1)}, f32[512,256]{1,0:T(8,128)S(1)}, u32[]{:S(2)}, u32[]{:S(2)}) %collective-permute-start.14) | collective-permute-done | bytes 524320 | tf_op jit(solution)/shard_map/ppermute | solution.py:105
  177.3 1.9 collective-permute-done.13
  184.4 14.9 %collective-permute-done.22 = f32[512,256]{1,0:T(8,128)S(1)} collective-permute-done((f32[512,256]{1,0:T(8,128)S(1)}, f32[512,256]{1,0:T(8,128)S(1)}, u32[]{:S(2)}, u32[]{:S(2)}) %collective-permute-start.22) | collective-permute-done | bytes 524320 | tf_op jit(solution)/shard_map/ppermute | solution.py:105
  199.3 2.0 collective-permute-done.21
  211.1 5.2 %collective-permute-done.27 = f32[6,32,256]{2,1,0:T(8,128)S(1)} collective-permute-done((f32[6,32,256]{2,1,0:T(8,128)S(1)}, f32[6,32,256]{2,1,0:T(8,128)S(1)}, u32[]{:S(2)}, u32[]{:S(2)}) %collective-permute-start.27) | collective-permute-done | bytes 196640 | tf_op jit(solution)/shard_map/ppermute | solution.py:105
  216.4 2.0 collective-permute-done.26
  226.2 3.2 %collective-permute-start.35 = (f32[1,32,64]{2,1,0:T(8,128)S(1)}, f32[1,32,64]{2,1,0:T(8,128)S(1)}, u32[]{:S(2)}, u32[]{:S(2)}) collective-permute-start(f32[1,32,64]{2,1,0:T(8,128)S(1)} %get-tuple-element.36), channel_id=1, source_target_pairs={{0,8},{8,0},{16,24},{24,16},{1,9},{9,1},{17,25},{25,17},{2,10},{10... | collective-permute-start | bytes 24584 | tf_op jit(solution)/shard_map/ppermute | solution.py:147
  (162 shorter events, 56.0 us)
Async XLA Ops:
  0.6 17.8 %collective-permute-start = (bf16[512,256]{1,0:T(8,128)(2,1)}, bf16[512,256]{1,0:T(8,128)(2,1)S(1)}, u32[]{:S(2)}, u32[]{:S(2)}) collective-permute-start(bf16[512,256]{1,0:T(8,128)(2,1)} %param.11), channel_id=1, source_target_pairs={{0,0},{1,8},{2,16},{3,24},{4,1},{5,9},{6,17},{7,25},{8,2},{9,10},{... | collective-permute-start | bytes 786440 | tf_op jit(solution)/shard_map/ppermute | solution.py:45
  2.2 21.3 %collective-permute-start.1 = (bf16[512,256]{1,0:T(8,128)(2,1)}, bf16[512,256]{1,0:T(8,128)(2,1)S(1)}, u32[]{:S(2)}, u32[]{:S(2)}) collective-permute-start(bf16[512,256]{1,0:T(8,128)(2,1)} %param.11), channel_id=1, source_target_pairs={{0,8},{1,0},{2,24},{3,16},{4,9},{5,1},{6,25},{7,17},{8,10},{9,2},{... | collective-permute-start | bytes 786440 | tf_op jit(solution)/shard_map/ppermute | solution.py:45
  7.0 35.9 %collective-permute-start.2 = (bf16[512,256]{1,0:T(8,128)(2,1)}, bf16[512,256]{1,0:T(8,128)(2,1)S(1)}, u32[]{:S(2)}, u32[]{:S(2)}) collective-permute-start(bf16[512,256]{1,0:T(8,128)(2,1)} %param.11), channel_id=1, source_target_pairs={{0,16},{1,24},{2,0},{3,8},{4,17},{5,25},{6,1},{7,9},{8,18},{9,26},... | collective-permute-start | bytes 786440 | tf_op jit(solution)/shard_map/ppermute | solution.py:45
  8.8 36.0 %collective-permute-start.3 = (bf16[512,256]{1,0:T(8,128)(2,1)}, bf16[512,256]{1,0:T(8,128)(2,1)S(1)}, u32[]{:S(2)}, u32[]{:S(2)}) collective-permute-start(bf16[512,256]{1,0:T(8,128)(2,1)} %param.11), channel_id=1, source_target_pairs={{0,24},{1,16},{2,8},{3,0},{4,25},{5,17},{6,9},{7,1},{8,26},{9,18},... | collective-permute-start | bytes 786440 | tf_op jit(solution)/shard_map/ppermute | solution.py:45
  15.8 41.9 %collective-permute-start.8 = (bf16[512,256]{1,0:T(8,128)(2,1)S(1)}, bf16[512,256]{1,0:T(8,128)(2,1)S(1)}, u32[]{:S(2)}, u32[]{:S(2)}) collective-permute-start(bf16[512,256]{1,0:T(8,128)(2,1)S(1)} %broadcast_select_fusion.2), channel_id=1, source_target_pairs={{0,0},{1,8},{2,16},{3,24},{4,1},{5,9},{6,17},{7,25},{8,2},{9,10},{... | collective-permute-start | bytes 786440 | tf_op jit(solution)/shard_map/ppermute | solution.py:45
  18.4 46.4 %collective-permute-start.9 = (bf16[512,256]{1,0:T(8,128)(2,1)S(1)}, bf16[512,256]{1,0:T(8,128)(2,1)S(1)}, u32[]{:S(2)}, u32[]{:S(2)}) collective-permute-start(bf16[512,256]{1,0:T(8,128)(2,1)S(1)} %broadcast_select_fusion.2), channel_id=1, source_target_pairs={{0,8},{1,0},{2,24},{3,16},{4,9},{5,1},{6,25},{7,17},{8,10},{9,2},{... | collective-permute-start | bytes 786440 | tf_op jit(solution)/shard_map/ppermute | solution.py:45
  23.5 41.3 %collective-permute-start.10 = (bf16[512,256]{1,0:T(8,128)(2,1)S(1)}, bf16[512,256]{1,0:T(8,128)(2,1)S(1)}, u32[]{:S(2)}, u32[]{:S(2)}) collective-permute-start(bf16[512,256]{1,0:T(8,128)(2,1)S(1)} %broadcast_select_fusion.2), channel_id=1, source_target_pairs={{0,16},{1,24},{2,0},{3,8},{4,17},{5,25},{6,1},{7,9},{8,18},{9,26},... | collective-permute-start | bytes 786440 | tf_op jit(solution)/shard_map/ppermute | solution.py:45
  42.9 26.6 %collective-permute-start.11 = (bf16[512,256]{1,0:T(8,128)(2,1)S(1)}, bf16[512,256]{1,0:T(8,128)(2,1)S(1)}, u32[]{:S(2)}, u32[]{:S(2)}) collective-permute-start(bf16[512,256]{1,0:T(8,128)(2,1)S(1)} %broadcast_select_fusion.2), channel_id=1, source_target_pairs={{0,24},{1,16},{2,8},{3,0},{4,25},{5,17},{6,9},{7,1},{8,26},{9,18},... | collective-permute-start | bytes 786440 | tf_op jit(solution)/shard_map/ppermute | solution.py:45
  44.8 36.0 %collective-permute-start.16 = (bf16[512,256]{1,0:T(8,128)(2,1)S(1)}, bf16[512,256]{1,0:T(8,128)(2,1)S(1)}, u32[]{:S(2)}, u32[]{:S(2)}) collective-permute-start(bf16[512,256]{1,0:T(8,128)(2,1)S(1)} %broadcast_select_fusion.1), channel_id=1, source_target_pairs={{0,0},{1,8},{2,16},{3,24},{4,1},{5,9},{6,17},{7,25},{8,2},{9,10},{... | collective-permute-start | bytes 786440 | tf_op jit(solution)/shard_map/ppermute | solution.py:45
  57.6 23.7 %collective-permute-start.17 = (bf16[512,256]{1,0:T(8,128)(2,1)S(1)}, bf16[512,256]{1,0:T(8,128)(2,1)S(1)}, u32[]{:S(2)}, u32[]{:S(2)}) collective-permute-start(bf16[512,256]{1,0:T(8,128)(2,1)S(1)} %broadcast_select_fusion.1), channel_id=1, source_target_pairs={{0,8},{1,0},{2,24},{3,16},{4,9},{5,1},{6,25},{7,17},{8,10},{9,2},{... | collective-permute-start | bytes 786440 | tf_op jit(solution)/shard_map/ppermute | solution.py:45
  64.8 16.5 %collective-permute-start.18 = (bf16[512,256]{1,0:T(8,128)(2,1)S(1)}, bf16[512,256]{1,0:T(8,128)(2,1)S(1)}, u32[]{:S(2)}, u32[]{:S(2)}) collective-permute-start(bf16[512,256]{1,0:T(8,128)(2,1)S(1)} %broadcast_select_fusion.1), channel_id=1, source_target_pairs={{0,16},{1,24},{2,0},{3,8},{4,17},{5,25},{6,1},{7,9},{8,18},{9,26},... | collective-permute-start | bytes 786440 | tf_op jit(solution)/shard_map/ppermute | solution.py:45
  69.5 50.1 %collective-permute-start.4 = (f32[4,512,256]{2,1,0:T(8,128)}, f32[4,512,256]{2,1,0:T(8,128)}, u32[]{:S(2)}, u32[]{:S(2)}) collective-permute-start(f32[4,512,256]{2,1,0:T(8,128)} %shard_map.112), channel_id=1, source_target_pairs={{0,1},{1,0},{2,3},{3,2},{4,5},{5,4},{6,7},{7,6},{8,9},{9,8},{10,11... | collective-permute-start | bytes 6291464 | tf_op jit(solution)/shard_map/ppermute | solution.py:101
  80.8 63.3 %collective-permute-start.12 = (f32[4,512,256]{2,1,0:T(8,128)S(1)}, f32[4,512,256]{2,1,0:T(8,128)}, u32[]{:S(2)}, u32[]{:S(2)}) collective-permute-start(f32[4,512,256]{2,1,0:T(8,128)S(1)} %shard_map.114), channel_id=1, source_target_pairs={{0,1},{1,0},{2,3},{3,2},{4,5},{5,4},{6,7},{7,6},{8,9},{9,8},{10,11... | collective-permute-start | bytes 6291464 | tf_op jit(solution)/shard_map/ppermute | solution.py:101
  93.5 54.1 %collective-permute-start.20 = (f32[4,512,256]{2,1,0:T(8,128)}, f32[4,512,256]{2,1,0:T(8,128)}, u32[]{:S(2)}, u32[]{:S(2)}) collective-permute-start(f32[4,512,256]{2,1,0:T(8,128)} %shard_map.116), channel_id=1, source_target_pairs={{0,1},{1,0},{2,3},{3,2},{4,5},{5,4},{6,7},{7,6},{8,9},{9,8},{10,11... | collective-permute-start | bytes 6291464 | tf_op jit(solution)/shard_map/ppermute | solution.py:101
  121.6 28.7 %collective-permute-start.7 = (f32[512,256]{1,0:T(8,128)S(1)}, f32[512,256]{1,0:T(8,128)S(1)}, u32[]{:S(2)}, u32[]{:S(2)}) collective-permute-start(f32[512,256]{1,0:T(8,128)S(1)} %get-tuple-element.25), channel_id=1, source_target_pairs={{0,6},{1,7},{2,4},{3,5},{4,2},{5,3},{6,0},{7,1},{8,14},{9,15},{10,... | collective-permute-start | bytes 1572872 | tf_op jit(solution)/shard_map/ppermute | solution.py:105
  123.2 31.8 %collective-permute-start.6 = (f32[512,256]{1,0:T(8,128)S(1)}, f32[512,256]{1,0:T(8,128)S(1)}, u32[]{:S(2)}, u32[]{:S(2)}) collective-permute-start(f32[512,256]{1,0:T(8,128)S(1)} %get-tuple-element.26), channel_id=1, source_target_pairs={{0,4},{1,5},{2,6},{3,7},{4,0},{5,1},{6,2},{7,3},{8,12},{9,13},{10,... | collective-permute-start | bytes 1572872 | tf_op jit(solution)/shard_map/ppermute | solution.py:105
  131.4 25.4 %collective-permute-start.5 = (f32[512,256]{1,0:T(8,128)S(1)}, f32[512,256]{1,0:T(8,128)S(1)}, u32[]{:S(2)}, u32[]{:S(2)}) collective-permute-start(f32[512,256]{1,0:T(8,128)S(1)} %get-tuple-element.24), channel_id=1, source_target_pairs={{0,2},{1,3},{2,0},{3,1},{4,6},{5,7},{6,4},{7,5},{8,10},{9,11},{10,... | collective-permute-start | bytes 1572872 | tf_op jit(solution)/shard_map/ppermute | solution.py:105
  146.1 16.7 %collective-permute-start.15 = (f32[512,256]{1,0:T(8,128)S(1)}, f32[512,256]{1,0:T(8,128)S(1)}, u32[]{:S(2)}, u32[]{:S(2)}) collective-permute-start(f32[512,256]{1,0:T(8,128)S(1)} %get-tuple-element.22), channel_id=1, source_target_pairs={{0,6},{1,7},{2,4},{3,5},{4,2},{5,3},{6,0},{7,1},{8,14},{9,15},{10,... | collective-permute-start | bytes 1572872 | tf_op jit(solution)/shard_map/ppermute | solution.py:105
  147.6 29.7 %collective-permute-start.14 = (f32[512,256]{1,0:T(8,128)S(1)}, f32[512,256]{1,0:T(8,128)S(1)}, u32[]{:S(2)}, u32[]{:S(2)}) collective-permute-start(f32[512,256]{1,0:T(8,128)S(1)} %get-tuple-element.23), channel_id=1, source_target_pairs={{0,4},{1,5},{2,6},{3,7},{4,0},{5,1},{6,2},{7,3},{8,12},{9,13},{10,... | collective-permute-start | bytes 1572872 | tf_op jit(solution)/shard_map/ppermute | solution.py:105
  150.3 29.0 %collective-permute-start.13 = (f32[512,256]{1,0:T(8,128)S(1)}, f32[512,256]{1,0:T(8,128)S(1)}, u32[]{:S(2)}, u32[]{:S(2)}) collective-permute-start(f32[512,256]{1,0:T(8,128)S(1)} %get-tuple-element.21), channel_id=1, source_target_pairs={{0,2},{1,3},{2,0},{3,1},{4,6},{5,7},{6,4},{7,5},{8,10},{9,11},{10,... | collective-permute-start | bytes 1572872 | tf_op jit(solution)/shard_map/ppermute | solution.py:105
  155.0 29.4 %collective-permute-start.23 = (f32[512,256]{1,0:T(8,128)S(1)}, f32[512,256]{1,0:T(8,128)S(1)}, u32[]{:S(2)}, u32[]{:S(2)}) collective-permute-start(f32[512,256]{1,0:T(8,128)S(1)} %get-tuple-element.19), channel_id=1, source_target_pairs={{0,6},{1,7},{2,4},{3,5},{4,2},{5,3},{6,0},{7,1},{8,14},{9,15},{10,... | collective-permute-start | bytes 1572872 | tf_op jit(solution)/shard_map/ppermute | solution.py:105
  156.7 42.6 %collective-permute-start.22 = (f32[512,256]{1,0:T(8,128)S(1)}, f32[512,256]{1,0:T(8,128)S(1)}, u32[]{:S(2)}, u32[]{:S(2)}) collective-permute-start(f32[512,256]{1,0:T(8,128)S(1)} %get-tuple-element.20), channel_id=1, source_target_pairs={{0,4},{1,5},{2,6},{3,7},{4,0},{5,1},{6,2},{7,3},{8,12},{9,13},{10,... | collective-permute-start | bytes 1572872 | tf_op jit(solution)/shard_map/ppermute | solution.py:105
  162.8 38.5 %collective-permute-start.21 = (f32[512,256]{1,0:T(8,128)S(1)}, f32[512,256]{1,0:T(8,128)S(1)}, u32[]{:S(2)}, u32[]{:S(2)}) collective-permute-start(f32[512,256]{1,0:T(8,128)S(1)} %get-tuple-element.18), channel_id=1, source_target_pairs={{0,2},{1,3},{2,0},{3,1},{4,6},{5,7},{6,4},{7,5},{8,10},{9,11},{10,... | collective-permute-start | bytes 1572872 | tf_op jit(solution)/shard_map/ppermute | solution.py:105
  182.6 24.8 %collective-permute-start.24 = (f32[4,6,32,256]{3,2,0,1:T(8,128)S(1)}, f32[4,6,32,256]{3,2,0,1:T(8,128)S(1)}, u32[]{:S(2)}, u32[]{:S(2)}) collective-permute-start(f32[4,6,32,256]{3,2,0,1:T(8,128)S(1)} %dynamic-slice_bitcast_fusion), channel_id=1, source_target_pairs={{0,1},{1,0},{2,3},{3,2},{4,5},{5,4},{6,7},{7,6},{8,9},{9,8},{10,11... | collective-permute-start | bytes 2359304 | tf_op jit(solution)/shard_map/ppermute | solution.py:101
  (36 other events, 398.5 us)

commit v2 on v0

v2 whole, which is shorter than its diff:
```python
import functools

import jax
import jax.numpy as jnp
from jax import lax
from jax.experimental import pallas as pl
from jax.experimental.pallas import tpu as pltpu
from jax.sharding import PartitionSpec as P

F32 = jnp.float32
BF16 = jnp.bfloat16
F16 = jnp.float16
SCALE = 32.0
LITTLE = pl.CostEstimate(flops=1, bytes_accessed=1, transcendentals=0)


def product(former, latter):
    return jnp.dot(
        former, latter, precision=lax.Precision.HIGHEST, preferred_element_type=F32
    )


def piece_keep(listed, start_row, slab_rows, block_width):
    rows_here = start_row + jnp.arange(slab_rows, dtype=jnp.int32)
    matches = (rows_here // block_width)[:, None] == listed[None, :]
    return jnp.any(matches, axis=1).astype(F32)[:, None]


def spread_step(own, step, rows, cols):
    ratio = cols // rows
    pairs = []
    for plane in range(rows):
        for place in range(cols):
            target = ((place % rows) ^ step) * cols + plane * ratio + place // rows
            pairs.append((plane * cols + place, target))
    return lax.ppermute(own, ("row", "col"), pairs)


def spread_panel(own, rows, cols):
    return [spread_step(own, step, rows, cols) for step in range(rows)]


def split_dot(former, latter, dims):
    high = former.astype(BF16)
    low = (former - high.astype(F32)).astype(BF16)
    dims = (dims, ((), ()))
    return lax.dot_general(high, latter, dims, preferred_element_type=F32) + lax.dot_general(
        low, latter, dims, preferred_element_type=F32
    )


def join_kernel(*refs):
    span = refs[0].shape[1]
    for index, panel_ref in enumerate(refs[:-1]):
        refs[-1][:, index * span : (index + 1) * span] = panel_ref[...]


def join(panels):
    rows, span = panels[0].shape
    whole = pl.BlockSpec(memory_space=pltpu.VMEM)
    return pl.pallas_call(
        join_kernel,
        in_specs=[whole] * len(panels),
        out_specs=whole,
        out_shape=jax.ShapeDtypeStruct((rows, span * len(panels)), panels[0].dtype),
        cost_estimate=LITTLE,
    )(*panels)


def kept(keeps, panel, row, span, value):
    return jnp.where(keeps[panel, row // span] > 0, value, jnp.zeros_like(value))


def multiply_kernel(where, keeps, s_ref, *refs, depth, span):
    pieces, out_ref, panel = refs[:-2], refs[-2], refs[-1]

    @pl.when(pl.program_id(0) == 0)
    def _():
        unit = min(depth, span)
        for step, piece in enumerate(pieces):
            begin = (where[0] ^ step) * depth
            for part in range(0, depth, unit):
                target = pl.ds(pl.multiple_of(begin + part, unit), unit)
                for index in range(panel.shape[1] // span):
                    lanes = slice(index * span, (index + 1) * span)
                    panel[target, lanes] = kept(
                        keeps, index, where[3] + begin + part, span, piece[part : part + unit, lanes]
                    )

    out_ref[0] = split_dot(s_ref[...], panel[...], ((1,), (0,)))


def multiply(where, keeps, ancestor, pieces, span):
    local_rows, local_cols = ancestor.shape
    slab_rows, width = pieces[0].shape
    chips = local_rows // slab_rows // 2
    return pl.pallas_call(
        functools.partial(multiply_kernel, depth=slab_rows, span=span),
        grid_spec=pltpu.PrefetchScalarGridSpec(
            num_scalar_prefetch=2,
            grid=(chips,),
            in_specs=[
                pl.BlockSpec((slab_rows, local_cols), lambda i, where, keeps: (2 * i + where[1], 0))
            ]
            + [pl.BlockSpec(piece.shape, lambda *at: (0, 0)) for piece in pieces],
            out_specs=pl.BlockSpec((1, slab_rows, width), lambda i, *at: (i, 0, 0)),
            scratch_shapes=[pltpu.VMEM((local_cols, width), BF16)],
        ),
        out_shape=jax.ShapeDtypeStruct((chips, slab_rows, width), F32),
        compiler_params=pltpu.CompilerParams(vmem_limit_bytes=34 * 1024 * 1024),
        cost_estimate=LITTLE,
    )(where, keeps, ancestor, *pieces)


def sum_kernel(where, mine_ref, handed_ref, own_ref, sent_ref):
    step = pl.program_id(0)
    summed = mine_ref[0] + handed_ref[0]

    @pl.when(step == 0)
    def _():
        own_ref[...] = summed

    @pl.when(step > 0)
    def _():
        sent_ref[0] = summed * SCALE


def chip_sum(where, mine, handed):
    chips, depth, width = mine.shape
    taken = pl.BlockSpec((1, depth, width), lambda i, where: (where[2] ^ i, 0, 0))
    return pl.pallas_call(
        sum_kernel,
        grid_spec=pltpu.PrefetchScalarGridSpec(
            num_scalar_prefetch=1,
            grid=(chips,),
            in_specs=[taken, taken],
            out_specs=[
                pl.BlockSpec((depth, width), lambda *at: (0, 0)),
                pl.BlockSpec((1, depth, width), lambda i, *at: (jnp.maximum(i - 1, 0), 0, 0)),
            ],
        ),
        out_shape=[
            jax.ShapeDtypeStruct((depth, width), F32),
            jax.ShapeDtypeStruct((chips - 1, depth, width), F32),
        ],
        compiler_params=pltpu.CompilerParams(vmem_limit_bytes=24 * 1024 * 1024),
        cost_estimate=LITTLE,
    )(where, mine, handed)


def sibling(value, cols):
    return lax.ppermute(value, "col", [(c, c ^ 1) for c in range(cols)])


def to_chip(value, step, cols):
    return lax.ppermute(value, "col", [(c, c ^ (2 * step)) for c in range(cols)])


def after(value, others):
    return lax.optimization_barrier((value, others))[0]


def take(pieces, index):
    return lax.dynamic_index_in_dim(pieces, index, 0, keepdims=False)


def chip_scatter(summed, cols):
    chip = lax.axis_index("col") // 2
    total = take(summed, chip)
    arrived = [to_chip(take(summed, chip ^ step), step, cols) for step in range(1, cols // 2)]
    for piece in arrived:
        total = total + piece
    return total


def hand_over(payloads, cols):
    return [to_chip(payload, step + 1, cols) for step, payload in enumerate(payloads)]


def collect(own, arrived):
    total = own
    for payload in arrived:
        total = total + payload.astype(F32) * (1.0 / SCALE)
    return total


def small_kernel(where, keeps, sums, rows, couple, ends, out_ref):
    start, inner = ((0,), (0,)), ((1,), (0,))
    c_zero, c_one, c_two = couple[0], couple[1], couple[2]
    width = c_zero.shape[0]
    depth = rows.shape[0]
    unit = min(depth, width)

    def end(index):
        return jnp.where(where[4] == 0, ends[index], jnp.zeros_like(ends[index]))

    def turned(left, right):
        return split_dot(right, left, start).T

    def block(j, i):
        total = jnp.zeros((width, width), F32)
        for part in range(0, depth, unit):
            here = slice(part, part + unit)
            factor = rows[here, i * width : (i + 1) * width]
            factor = kept(keeps, i, where[4] + part, width, factor)
            total += split_dot(sums[here, j * width : (j + 1) * width], factor, start)
        return total

    t_oneone, t_twoone, t_threeone = block(0, 0), block(0, 1), block(0, 2)
    t_twotwo, t_threetwo, t_threethree = block(1, 1), block(1, 2), block(2, 2)
    m_twoone, m_threeone = t_twoone.T, t_threeone.T
    diag_one = end(0) + t_oneone.T
    cross_two = t_twoone - split_dot(diag_one, c_zero, inner)
    diag_two = (
        end(1) + t_twotwo.T - split_dot(m_twoone, c_zero, inner) - turned(c_zero, cross_two)
    )
    second_three = t_threetwo.T - split_dot(m_threeone, c_zero, inner)
    cross_first = t_threeone - split_dot(diag_one, c_one, inner) - split_dot(cross_two, c_two, inner)
    cross_second = (
        second_three.T
        - split_dot(cross_two, c_one, start)
        - split_dot(diag_two, c_two, inner)
    )
    diag_three = (
        end(2)
        + t_threethree.T
        - split_dot(m_threeone, c_one, inner)
        - split_dot(second_three, c_two, inner)
        - turned(c_one, cross_first)
        - turned(c_two, cross_second)
    )
    part = out_ref.shape[3]
    blocks = (diag_one, diag_two, diag_three, cross_two, cross_first, cross_second)
    for index, value in enumerate(blocks):
        value = value.T
        for place in range(width // part):
            out_ref[place % 2, place // 2, index] = value[place * part : (place + 1) * part, :]


def small_parts(where, keeps, sums, rows, couplings, ends, cols):
    width = couplings.shape[1]
    whole = pl.BlockSpec(memory_space=pltpu.VMEM)
    scalars = pl.BlockSpec(memory_space=pltpu.SMEM)
    return pl.pallas_call(
        small_kernel,
        in_specs=[scalars] * 2 + [whole] * 4,
        out_specs=whole,
        out_shape=jax.ShapeDtypeStruct((2, cols // 2, 6, width // cols, width), F32),
        compiler_params=pltpu.CompilerParams(vmem_limit_bytes=24 * 1024 * 1024),
        cost_estimate=LITTLE,
    )(where, keeps, sums, rows, couplings, ends)


def tile_scatter(split, rows, cols):
    row, core, chip = lax.axis_index("row"), lax.axis_index("col") % 2, lax.axis_index("col") // 2
    held = take(split, core) + sibling(take(split, 1 - core), cols)
    bit = cols // 4
    while bit:
        halves = held.reshape(2, bit, *held.shape[1:])
        side = chip // bit % 2
        held = take(halves, side) + to_chip(take(halves, 1 - side), bit, cols)
        bit //= 2
    held = held[0]
    bit = rows // 2
    while bit:
        size = held.shape[2] // 2
        side = row // bit % 2
        mine = lax.dynamic_slice_in_dim(held, side * size, size, 2)
        theirs = lax.dynamic_slice_in_dim(held, (1 - side) * size, size, 2)
        pairs = [(r, r ^ bit) for r in range(rows)]
        held = mine + lax.ppermute(theirs, "row", pairs)
        bit //= 2
    return jnp.swapaxes(held, 1, 2)


def body(
    rows,
    cols,
    ancestor,
    panel_one,
    panel_two,
    panel_three,
    couplings,
    diag_terms,
    list_two,
    list_three,
):
    block_width = couplings.shape[1]
    slab_rows = panel_one.shape[0]
    row_id, col_id = lax.axis_index("row"), lax.axis_index("col")
    device = row_id * cols + col_id
    core, chip = col_id % 2, col_id // 2
    others = [chip, col_id * ancestor.shape[1], device * slab_rows]
    where = jnp.stack([row_id, core] + others).astype(jnp.int32)
    other_where = jnp.stack([row_id, 1 - core] + others).astype(jnp.int32)
    keep_two = piece_keep(list_two, device * slab_rows, slab_rows, block_width)
    keep_three = piece_keep(list_three, device * slab_rows, slab_rows, block_width)
    blocks = jnp.arange(ancestor.shape[0] * rows // block_width, dtype=jnp.int32)
    listed_two = jnp.any(blocks[:, None] == list_two[None, :], axis=1)
    listed_three = jnp.any(blocks[:, None] == list_three[None, :], axis=1)
    keeps = jnp.stack([jnp.ones_like(listed_two), listed_two, listed_three]).astype(jnp.int32)

    own_rows = join([panel_one, panel_two, panel_three])
    pieces = spread_panel(own_rows, rows, cols)
    theirs = multiply(other_where, keeps, ancestor, pieces, block_width)
    handed = sibling(theirs, cols)
    mine = multiply(after(where, theirs), keeps, ancestor, pieces, block_width)
    own, sent = chip_sum(where, mine, handed)
    payloads = [sent[step].astype(F16) for step in range(cols // 2 - 1)]
    total = collect(own, hand_over(payloads, cols))
    parts = small_parts(where, keeps, total, own_rows, couplings, diag_terms, cols)
    own_tile = tile_scatter(parts, rows, cols)
    sum_one = total[:, :block_width]
    sum_two = total[:, block_width : 2 * block_width]
    sum_three = total[:, 2 * block_width :]
    inverse_one = -sum_one
    coupled = couplings.astype(F32)
    inverse_two = -(sum_two - product(sum_one, coupled[0])) * keep_two
    known = product(sum_one, coupled[1]) - product(inverse_two, coupled[2])
    inverse_three = (known - sum_three) * keep_three
    return (inverse_one, inverse_two, inverse_three, own_tile)


def solution(mesh):
    in_specs = (
        P("row", "col"),
        P(("row", "col"), None),
        P(("row", "col"), None),
        P(("row", "col"), None),
        P(),
        P(),
        P(),
        P(),
    )
    out_specs = (
        P(("row", "col"), None),
        P(("row", "col"), None),
        P(("row", "col"), None),
        P(None, "row", "col"),
    )
    local = functools.partial(body, mesh.shape["row"], mesh.shape["col"])
    return jax.shard_map(local, mesh=mesh, in_specs=in_specs, out_specs=out_specs, check_vma=False)
```

time: 485 us -> 205 us (0.42)
  waiting for transfers between devices: 388 us -> 105 us
  matrix products: 65.9 us -> 1.97 us
  Pallas kernels: 0 us -> 44.5 us
  starting transfers between devices: 0.34 us -> 40.8 us
  between operations: 14.1 us -> 1.01 us
    psum x2 -> x0, waiting for transfers between devices: 251 us -> none  [the longest x1 130 us: body(): lax.psum((blocks[0], blocks[1], blocks[2], blocks[3], blocks[4], blocks[5...]
    ppermute x0 -> x13, waiting for transfers between devices: none -> 105 us  [the longest x5 50.8 us: to_chip(): return lax.ppermute(value, 'col', [(c, c ^ 2 * step) for c in range(cols)])]
    reduce_scatter x1 -> x0, waiting for transfers between devices: 88.6 us -> none  [body(): lax.psum_scatter(partial_all, 'col', scatter_dimension=0, tiled=True)]
    dot_general x12 -> x3, matrix products: 55.6 us -> 1.97 us  [product(): jnp.dot(former, latter, precision=lax.Precision.HIGHEST, preferred_elemen...]
    all_gather x1 -> x0, waiting for transfers between devices: 48.3 us -> none  [spread_joint(): rows_all = lax.all_gather(own_piece, 'col', axis=0, tiled=True)]
    pallas_call x0 -> x5, Pallas kernels: none -> 44.5 us  [the longest x2 34.9 us: multiply(): pl.pallas_call(functools.partial(multiply_kernel, depth=slab_rows, span=s...]
    ppermute x0 -> x13, starting transfers between devices: none -> 40.8 us  [the longest x5 27.5 us: to_chip(): return lax.ppermute(value, 'col', [(c, c ^ 2 * step) for c in range(cols)])]
    dot_general x10 -> x0, matrix products: 10.2 us -> none  [inner_product(): lax.dot_general(former, latter, (((0,), (0,)), ((), ())), precision=lax.P...]
  transfers between devices with their start and end apart: 4 -> 13, of which waited for: 4 -> 10; matrix products, arithmetic and copies ran while one was open for 1% -> 2% of each run, Pallas kernels for 0% -> 8%
where the time goes in v2:
time: 205 us; the launch traced here: 204 us
  waiting for transfers between devices  105 us (51%)
  Pallas kernels  44.5 us (22%)
  starting transfers between devices  40.8 us (20%)
  other arithmetic  6.91 us (3%)
  local copies, waits for them, and re-layouts  4.32 us (2%)
    ppermute x5, waiting for transfers between devices, to_chip(): return lax.ppermute(value, 'col', [(c, c ^ 2 * step) for c in range(cols)])  50.8 us
    ppermute x4, waiting for transfers between devices, spread_step(): return lax.ppermute(own, ('row', 'col'), pairs)  42.7 us
    pallas_call x2, Pallas kernels, multiply(): pl.pallas_call(functools.partial(multiply_kernel, depth=slab_rows, span=s...  34.9 us
    ppermute x5, starting transfers between devices, to_chip(): return lax.ppermute(value, 'col', [(c, c ^ 2 * step) for c in range(cols)])  27.5 us
    ppermute x4, starting transfers between devices, spread_step(): return lax.ppermute(own, ('row', 'col'), pairs)  13.2 us
    ppermute x2, waiting for transfers between devices, tile_scatter(): held = mine + lax.ppermute(theirs, 'row', pairs)  8.62 us
    pallas_call x1, Pallas kernels, chip_sum(): pl.pallas_call(sum_kernel, grid_spec=pltpu.PrefetchScalarGridSpec(num_sca...  4.49 us
  transfers between devices with their start and end apart: 13, of which 10 were waited for; matrix products, arithmetic and copies ran while one was open for 2% of the time, Pallas kernels for 8%

profile of v2, /device:TPU:0, one launch (start us, length us, event | category | flops | bytes accessed | tf_op | source)
XLA Modules:
  0.0 204.3 jit_solution(2132195531134513120)
XLA Ops:
  0.7 2.1 %shard_map.111.rows = bf16[512,768]{1,0:T(8,128)(2,1)} custom-call(bf16[512,256]{1,0:T(8,128)(2,1)} %refs_0_.1, bf16[512,256]{1,0:T(8,128)(2,1)} %refs_1_.1, bf16[512,256]{1,0:T(8,128)(2,1)} %refs_2_.1), custom_call_target="tpu_custom_call" | custom-call | flops 1 | bytes 1 | tf_op jit(solution)/shard_map/pallas_call | solution.py:61
  2.8 1.8 collective-permute-start
  4.5 4.6 %collective-permute-start.1 = (bf16[512,768]{1,0:T(8,128)(2,1)}, bf16[512,768]{1,0:T(8,128)(2,1)S(1)}, u32[]{:S(2)}, u32[]{:S(2)}) collective-permute-start(bf16[512,768]{1,0:T(8,128)(2,1)} %shard_map.111.rows), channel_id=1, source_target_pairs={{0,8},{1,0},{2,24},{3,16},{4,9},{5,1},{6,25},{7,17},{8,10},{9,2},{... | collective-permute-start | bytes 2359304 | tf_op jit(solution)/shard_map/ppermute | solution.py:36
  9.1 1.8 collective-permute-start.2
  10.9 5.0 %collective-permute-start.3 = (bf16[512,768]{1,0:T(8,128)(2,1)}, bf16[512,768]{1,0:T(8,128)(2,1)S(1)}, u32[]{:S(2)}, u32[]{:S(2)}) collective-permute-start(bf16[512,768]{1,0:T(8,128)(2,1)} %shard_map.111.rows), channel_id=1, source_target_pairs={{0,24},{1,16},{2,8},{3,0},{4,25},{5,17},{6,9},{7,1},{8,26},{9,18},... | collective-permute-start | bytes 2359304 | tf_op jit(solution)/shard_map/ppermute | solution.py:36
  16.4 11.0 %collective-permute-done.1.refs_1_ = bf16[512,768]{1,0:T(8,128)(2,1)S(1)} collective-permute-done((bf16[512,768]{1,0:T(8,128)(2,1)}, bf16[512,768]{1,0:T(8,128)(2,1)S(1)}, u32[]{:S(2)}, u32[]{:S(2)}) %collective-permute-start.1) | collective-permute-done | bytes 786464 | tf_op jit(solution)/shard_map/ppermute | solution.py:36
  27.4 16.9 %collective-permute-done.2.refs_2_ = bf16[512,768]{1,0:T(8,128)(2,1)S(1)} collective-permute-done((bf16[512,768]{1,0:T(8,128)(2,1)}, bf16[512,768]{1,0:T(8,128)(2,1)S(1)}, u32[]{:S(2)}, u32[]{:S(2)}) %collective-permute-start.2) | collective-permute-done | bytes 786464 | tf_op jit(solution)/shard_map/ppermute | solution.py:36
  44.3 14.8 %collective-permute-done.3.refs_3_ = bf16[512,768]{1,0:T(8,128)(2,1)S(1)} collective-permute-done((bf16[512,768]{1,0:T(8,128)(2,1)}, bf16[512,768]{1,0:T(8,128)(2,1)S(1)}, u32[]{:S(2)}, u32[]{:S(2)}) %collective-permute-start.3) | collective-permute-done | bytes 786464 | tf_op jit(solution)/shard_map/ppermute | solution.py:36
  59.1 18.1 %shard_map.112 = f32[4,512,768]{2,1,0:T(8,128)} custom-call(s32[5]{0:T(128)S(1)} %stack.44.where, s32[3,64]{1,0:T(4,128)S(1)} %add_convert_fusion.keeps, f32[4096,2048]{1,0:T(8,128)} %s_ref.3, bf16[512,768]{1,0:T(8,128)(2,1)S(1)} %collective-permute-done.refs_0_, bf16[512,768]{1,0:T(8,128)(2,1)S(1)} %collective-permute-done.1.refs_1_, ...), custom_call_target="tpu_custom_call" | custom-call | flops 1 | bytes 1 | tf_op jit(solution)/shard_map/pallas_call | solution.py:97
  77.3 16.9 %shard_map.113.mine_ref = f32[4,512,768]{2,1,0:T(8,128)S(1)} custom-call(s32[5]{0:T(128)S(1)} %stack.42.where, s32[3,64]{1,0:T(4,128)S(1)} %add_convert_fusion.keeps, f32[4096,2048]{1,0:T(8,128)} %s_ref.3, bf16[512,768]{1,0:T(8,128)(2,1)S(1)} %collective-permute-done.refs_0_, bf16[512,768]{1,0:T(8,128)(2,1)S(1)} %collective-permute-done.1.refs_1_, ...), custom_call_target="tpu_custom_call" | custom-call | flops 1 | bytes 1 | tf_op jit(solution)/shard_map/pallas_call | solution.py:97
  94.1 4.5 %shard_map.114 = (f32[512,768]{1,0:T(8,128)S(1)}, f32[3,512,768]{2,1,0:T(8,128)S(1)}) custom-call(s32[5]{0:T(128)S(1)} %stack.42.where, f32[4,512,768]{2,1,0:T(8,128)S(1)} %shard_map.113.mine_ref, f32[4,512,768]{2,1,0:T(8,128)} %collective-permute-done.4.handed_ref), custom_call_target="tpu_custom_call" | custom-call | flops 1 | bytes 1 | tf_op jit(solution)/shard_map/pallas_call | solution.py:131
  99.0 1.4 slice_bitcast_fusion.2
  100.3 3.2 %collective-permute-start.5 = (f16[512,768]{1,0:T(8,128)(2,1)}, f16[512,768]{1,0:T(8,128)(2,1)}, u32[]{:S(2)}, u32[]{:S(2)}) collective-permute-start(f16[512,768]{1,0:T(8,128)(2,1)} %get-tuple-element.10), channel_id=1, source_target_pairs={{0,2},{1,3},{2,0},{3,1},{4,6},{5,7},{6,4},{7,5},{8,10},{9,11},{10,... | collective-permute-start | bytes 2359304 | tf_op jit(solution)/shard_map/ppermute | solution.py:156
  103.5 22.0 %collective-permute-start.6 = (f16[512,768]{1,0:T(8,128)(2,1)S(1)}, f16[512,768]{1,0:T(8,128)(2,1)}, u32[]{:S(2)}, u32[]{:S(2)}) collective-permute-start(f16[512,768]{1,0:T(8,128)(2,1)S(1)} %get-tuple-element.12), channel_id=1, source_target_pairs={{0,4},{1,5},{2,6},{3,7},{4,0},{5,1},{6,2},{7,3},{8,12},{9,13},{10,... | collective-permute-start | bytes 2359304 | tf_op jit(solution)/shard_map/ppermute | solution.py:156
  125.6 1.5 collective-permute-start.7
  127.0 32.9 %collective-permute-done.6 = f16[512,768]{1,0:T(8,128)(2,1)} collective-permute-done((f16[512,768]{1,0:T(8,128)(2,1)S(1)}, f16[512,768]{1,0:T(8,128)(2,1)}, u32[]{:S(2)}, u32[]{:S(2)}) %collective-permute-start.6) | collective-permute-done | bytes 786464 | tf_op jit(solution)/shard_map/ppermute | solution.py:156
  159.9 2.2 %collective-permute-done.7 = f16[512,768]{1,0:T(8,128)(2,1)} collective-permute-done((f16[512,768]{1,0:T(8,128)(2,1)S(1)}, f16[512,768]{1,0:T(8,128)(2,1)}, u32[]{:S(2)}, u32[]{:S(2)}) %collective-permute-start.7) | collective-permute-done | bytes 786464 | tf_op jit(solution)/shard_map/ppermute | solution.py:156
  162.1 2.2 %multiply_add_fusion.sums = f32[512,768]{1,0:T(8,128)S(1)} fusion(f16[512,768]{1,0:T(8,128)(2,1)} %collective-permute-done.7, f16[512,768]{1,0:T(8,128)(2,1)} %collective-permute-done.6, f32[512,768]{1,0:T(8,128)S(1)} %get-tuple-element.8, f16[512,768]{1,0:T(8,128)(2,1)} %collective-permute-done.5), kind=kLoop, calls=%fused_computation | loop fusion | flops 3538944 | bytes 5505024 | tf_op jit(solution)/shard_map/add | solution.py:183
  164.4 3.0 %shard_map.115 = f32[2,4,6,32,256]{4,3,2,1,0:T(8,128)S(1)} custom-call(s32[5]{0:T(128)S(1)} %stack.42.where, s32[3,64]{1,0:T(4,128)S(1)} %add_convert_fusion.keeps, f32[512,768]{1,0:T(8,128)S(1)} %multiply_add_fusion.sums, bf16[512,768]{1,0:T(8,128)(2,1)S(1)} %copy-done, bf16[3,256,256]{2,1,0:T(8,128)(2,1)S(1)} %copy-done.1, f32[3,256,256]{2,1,0:T(8,128)S(1)} %copy-done.2), custom_call_target="tpu_custom_call" | custom-call | flops 1 | bytes 1 | tf_op jit(solution)/shard_map/pallas_call | solution.py:244
  168.3 2.6 %collective-permute-done.8 = f32[4,6,32,256]{3,2,1,0:T(8,128)} collective-permute-done((f32[4,6,32,256]{3,2,1,0:T(8,128)}, f32[4,6,32,256]{3,2,1,0:T(8,128)}, u32[]{:S(2)}, u32[]{:S(2)}) %collective-permute-start.8) | collective-permute-done | bytes 786464 | tf_op jit(solution)/shard_map/ppermute | solution.py:152
  174.9 10.4 %collective-permute-done.9 = f32[2,6,32,256]{3,2,1,0:T(8,128)} collective-permute-done((f32[2,6,32,256]{3,2,1,0:T(8,128)}, f32[2,6,32,256]{3,2,1,0:T(8,128)}, u32[]{:S(2)}, u32[]{:S(2)}) %collective-permute-start.9) | collective-permute-done | bytes 393248 | tf_op jit(solution)/shard_map/ppermute | solution.py:156
  187.2 5.4 %collective-permute-done.10 = f32[1,6,32,256]{3,2,1,0:T(8,128)S(1)} collective-permute-done((f32[1,6,32,256]{3,2,1,0:T(8,128)S(1)}, f32[1,6,32,256]{3,2,1,0:T(8,128)S(1)}, u32[]{:S(2)}, u32[]{:S(2)}) %collective-permute-start.10) | collective-permute-done | bytes 196640 | tf_op jit(solution)/shard_map/ppermute | solution.py:156
  193.9 4.8 %collective-permute-done.11 = f32[6,32,128]{2,1,0:T(8,128)S(1)} collective-permute-done((f32[6,32,128]{2,1,0:T(8,128)S(1)}, f32[6,32,128]{2,1,0:T(8,128)S(1)}, u32[]{:S(2)}, u32[]{:S(2)}) %collective-permute-start.11) | collective-permute-done | bytes 98336 | tf_op jit(solution)/shard_map/ppermute | solution.py:271
  199.8 3.8 %collective-permute-done.12 = f32[6,32,64]{2,1,0:T(8,128)S(1)} collective-permute-done((f32[6,32,64]{2,1,0:T(8,128)S(1)}, f32[6,32,64]{2,1,0:T(8,128)S(1)}, u32[]{:S(2)}, u32[]{:S(2)}) %collective-permute-start.12) | collective-permute-done | bytes 49184 | tf_op jit(solution)/shard_map/ppermute | solution.py:271
  (51 shorter events, 10.6 us)
Async XLA Ops:
  0.6 15.5 %copy-start.6 = (s32[60]{0:T(128)S(1)}, s32[60]{0:T(128)}, u32[]{:S(2)}) copy-start(s32[60]{0:T(128)} %param.14) | copy-start | bytes 724
  0.6 15.6 %copy-start.7 = (s32[56]{0:T(128)S(1)}, s32[56]{0:T(128)}, u32[]{:S(2)}) copy-start(s32[56]{0:T(128)} %param.15) | copy-start | bytes 676
  2.8 13.6 %collective-permute-start = (bf16[512,768]{1,0:T(8,128)(2,1)}, bf16[512,768]{1,0:T(8,128)(2,1)S(1)}, u32[]{:S(2)}, u32[]{:S(2)}) collective-permute-start(bf16[512,768]{1,0:T(8,128)(2,1)} %shard_map.111.rows), channel_id=1, source_target_pairs={{0,0},{1,8},{2,16},{3,24},{4,1},{5,9},{6,17},{7,25},{8,2},{9,10},{... | collective-permute-start | bytes 2359304 | tf_op jit(solution)/shard_map/ppermute | solution.py:36
  4.5 22.9 %collective-permute-start.1 = (bf16[512,768]{1,0:T(8,128)(2,1)}, bf16[512,768]{1,0:T(8,128)(2,1)S(1)}, u32[]{:S(2)}, u32[]{:S(2)}) collective-permute-start(bf16[512,768]{1,0:T(8,128)(2,1)} %shard_map.111.rows), channel_id=1, source_target_pairs={{0,8},{1,0},{2,24},{3,16},{4,9},{5,1},{6,25},{7,17},{8,10},{9,2},{... | collective-permute-start | bytes 2359304 | tf_op jit(solution)/shard_map/ppermute | solution.py:36
  9.1 35.2 %collective-permute-start.2 = (bf16[512,768]{1,0:T(8,128)(2,1)}, bf16[512,768]{1,0:T(8,128)(2,1)S(1)}, u32[]{:S(2)}, u32[]{:S(2)}) collective-permute-start(bf16[512,768]{1,0:T(8,128)(2,1)} %shard_map.111.rows), channel_id=1, source_target_pairs={{0,16},{1,24},{2,0},{3,8},{4,17},{5,25},{6,1},{7,9},{8,18},{9,26},... | collective-permute-start | bytes 2359304 | tf_op jit(solution)/shard_map/ppermute | solution.py:36
  10.9 48.2 %collective-permute-start.3 = (bf16[512,768]{1,0:T(8,128)(2,1)}, bf16[512,768]{1,0:T(8,128)(2,1)S(1)}, u32[]{:S(2)}, u32[]{:S(2)}) collective-permute-start(bf16[512,768]{1,0:T(8,128)(2,1)} %shard_map.111.rows), channel_id=1, source_target_pairs={{0,24},{1,16},{2,8},{3,0},{4,25},{5,17},{6,9},{7,1},{8,26},{9,18},... | collective-permute-start | bytes 2359304 | tf_op jit(solution)/shard_map/ppermute | solution.py:36
  77.2 17.0 %collective-permute-start.4 = (f32[4,512,768]{2,1,0:T(8,128)}, f32[4,512,768]{2,1,0:T(8,128)}, u32[]{:S(2)}, u32[]{:S(2)}) collective-permute-start(f32[4,512,768]{2,1,0:T(8,128)} %shard_map.112), channel_id=1, source_target_pairs={{0,1},{1,0},{2,3},{3,2},{4,5},{5,4},{6,7},{7,6},{8,9},{9,8},{10,11... | collective-permute-start | bytes 18874376 | tf_op jit(solution)/shard_map/ppermute | solution.py:152
  100.3 26.7 %collective-permute-start.5 = (f16[512,768]{1,0:T(8,128)(2,1)}, f16[512,768]{1,0:T(8,128)(2,1)}, u32[]{:S(2)}, u32[]{:S(2)}) collective-permute-start(f16[512,768]{1,0:T(8,128)(2,1)} %get-tuple-element.10), channel_id=1, source_target_pairs={{0,2},{1,3},{2,0},{3,1},{4,6},{5,7},{6,4},{7,5},{8,10},{9,11},{10,... | collective-permute-start | bytes 2359304 | tf_op jit(solution)/shard_map/ppermute | solution.py:156
  103.5 56.4 %collective-permute-start.6 = (f16[512,768]{1,0:T(8,128)(2,1)S(1)}, f16[512,768]{1,0:T(8,128)(2,1)}, u32[]{:S(2)}, u32[]{:S(2)}) collective-permute-start(f16[512,768]{1,0:T(8,128)(2,1)S(1)} %get-tuple-element.12), channel_id=1, source_target_pairs={{0,4},{1,5},{2,6},{3,7},{4,0},{5,1},{6,2},{7,3},{8,12},{9,13},{10,... | collective-permute-start | bytes 2359304 | tf_op jit(solution)/shard_map/ppermute | solution.py:156
  125.6 36.6 %collective-permute-start.7 = (f16[512,768]{1,0:T(8,128)(2,1)S(1)}, f16[512,768]{1,0:T(8,128)(2,1)}, u32[]{:S(2)}, u32[]{:S(2)}) collective-permute-start(f16[512,768]{1,0:T(8,128)(2,1)S(1)} %get-tuple-element.11), channel_id=1, source_target_pairs={{0,6},{1,7},{2,4},{3,5},{4,2},{5,3},{6,0},{7,1},{8,14},{9,15},{10,... | collective-permute-start | bytes 2359304 | tf_op jit(solution)/shard_map/ppermute | solution.py:156
  162.1 2.2 %copy-start = (bf16[512,768]{1,0:T(8,128)(2,1)S(1)}, bf16[512,768]{1,0:T(8,128)(2,1)}, u32[]{:S(2)}) copy-start(bf16[512,768]{1,0:T(8,128)(2,1)} %shard_map.111.rows) | copy-start | bytes 2359300
  162.1 2.2 %copy-start.1 = (bf16[3,256,256]{2,1,0:T(8,128)(2,1)S(1)}, bf16[3,256,256]{2,1,0:T(8,128)(2,1)}, u32[]{:S(2)}) copy-start(bf16[3,256,256]{2,1,0:T(8,128)(2,1)} %couple.1) | copy-start | bytes 1179652
  162.1 2.2 %copy-start.2 = (f32[3,256,256]{2,1,0:T(8,128)S(1)}, f32[3,256,256]{2,1,0:T(8,128)}, u32[]{:S(2)}) copy-start(f32[3,256,256]{2,1,0:T(8,128)} %ends.1) | copy-start | bytes 2359300
  168.3 2.6 %collective-permute-start.8 = (f32[4,6,32,256]{3,2,1,0:T(8,128)}, f32[4,6,32,256]{3,2,1,0:T(8,128)}, u32[]{:S(2)}, u32[]{:S(2)}) collective-permute-start(f32[4,6,32,256]{3,2,1,0:T(8,128)} %dynamic-slice_bitcast_fusion), channel_id=1, source_target_pairs={{0,1},{1,0},{2,3},{3,2},{4,5},{5,4},{6,7},{7,6},{8,9},{9,8},{10,11... | collective-permute-start | bytes 2359304 | tf_op jit(solution)/shard_map/ppermute | solution.py:152
  172.2 0.9 copy-start.3
  173.8 11.5 %copy-start.4 = (f32[4,6,32,256]{3,2,1,0:T(8,128)S(1)}, f32[4,6,32,256]{3,2,1,0:T(8,128)}, u32[]{:S(2)}) copy-start(f32[4,6,32,256]{3,2,1,0:T(8,128)} %copy-done.3) | copy-start | bytes 2359300
  173.8 11.5 %collective-permute-start.9 = (f32[2,6,32,256]{3,2,1,0:T(8,128)}, f32[2,6,32,256]{3,2,1,0:T(8,128)}, u32[]{:S(2)}, u32[]{:S(2)}) collective-permute-start(f32[2,6,32,256]{3,2,1,0:T(8,128)} %dynamic-slice_bitcast_fusion.1), channel_id=1, source_target_pairs={{0,4},{1,5},{2,6},{3,7},{4,0},{5,1},{6,2},{7,3},{8,12},{9,13},{10,... | collective-permute-start | bytes 1179656 | tf_op jit(solution)/shard_map/ppermute | solution.py:156
  174.9 17.7 %copy-start.5 = (f32[512,256]{1,0:T(8,128)}, f32[512,256]{1,0:T(8,128)S(1)}, u32[]{:S(2)}) copy-start(f32[512,256]{1,0:T(8,128)S(1)} %fusion.3) | copy-start | bytes 1572868
  186.4 6.2 %collective-permute-start.10 = (f32[1,6,32,256]{3,2,1,0:T(8,128)S(1)}, f32[1,6,32,256]{3,2,1,0:T(8,128)S(1)}, u32[]{:S(2)}, u32[]{:S(2)}) collective-permute-start(f32[1,6,32,256]{3,2,1,0:T(8,128)S(1)} %constant_dynamic-slice_fusion.1), channel_id=1, source_target_pairs={{0,2},{1,3},{2,0},{3,1},{4,6},{5,7},{6,4},{7,5},{8,10},{9,11},{10,... | collective-permute-start | bytes 589832 | tf_op jit(solution)/shard_map/ppermute | solution.py:156
  192.6 6.1 %collective-permute-start.11 = (f32[6,32,128]{2,1,0:T(8,128)S(1)}, f32[6,32,128]{2,1,0:T(8,128)S(1)}, u32[]{:S(2)}, u32[]{:S(2)}) collective-permute-start(f32[6,32,128]{2,1,0:T(8,128)S(1)} %dynamic-slice_bitcast_fusion.2), channel_id=1, source_target_pairs={{0,16},{8,24},{16,0},{24,8},{1,17},{9,25},{17,1},{25,9},{2,18},{10... | collective-permute-start | bytes 294920 | tf_op jit(solution)/shard_map/ppermute | solution.py:271
  198.9 4.7 %collective-permute-start.12 = (f32[6,32,64]{2,1,0:T(8,128)S(1)}, f32[6,32,64]{2,1,0:T(8,128)S(1)}, u32[]{:S(2)}, u32[]{:S(2)}) collective-permute-start(f32[6,32,64]{2,1,0:T(8,128)S(1)} %constant_dynamic-slice_fusion), channel_id=1, source_target_pairs={{0,8},{8,0},{16,24},{24,16},{1,9},{9,1},{17,25},{25,17},{2,10},{10... | collective-permute-start | bytes 147464 | tf_op jit(solution)/shard_map/ppermute | solution.py:271

commit v3 on v2

--- a/solution.py
+++ b/solution.py
@@ -26,18 +26,25 @@
     return jnp.any(matches, axis=1).astype(F32)[:, None]
 
 
+def swap_of(plane, rows):
+    return plane % 2 * (rows // 2)
+
+
 def spread_step(own, step, rows, cols):
     ratio = cols // rows
     pairs = []
     for plane in range(rows):
         for place in range(cols):
-            target = ((place % rows) ^ step) * cols + plane * ratio + place // rows
-            pairs.append((plane * cols + place, target))
+            to_plane = (place % rows) ^ step ^ swap_of(plane, rows)
+            pairs.append((plane * cols + place, to_plane * cols + plane * ratio + place // rows))
     return lax.ppermute(own, ("row", "col"), pairs)
 
 
-def spread_panel(own, rows, cols):
-    return [spread_step(own, step, rows, cols) for step in range(rows)]
+def spread(own, rows, cols):
+    half = rows // 2
+    early = [spread_step(own, step, rows, cols) for step in range(half)]
+    late = [spread_step(after(own, early), half + step, rows, cols) for step in range(half)]
+    return [(0, early)], [(half, late)]
 
 
 def split_dot(former, latter, dims):
@@ -71,45 +78,86 @@
     return jnp.where(keeps[panel, row // span] > 0, value, jnp.zeros_like(value))
 
 
-def multiply_kernel(where, keeps, s_ref, *refs, depth, span):
-    pieces, out_ref, panel = refs[:-2], refs[-2], refs[-1]
-
-    @pl.when(pl.program_id(0) == 0)
+def multiply_kernel(where, keeps, *refs, depth, span, runs, kinds, added):
+    s_refs, refs = refs[: len(runs)], refs[len(runs) :]
+    panel = refs[-1]
+    outs = refs[-1 - kinds : -1]
+
+    @pl.when((pl.program_id(0) == 0) & (pl.program_id(1) == 0))
     def _():
         unit = min(depth, span)
-        for step, piece in enumerate(pieces):
-            begin = (where[0] ^ step) * depth
-            for part in range(0, depth, unit):
-                target = pl.ds(pl.multiple_of(begin + part, unit), unit)
-                for index in range(panel.shape[1] // span):
-                    lanes = slice(index * span, (index + 1) * span)
-                    panel[target, lanes] = kept(
-                        keeps, index, where[3] + begin + part, span, piece[part : part + unit, lanes]
-                    )
-
-    out_ref[0] = split_dot(s_ref[...], panel[...], ((1,), (0,)))
-
-
-def multiply(where, keeps, ancestor, pieces, span):
-    local_rows, local_cols = ancestor.shape
+        held = 0
+        for first, count in runs:
+            for step in range(count):
+                piece = refs[held + step]
+                place = where[0] ^ (first + step)
+                for part in range(0, depth, unit):
+                    begin = held * depth + place % count * depth + part
+                    target = pl.ds(pl.multiple_of(begin, unit), unit)
+                    row = where[3] + place * depth + part
+                    for index in range(panel.shape[1] // span):
+                        lanes = slice(index * span, (index + 1) * span)
+                        value = piece[part : part + unit, lanes]
+                        panel[target, lanes] = kept(keeps, index, row, span, value)
+            held += count
+
+    result = refs[-2 - kinds][0] if added else None
+    begin = 0
+    for s_ref in s_refs:
+        end = begin + s_ref.shape[1]
+        partial = split_dot(s_ref[...], panel[begin:end, :], ((1,), (0,)))
+        result = partial if result is None else result + partial
+        begin = end
+    for kind, out_ref in enumerate(outs):
+
+        @pl.when(pl.program_id(0) == kind)
+        def _():
+            out_ref[0] = result
+
+
+def multiply(where, keeps, ancestor, runs, span, kinds, added=None):
+    local_rows = ancestor.shape[0]
+    pieces = [piece for _, run in runs for piece in run]
     slab_rows, width = pieces[0].shape
     chips = local_rows // slab_rows // 2
+
+    def block_of(first, count):
+        def at(h, i, where, keeps):
+            kind = jnp.where(h == 0, where[1], 1 - where[1])
+            return 2 * i + kind, (where[0] ^ first) // count
+
+        return pl.BlockSpec((slab_rows, count * slab_rows), at)
+
+    def out_at(kind):
+        if kind == 0:
+            return lambda h, i, *at: (jnp.where(h == 0, i, chips - 1), 0, 0)
+        return lambda h, i, *at: (i * h, 0, 0)
+
+    counts = tuple((first, len(run)) for first, run in runs)
+    part = (1, slab_rows, width)
+    extra = [] if added is None else [added]
     return pl.pallas_call(
-        functools.partial(multiply_kernel, depth=slab_rows, span=span),
+        functools.partial(
+            multiply_kernel,
+            depth=slab_rows,
+            span=span,
+            runs=counts,
+            kinds=kinds,
+            added=len(extra),
+        ),
         grid_spec=pltpu.PrefetchScalarGridSpec(
             num_scalar_prefetch=2,
-            grid=(chips,),
-            in_specs=[
-                pl.BlockSpec((slab_rows, local_cols), lambda i, where, keeps: (2 * i + where[1], 0))
-            ]
-            + [pl.BlockSpec(piece.shape, lambda *at: (0, 0)) for piece in pieces],
-            out_specs=pl.BlockSpec((1, slab_rows, width), lambda i, *at: (i, 0, 0)),
-            scratch_shapes=[pltpu.VMEM((local_cols, width), BF16)],
+            grid=(kinds, chips),
+            in_specs=[block_of(*run) for run in counts]
+            + [pl.BlockSpec(piece.shape, lambda *at: (0, 0)) for piece in pieces]
+            + [pl.BlockSpec(part, out_at(0)) for _ in extra],
+            out_specs=[pl.BlockSpec(part, out_at(kind)) for kind in range(kinds)],
+            scratch_shapes=[pltpu.VMEM((len(pieces) * slab_rows, width), BF16)],
         ),
-        out_shape=jax.ShapeDtypeStruct((chips, slab_rows, width), F32),
+        out_shape=[jax.ShapeDtypeStruct((chips, slab_rows, width), F32)] * kinds,
         compiler_params=pltpu.CompilerParams(vmem_limit_bytes=34 * 1024 * 1024),
         cost_estimate=LITTLE,
-    )(where, keeps, ancestor, *pieces)
+    )(where, keeps, *([ancestor] * len(runs)), *pieces, *extra)
 
 
 def sum_kernel(where, mine_ref, handed_ref, own_ref, sent_ref):
@@ -254,13 +302,8 @@
 def tile_scatter(split, rows, cols):
     row, core, chip = lax.axis_index("row"), lax.axis_index("col") % 2, lax.axis_index("col") // 2
     held = take(split, core) + sibling(take(split, 1 - core), cols)
-    bit = cols // 4
-    while bit:
-        halves = held.reshape(2, bit, *held.shape[1:])
-        side = chip // bit % 2
-        held = take(halves, side) + to_chip(take(halves, 1 - side), bit, cols)
-        bit //= 2
-    held = held[0]
+    arrived = [to_chip(take(held, chip ^ step), step, cols) for step in range(1, cols // 2)]
+    held = functools.reduce(jnp.add, arrived, take(held, chip))
     bit = rows // 2
     while bit:
         size = held.shape[2] // 2
@@ -291,8 +334,9 @@
     device = row_id * cols + col_id
     core, chip = col_id % 2, col_id // 2
     others = [chip, col_id * ancestor.shape[1], device * slab_rows]
-    where = jnp.stack([row_id, core] + others).astype(jnp.int32)
-    other_where = jnp.stack([row_id, 1 - core] + others).astype(jnp.int32)
+    turned_row = row_id ^ swap_of(col_id // (cols // rows), rows)
+    where = jnp.stack([turned_row, core] + others).astype(jnp.int32)
+    other_where = jnp.stack([turned_row, 1 - core] + others).astype(jnp.int32)
     keep_two = piece_keep(list_two, device * slab_rows, slab_rows, block_width)
     keep_three = piece_keep(list_three, device * slab_rows, slab_rows, block_width)
     blocks = jnp.arange(ancestor.shape[0] * rows // block_width, dtype=jnp.int32)
@@ -301,10 +345,13 @@
     keeps = jnp.stack([jnp.ones_like(listed_two), listed_two, listed_three]).astype(jnp.int32)
 
     own_rows = join([panel_one, panel_two, panel_three])
-    pieces = spread_panel(own_rows, rows, cols)
-    theirs = multiply(other_where, keeps, ancestor, pieces, block_width)
+    early, late = spread(own_rows, rows, cols)
+    shared = (keeps, ancestor)
+    theirs, mine = multiply(other_where, *shared, early, block_width, 2)
+    (theirs,) = multiply(other_where, *shared, late, block_width, 1, theirs)
     handed = sibling(theirs, cols)
-    mine = multiply(after(where, theirs), keeps, ancestor, pieces, block_width)
+    turn = after(where, theirs)
+    (mine,) = multiply(turn, *shared, late, block_width, 1, mine)
     own, sent = chip_sum(where, mine, handed)
     payloads = [sent[step].astype(F16) for step in range(cols // 2 - 1)]
     total = collect(own, hand_over(payloads, cols))

time: 205 us -> 190 us (0.927)
  waiting for transfers between devices: 105 us -> 76.3 us
  starting transfers between devices: 40.8 us -> 48.3 us
  local copies, waits for them, and re-layouts: 4.32 us -> 8.15 us
  Pallas kernels: 44.5 us -> 48.1 us
    ppermute x4, starting transfers between devices: 13.2 us -> 38.9 us  [spread_step(): return lax.ppermute(own, ('row', 'col'), pairs)]
    ppermute x4, waiting for transfers between devices: 42.7 us -> 22.4 us  [spread_step(): return lax.ppermute(own, ('row', 'col'), pairs)]
    ppermute x5 -> x6, starting transfers between devices: 27.5 us -> 7.84 us  [to_chip(): return lax.ppermute(value, 'col', [(c, c ^ 2 * step) for c in range(cols)])]
    ppermute x5 -> x6, waiting for transfers between devices: 50.8 us -> 43 us  [to_chip(): return lax.ppermute(value, 'col', [(c, c ^ 2 * step) for c in range(cols)])]
    unnamed x16, local copies, waits for them, and re-layouts: 0.91 us -> 5.45 us
    pallas_call x2 -> x3, Pallas kernels: 34.9 us -> 38.6 us  [multiply(): pl.pallas_call(functools.partial(multiply_kernel, depth=slab_rows, span=s...]
  transfers between devices with their start and end apart: 13 -> 14, of which waited for: 10 -> 9; matrix products, arithmetic and copies ran while one was open for 2% -> 2% of each run, Pallas kernels for 8% -> 14%
where the time goes in v3:
time: 190 us
  waiting for transfers between devices  76.3 us (40%)
  starting transfers between devices  48.3 us (25%)
  Pallas kernels  48.1 us (25%)
  local copies, waits for them, and re-layouts  8.15 us (4%)
  other arithmetic  5.9 us (3%)
  matrix products  1.95 us (1%)
    ppermute x6, waiting for transfers between devices, to_chip(): return lax.ppermute(value, 'col', [(c, c ^ 2 * step) for c in range(cols)])  43 us
    ppermute x4, starting transfers between devices, spread_step(): return lax.ppermute(own, ('row', 'col'), pairs)  38.9 us
    pallas_call x3, Pallas kernels, multiply(): pl.pallas_call(functools.partial(multiply_kernel, depth=slab_rows, span=s...  38.6 us
    ppermute x4, waiting for transfers between devices, spread_step(): return lax.ppermute(own, ('row', 'col'), pairs)  22.4 us
    ppermute x2, waiting for transfers between devices, tile_scatter(): held = mine + lax.ppermute(theirs, 'row', pairs)  9.04 us
    ppermute x6, starting transfers between devices, to_chip(): return lax.ppermute(value, 'col', [(c, c ^ 2 * step) for c in range(cols)])  7.84 us
    unnamed x16, local copies, waits for them, and re-layouts  5.45 us
    pallas_call x1, Pallas kernels, chip_sum(): pl.pallas_call(sum_kernel, grid_spec=pltpu.PrefetchScalarGridSpec(num_sca...  4.49 us
  transfers between devices with their start and end apart: 14, of which 9 were waited for; matrix products, arithmetic and copies ran while one was open for 2% of the time, Pallas kernels for 14%

profile of v3, /device:TPU:0, one launch (start us, length us, event | category | flops | bytes accessed | tf_op | source)
XLA Modules:
  0.0 189.7 jit_solution(8316868025623579459)
XLA Ops:
  0.7 2.1 %shard_map.111.rows = bf16[512,768]{1,0:T(8,128)(2,1)} custom-call(bf16[512,256]{1,0:T(8,128)(2,1)} %refs_0_.4, bf16[512,256]{1,0:T(8,128)(2,1)} %refs_1_.1, bf16[512,256]{1,0:T(8,128)(2,1)} %refs_2_.1), custom_call_target="tpu_custom_call" | custom-call | flops 1 | bytes 1 | tf_op jit(solution)/shard_map/pallas_call | solution.py:68
  2.7 1.8 collective-permute-start
  4.5 7.6 %collective-permute-start.1 = (bf16[512,768]{1,0:T(8,128)(2,1)}, bf16[512,768]{1,0:T(8,128)(2,1)S(1)}, u32[]{:S(2)}, u32[]{:S(2)}) collective-permute-start(bf16[512,768]{1,0:T(8,128)(2,1)} %shard_map.111.rows), channel_id=1, source_target_pairs={{0,8},{1,0},{2,24},{3,16},{4,9},{5,1},{6,25},{7,17},{8,26},{9,18},... | collective-permute-start | bytes 2359304 | tf_op jit(solution)/shard_map/ppermute | solution.py:40
  12.1 13.2 %collective-permute-done.1.refs_2_ = bf16[512,768]{1,0:T(8,128)(2,1)S(1)} collective-permute-done((bf16[512,768]{1,0:T(8,128)(2,1)}, bf16[512,768]{1,0:T(8,128)(2,1)S(1)}, u32[]{:S(2)}, u32[]{:S(2)}) %collective-permute-start.1) | collective-permute-done | bytes 786464 | tf_op jit(solution)/shard_map/ppermute | solution.py:40
  25.3 24.5 %collective-permute-start.2 = (bf16[512,768]{1,0:T(8,128)(2,1)}, bf16[512,768]{1,0:T(8,128)(2,1)S(1)}, u32[]{:S(2)}, u32[]{:S(2)}) collective-permute-start(bf16[512,768]{1,0:T(8,128)(2,1)} %shard_map.111.rows), channel_id=1, source_target_pairs={{0,16},{1,24},{2,0},{3,8},{4,17},{5,25},{6,1},{7,9},{8,2},{9,10},{... | collective-permute-start | bytes 2359304 | tf_op jit(solution)/shard_map/ppermute | solution.py:40
  49.8 5.1 %collective-permute-start.3 = (bf16[512,768]{1,0:T(8,128)(2,1)}, bf16[512,768]{1,0:T(8,128)(2,1)S(1)}, u32[]{:S(2)}, u32[]{:S(2)}) collective-permute-start(bf16[512,768]{1,0:T(8,128)(2,1)} %shard_map.111.rows), channel_id=1, source_target_pairs={{0,24},{1,16},{2,8},{3,0},{4,25},{5,17},{6,9},{7,1},{8,10},{9,2},{... | collective-permute-start | bytes 2359304 | tf_op jit(solution)/shard_map/ppermute | solution.py:40
  55.3 17.7 %shard_map.112 = (f32[4,512,768]{2,1,0:T(8,128)S(1)}, f32[4,512,768]{2,1,0:T(8,128)S(1)}) custom-call(s32[5]{0:T(128)S(1)} %stack.44.where, s32[3,64]{1,0:T(4,128)S(1)} %add_convert_fusion.keeps, f32[4096,2048]{1,0:T(8,128)} %refs_0_.7, bf16[512,768]{1,0:T(8,128)(2,1)S(1)} %collective-permute-done.refs_1_, bf16[512,768]{1,0:T(8,128)(2,1)S(1)} %collective-permute-done.1.refs_2_), custom_call_target="tpu_custom_call" | custom-call | flops 1 | bytes 1 | tf_op jit(solution)/shard_map/pallas_call | solution.py:139
  73.1 2.6 %copy-done = f32[4,512,768]{2,1,0:T(8,128)} copy-done((f32[4,512,768]{2,1,0:T(8,128)}, f32[4,512,768]{2,1,0:T(8,128)S(1)}, u32[]{:S(2)}) %copy-start) | copy-done | bytes 6291480
  75.7 9.1 %collective-permute-done.3.refs_2_ = bf16[512,768]{1,0:T(8,128)(2,1)S(1)} collective-permute-done((bf16[512,768]{1,0:T(8,128)(2,1)}, bf16[512,768]{1,0:T(8,128)(2,1)S(1)}, u32[]{:S(2)}, u32[]{:S(2)}) %collective-permute-start.3) | collective-permute-done | bytes 786464 | tf_op jit(solution)/shard_map/ppermute | solution.py:40
  84.9 11.2 %shard_map.113 = f32[4,512,768]{2,1,0:T(8,128)} custom-call(s32[5]{0:T(128)S(1)} %stack.44.where, s32[3,64]{1,0:T(4,128)S(1)} %add_convert_fusion.keeps, f32[4096,2048]{1,0:T(8,128)} %refs_0_.7, bf16[512,768]{1,0:T(8,128)(2,1)S(1)} %collective-permute-done.2.refs_1_, bf16[512,768]{1,0:T(8,128)(2,1)S(1)} %collective-permute-done.3.refs_2_, ...), custom_call_target="tpu_custom_call" | custom-call | flops 1 | bytes 1 | tf_op jit(solution)/shard_map/pallas_call | solution.py:139
  96.3 2.8 %copy-done.1 = f32[4,512,768]{2,1,0:T(8,128)S(1)} copy-done((f32[4,512,768]{2,1,0:T(8,128)S(1)}, f32[4,512,768]{2,1,0:T(8,128)}, u32[]{:S(2)}) %copy-start.1) | copy-done | bytes 6291480
  99.1 9.7 %shard_map.114.mine_ref = f32[4,512,768]{2,1,0:T(8,128)S(1)} custom-call(s32[5]{0:T(128)S(1)} %stack.42.where, s32[3,64]{1,0:T(4,128)S(1)} %add_convert_fusion.keeps, f32[4096,2048]{1,0:T(8,128)} %refs_0_.7, bf16[512,768]{1,0:T(8,128)(2,1)S(1)} %collective-permute-done.2.refs_1_, bf16[512,768]{1,0:T(8,128)(2,1)S(1)} %collective-permute-done.3.refs_2_, ...), custom_call_target="tpu_custom_call" | custom-call | flops 1 | bytes 1 | tf_op jit(solution)/shard_map/pallas_call | solution.py:139
  108.8 4.5 %shard_map.115 = (f32[512,768]{1,0:T(8,128)S(1)}, f32[3,512,768]{2,1,0:T(8,128)S(1)}) custom-call(s32[5]{0:T(128)S(1)} %stack.42.where, f32[4,512,768]{2,1,0:T(8,128)S(1)} %shard_map.114.mine_ref, f32[4,512,768]{2,1,0:T(8,128)} %collective-permute-done.4.handed_ref), custom_call_target="tpu_custom_call" | custom-call | flops 1 | bytes 1 | tf_op jit(solution)/shard_map/pallas_call | solution.py:179
  115.0 3.7 %collective-permute-start.7 = (f16[512,768]{1,0:T(8,128)(2,1)}, f16[512,768]{1,0:T(8,128)(2,1)}, u32[]{:S(2)}, u32[]{:S(2)}) collective-permute-start(f16[512,768]{1,0:T(8,128)(2,1)} %get-tuple-element.17), channel_id=1, source_target_pairs={{0,6},{1,7},{2,4},{3,5},{4,2},{5,3},{6,0},{7,1},{8,14},{9,15},{10,... | collective-permute-start | bytes 2359304 | tf_op jit(solution)/shard_map/ppermute | solution.py:204
  119.3 18.2 %collective-permute-done.7 = f16[512,768]{1,0:T(8,128)(2,1)} collective-permute-done((f16[512,768]{1,0:T(8,128)(2,1)}, f16[512,768]{1,0:T(8,128)(2,1)}, u32[]{:S(2)}, u32[]{:S(2)}) %collective-permute-start.7) | collective-permute-done | bytes 786464 | tf_op jit(solution)/shard_map/ppermute | solution.py:204
  137.5 16.6 %collective-permute-done.6 = f16[512,768]{1,0:T(8,128)(2,1)} collective-permute-done((f16[512,768]{1,0:T(8,128)(2,1)S(1)}, f16[512,768]{1,0:T(8,128)(2,1)}, u32[]{:S(2)}, u32[]{:S(2)}) %collective-permute-start.6) | collective-permute-done | bytes 786464 | tf_op jit(solution)/shard_map/ppermute | solution.py:204
  154.1 2.2 %multiply_add_fusion.sums = f32[512,768]{1,0:T(8,128)S(1)} fusion(f16[512,768]{1,0:T(8,128)(2,1)} %collective-permute-done.7, f16[512,768]{1,0:T(8,128)(2,1)} %collective-permute-done.6, f32[512,768]{1,0:T(8,128)S(1)} %get-tuple-element.14, f16[512,768]{1,0:T(8,128)(2,1)} %collective-permute-done.5), kind=kLoop, calls=%fused_computation | loop fusion | flops 3538944 | bytes 5505024 | tf_op jit(solution)/shard_map/add | solution.py:231
  156.3 3.0 %shard_map.116 = f32[2,4,6,32,256]{4,3,2,1,0:T(8,128)S(1)} custom-call(s32[5]{0:T(128)S(1)} %stack.42.where, s32[3,64]{1,0:T(4,128)S(1)} %add_convert_fusion.keeps, f32[512,768]{1,0:T(8,128)S(1)} %multiply_add_fusion.sums, bf16[512,768]{1,0:T(8,128)(2,1)S(1)} %copy-done.2, bf16[3,256,256]{2,1,0:T(8,128)(2,1)S(1)} %copy-done.3, f32[3,256,256]{2,1,0:T(8,128)S(1)} %copy-done.4), custom_call_target="tpu_custom_call" | custom-call | flops 1 | bytes 1 | tf_op jit(solution)/shard_map/pallas_call | solution.py:292
  161.0 1.9 collective-permute-done.8
  165.8 1.7 collective-permute-start.10
  168.1 4.8 %collective-permute-done.11 = f32[6,32,256]{2,1,0:T(8,128)S(1)} collective-permute-done((f32[6,32,256]{2,1,0:T(8,128)S(1)}, f32[6,32,256]{2,1,0:T(8,128)S(1)}, u32[]{:S(2)}, u32[]{:S(2)}) %collective-permute-start.11) | collective-permute-done | bytes 196640 | tf_op jit(solution)/shard_map/ppermute | solution.py:204
  173.0 3.4 %collective-permute-done.10 = f32[6,32,256]{2,1,0:T(8,128)S(1)} collective-permute-done((f32[6,32,256]{2,1,0:T(8,128)S(1)}, f32[6,32,256]{2,1,0:T(8,128)S(1)}, u32[]{:S(2)}, u32[]{:S(2)}) %collective-permute-start.10) | collective-permute-done | bytes 196640 | tf_op jit(solution)/shard_map/ppermute | solution.py:204
  178.9 5.3 %collective-permute-done.12 = f32[6,32,128]{2,1,0:T(8,128)S(1)} collective-permute-done((f32[6,32,128]{2,1,0:T(8,128)S(1)}, f32[6,32,128]{2,1,0:T(8,128)S(1)}, u32[]{:S(2)}, u32[]{:S(2)}) %collective-permute-start.12) | collective-permute-done | bytes 98336 | tf_op jit(solution)/shard_map/ppermute | solution.py:314
  185.2 3.8 %collective-permute-done.13 = f32[6,32,64]{2,1,0:T(8,128)S(1)} collective-permute-done((f32[6,32,64]{2,1,0:T(8,128)S(1)}, f32[6,32,64]{2,1,0:T(8,128)S(1)}, u32[]{:S(2)}, u32[]{:S(2)}) %collective-permute-start.13) | collective-permute-done | bytes 49184 | tf_op jit(solution)/shard_map/ppermute | solution.py:314
  (52 shorter events, 12.4 us)
Async XLA Ops:
  0.6 54.4 %copy-start.6 = (s32[60]{0:T(128)S(1)}, s32[60]{0:T(128)}, u32[]{:S(2)}) copy-start(s32[60]{0:T(128)} %param.14) | copy-start | bytes 724
  0.6 54.5 %copy-start.7 = (s32[56]{0:T(128)S(1)}, s32[56]{0:T(128)}, u32[]{:S(2)}) copy-start(s32[56]{0:T(128)} %param.15) | copy-start | bytes 676
  2.7 9.3 %collective-permute-start = (bf16[512,768]{1,0:T(8,128)(2,1)}, bf16[512,768]{1,0:T(8,128)(2,1)S(1)}, u32[]{:S(2)}, u32[]{:S(2)}) collective-permute-start(bf16[512,768]{1,0:T(8,128)(2,1)} %shard_map.111.rows), channel_id=1, source_target_pairs={{0,0},{1,8},{2,16},{3,24},{4,1},{5,9},{6,17},{7,25},{8,18},{9,26},... | collective-permute-start | bytes 2359304 | tf_op jit(solution)/shard_map/ppermute | solution.py:40
  4.5 20.8 %collective-permute-start.1 = (bf16[512,768]{1,0:T(8,128)(2,1)}, bf16[512,768]{1,0:T(8,128)(2,1)S(1)}, u32[]{:S(2)}, u32[]{:S(2)}) collective-permute-start(bf16[512,768]{1,0:T(8,128)(2,1)} %shard_map.111.rows), channel_id=1, source_target_pairs={{0,8},{1,0},{2,24},{3,16},{4,9},{5,1},{6,25},{7,17},{8,26},{9,18},... | collective-permute-start | bytes 2359304 | tf_op jit(solution)/shard_map/ppermute | solution.py:40
  25.3 50.4 %collective-permute-start.2 = (bf16[512,768]{1,0:T(8,128)(2,1)}, bf16[512,768]{1,0:T(8,128)(2,1)S(1)}, u32[]{:S(2)}, u32[]{:S(2)}) collective-permute-start(bf16[512,768]{1,0:T(8,128)(2,1)} %shard_map.111.rows), channel_id=1, source_target_pairs={{0,16},{1,24},{2,0},{3,8},{4,17},{5,25},{6,1},{7,9},{8,2},{9,10},{... | collective-permute-start | bytes 2359304 | tf_op jit(solution)/shard_map/ppermute | solution.py:40
  49.8 35.0 %collective-permute-start.3 = (bf16[512,768]{1,0:T(8,128)(2,1)}, bf16[512,768]{1,0:T(8,128)(2,1)S(1)}, u32[]{:S(2)}, u32[]{:S(2)}) collective-permute-start(bf16[512,768]{1,0:T(8,128)(2,1)} %shard_map.111.rows), channel_id=1, source_target_pairs={{0,24},{1,16},{2,8},{3,0},{4,25},{5,17},{6,9},{7,1},{8,10},{9,2},{... | collective-permute-start | bytes 2359304 | tf_op jit(solution)/shard_map/ppermute | solution.py:40
  73.1 2.6 %copy-start = (f32[4,512,768]{2,1,0:T(8,128)}, f32[4,512,768]{2,1,0:T(8,128)S(1)}, u32[]{:S(2)}) copy-start(f32[4,512,768]{2,1,0:T(8,128)S(1)} %get-tuple-element.13.refs_3_) | copy-start | bytes 18874372
  96.1 12.7 %collective-permute-start.4 = (f32[4,512,768]{2,1,0:T(8,128)}, f32[4,512,768]{2,1,0:T(8,128)}, u32[]{:S(2)}, u32[]{:S(2)}) collective-permute-start(f32[4,512,768]{2,1,0:T(8,128)} %shard_map.113), channel_id=1, source_target_pairs={{0,1},{1,0},{2,3},{3,2},{4,5},{5,4},{6,7},{7,6},{8,9},{9,8},{10,11... | collective-permute-start | bytes 18874376 | tf_op jit(solution)/shard_map/ppermute | solution.py:200
  96.3 2.8 %copy-start.1 = (f32[4,512,768]{2,1,0:T(8,128)S(1)}, f32[4,512,768]{2,1,0:T(8,128)}, u32[]{:S(2)}) copy-start(f32[4,512,768]{2,1,0:T(8,128)} %copy-done) | copy-start | bytes 18874372
  115.0 22.5 %collective-permute-start.7 = (f16[512,768]{1,0:T(8,128)(2,1)}, f16[512,768]{1,0:T(8,128)(2,1)}, u32[]{:S(2)}, u32[]{:S(2)}) collective-permute-start(f16[512,768]{1,0:T(8,128)(2,1)} %get-tuple-element.17), channel_id=1, source_target_pairs={{0,6},{1,7},{2,4},{3,5},{4,2},{5,3},{6,0},{7,1},{8,14},{9,15},{10,... | collective-permute-start | bytes 2359304 | tf_op jit(solution)/shard_map/ppermute | solution.py:204
  118.7 35.4 %collective-permute-start.6 = (f16[512,768]{1,0:T(8,128)(2,1)S(1)}, f16[512,768]{1,0:T(8,128)(2,1)}, u32[]{:S(2)}, u32[]{:S(2)}) collective-permute-start(f16[512,768]{1,0:T(8,128)(2,1)S(1)} %get-tuple-element.18), channel_id=1, source_target_pairs={{0,4},{1,5},{2,6},{3,7},{4,0},{5,1},{6,2},{7,3},{8,12},{9,13},{10,... | collective-permute-start | bytes 2359304 | tf_op jit(solution)/shard_map/ppermute | solution.py:204
  118.7 35.4 %collective-permute-start.5 = (f16[512,768]{1,0:T(8,128)(2,1)S(1)}, f16[512,768]{1,0:T(8,128)(2,1)}, u32[]{:S(2)}, u32[]{:S(2)}) collective-permute-start(f16[512,768]{1,0:T(8,128)(2,1)S(1)} %get-tuple-element.16), channel_id=1, source_target_pairs={{0,2},{1,3},{2,0},{3,1},{4,6},{5,7},{6,4},{7,5},{8,10},{9,11},{10,... | collective-permute-start | bytes 2359304 | tf_op jit(solution)/shard_map/ppermute | solution.py:204
  154.1 2.2 %copy-start.2 = (bf16[512,768]{1,0:T(8,128)(2,1)S(1)}, bf16[512,768]{1,0:T(8,128)(2,1)}, u32[]{:S(2)}) copy-start(bf16[512,768]{1,0:T(8,128)(2,1)} %shard_map.111.rows) | copy-start | bytes 2359300
  154.1 2.2 %copy-start.3 = (bf16[3,256,256]{2,1,0:T(8,128)(2,1)S(1)}, bf16[3,256,256]{2,1,0:T(8,128)(2,1)}, u32[]{:S(2)}) copy-start(bf16[3,256,256]{2,1,0:T(8,128)(2,1)} %couple.1) | copy-start | bytes 1179652
  154.1 2.2 %copy-start.4 = (f32[3,256,256]{2,1,0:T(8,128)S(1)}, f32[3,256,256]{2,1,0:T(8,128)}, u32[]{:S(2)}) copy-start(f32[3,256,256]{2,1,0:T(8,128)} %ends.1) | copy-start | bytes 2359300
  160.3 2.6 %collective-permute-start.8 = (f32[4,6,32,256]{3,2,1,0:T(8,128)}, f32[4,6,32,256]{3,2,1,0:T(8,128)}, u32[]{:S(2)}, u32[]{:S(2)}) collective-permute-start(f32[4,6,32,256]{3,2,1,0:T(8,128)} %dynamic-slice_bitcast_fusion), channel_id=1, source_target_pairs={{0,1},{1,0},{2,3},{3,2},{4,5},{5,4},{6,7},{7,6},{8,9},{9,8},{10,11... | collective-permute-start | bytes 2359304 | tf_op jit(solution)/shard_map/ppermute | solution.py:200
  161.0 6.8 %copy-start.5 = (f32[512,256]{1,0:T(8,128)}, f32[512,256]{1,0:T(8,128)S(1)}, u32[]{:S(2)}) copy-start(f32[512,256]{1,0:T(8,128)S(1)} %fusion.3) | copy-start | bytes 1572868
  164.2 8.8 %collective-permute-start.11 = (f32[6,32,256]{2,1,0:T(8,128)S(1)}, f32[6,32,256]{2,1,0:T(8,128)S(1)}, u32[]{:S(2)}, u32[]{:S(2)}) collective-permute-start(f32[6,32,256]{2,1,0:T(8,128)S(1)} %get-tuple-element.20), channel_id=1, source_target_pairs={{0,6},{1,7},{2,4},{3,5},{4,2},{5,3},{6,0},{7,1},{8,14},{9,15},{10,... | collective-permute-start | bytes 589832 | tf_op jit(solution)/shard_map/ppermute | solution.py:204
  165.8 10.5 %collective-permute-start.10 = (f32[6,32,256]{2,1,0:T(8,128)S(1)}, f32[6,32,256]{2,1,0:T(8,128)S(1)}, u32[]{:S(2)}, u32[]{:S(2)}) collective-permute-start(f32[6,32,256]{2,1,0:T(8,128)S(1)} %get-tuple-element.21), channel_id=1, source_target_pairs={{0,4},{1,5},{2,6},{3,7},{4,0},{5,1},{6,2},{7,3},{8,12},{9,13},{10,... | collective-permute-start | bytes 589832 | tf_op jit(solution)/shard_map/ppermute | solution.py:204
  167.5 8.8 %collective-permute-start.9 = (f32[6,32,256]{2,1,0:T(8,128)S(1)}, f32[6,32,256]{2,1,0:T(8,128)S(1)}, u32[]{:S(2)}, u32[]{:S(2)}) collective-permute-start(f32[6,32,256]{2,1,0:T(8,128)S(1)} %get-tuple-element.19), channel_id=1, source_target_pairs={{0,2},{1,3},{2,0},{3,1},{4,6},{5,7},{6,4},{7,5},{8,10},{9,11},{10,... | collective-permute-start | bytes 589832 | tf_op jit(solution)/shard_map/ppermute | solution.py:204
  176.4 7.8 %collective-permute-start.12 = (f32[6,32,128]{2,1,0:T(8,128)S(1)}, f32[6,32,128]{2,1,0:T(8,128)S(1)}, u32[]{:S(2)}, u32[]{:S(2)}) collective-permute-start(f32[6,32,128]{2,1,0:T(8,128)S(1)} %constant_dynamic-slice_fusion.1), channel_id=1, source_target_pairs={{0,16},{8,24},{16,0},{24,8},{1,17},{9,25},{17,1},{25,9},{2,18},{10... | collective-permute-start | bytes 294920 | tf_op jit(solution)/shard_map/ppermute | solution.py:314
  184.3 4.7 %collective-permute-start.13 = (f32[6,32,64]{2,1,0:T(8,128)S(1)}, f32[6,32,64]{2,1,0:T(8,128)S(1)}, u32[]{:S(2)}, u32[]{:S(2)}) collective-permute-start(f32[6,32,64]{2,1,0:T(8,128)S(1)} %constant_dynamic-slice_fusion), channel_id=1, source_target_pairs={{0,8},{8,0},{16,24},{24,16},{1,9},{9,1},{17,25},{25,17},{2,10},{10... | collective-permute-start | bytes 147464 | tf_op jit(solution)/shard_map/ppermute | solution.py:314

commit v4 on v3

--- a/solution.py
+++ b/solution.py
@@ -44,7 +44,7 @@
     half = rows // 2
     early = [spread_step(own, step, rows, cols) for step in range(half)]
     late = [spread_step(after(own, early), half + step, rows, cols) for step in range(half)]
-    return [(0, early)], [(half, late)]
+    return (0, early), (half, late)
 
 
 def split_dot(former, latter, dims):
@@ -78,91 +78,68 @@
     return jnp.where(keeps[panel, row // span] > 0, value, jnp.zeros_like(value))
 
 
-def multiply_kernel(where, keeps, *refs, depth, span, runs, kinds, added):
-    s_refs, refs = refs[: len(runs)], refs[len(runs) :]
-    panel = refs[-1]
-    outs = refs[-1 - kinds : -1]
+def multiply_kernel(where, keeps, s_ref, *refs, depth, span, first, count, added):
+    out_ref, panel = refs[-2:]
 
     @pl.when((pl.program_id(0) == 0) & (pl.program_id(1) == 0))
     def _():
         unit = min(depth, span)
-        held = 0
-        for first, count in runs:
-            for step in range(count):
-                piece = refs[held + step]
-                place = where[0] ^ (first + step)
-                for part in range(0, depth, unit):
-                    begin = held * depth + place % count * depth + part
-                    target = pl.ds(pl.multiple_of(begin, unit), unit)
-                    row = where[3] + place * depth + part
-                    for index in range(panel.shape[1] // span):
-                        lanes = slice(index * span, (index + 1) * span)
-                        value = piece[part : part + unit, lanes]
-                        panel[target, lanes] = kept(keeps, index, row, span, value)
-            held += count
-
-    result = refs[-2 - kinds][0] if added else None
-    begin = 0
-    for s_ref in s_refs:
-        end = begin + s_ref.shape[1]
-        partial = split_dot(s_ref[...], panel[begin:end, :], ((1,), (0,)))
-        result = partial if result is None else result + partial
-        begin = end
-    for kind, out_ref in enumerate(outs):
-
-        @pl.when(pl.program_id(0) == kind)
-        def _():
-            out_ref[0] = result
-
-
-def multiply(where, keeps, ancestor, runs, span, kinds, added=None):
-    local_rows = ancestor.shape[0]
-    pieces = [piece for _, run in runs for piece in run]
+        for step in range(count):
+            place = where[0] ^ (first + step)
+            for part in range(0, depth, unit):
+                target = pl.ds(pl.multiple_of(place % count * depth + part, unit), unit)
+                row = where[3] + place * depth + part
+                for index in range(panel.shape[1] // span):
+                    lanes = slice(index * span, (index + 1) * span)
+                    value = refs[step][part : part + unit, lanes]
+                    panel[target, lanes] = kept(keeps, index, row, span, value)
+
+    result = split_dot(s_ref[...], panel[...], ((1,), (0,)))
+    if added:
+        result += refs[count][0, 0]
+    out_ref[0, 0] = result
+
+
+def multiply(where, keeps, ancestor, run, span, kinds, added=None):
+    first, pieces = run
+    count = len(pieces)
     slab_rows, width = pieces[0].shape
-    chips = local_rows // slab_rows // 2
-
-    def block_of(first, count):
-        def at(h, i, where, keeps):
-            kind = jnp.where(h == 0, where[1], 1 - where[1])
-            return 2 * i + kind, (where[0] ^ first) // count
-
-        return pl.BlockSpec((slab_rows, count * slab_rows), at)
-
-    def out_at(kind):
-        if kind == 0:
-            return lambda h, i, *at: (jnp.where(h == 0, i, chips - 1), 0, 0)
-        return lambda h, i, *at: (i * h, 0, 0)
-
-    counts = tuple((first, len(run)) for first, run in runs)
-    part = (1, slab_rows, width)
+    chips = ancestor.shape[0] // slab_rows // 2
+    base = kinds[0]
+
+    def rows_at(h, i, where, keeps):
+        kind = jnp.where(h + base == 1, where[1], 1 - where[1])
+        return 2 * i + kind, (where[0] ^ first) // count
+
     extra = [] if added is None else [added]
+    part = (1, 1, slab_rows, width)
     return pl.pallas_call(
         functools.partial(
             multiply_kernel,
             depth=slab_rows,
             span=span,
-            runs=counts,
-            kinds=kinds,
+            first=first,
+            count=count,
             added=len(extra),
         ),
         grid_spec=pltpu.PrefetchScalarGridSpec(
             num_scalar_prefetch=2,
-            grid=(kinds, chips),
-            in_specs=[block_of(*run) for run in counts]
+            grid=(len(kinds), chips),
+            in_specs=[pl.BlockSpec((slab_rows, count * slab_rows), rows_at)]
             + [pl.BlockSpec(piece.shape, lambda *at: (0, 0)) for piece in pieces]
-            + [pl.BlockSpec(part, out_at(0)) for _ in extra],
-            out_specs=[pl.BlockSpec(part, out_at(kind)) for kind in range(kinds)],
-            scratch_shapes=[pltpu.VMEM((len(pieces) * slab_rows, width), BF16)],
+            + [pl.BlockSpec(part, lambda h, i, *at: (h + base, i, 0, 0)) for _ in extra],
+            out_specs=pl.BlockSpec(part, lambda h, i, *at: (h, i, 0, 0)),
+            scratch_shapes=[pltpu.VMEM((count * slab_rows, width), BF16)],
         ),
-        out_shape=[jax.ShapeDtypeStruct((chips, slab_rows, width), F32)] * kinds,
-        compiler_params=pltpu.CompilerParams(vmem_limit_bytes=34 * 1024 * 1024),
+        out_shape=jax.ShapeDtypeStruct((len(kinds), chips, slab_rows, width), F32),
+        compiler_params=pltpu.CompilerParams(vmem_limit_bytes=21 * 1024 * 1024),
         cost_estimate=LITTLE,
-    )(where, keeps, *([ancestor] * len(runs)), *pieces, *extra)
+    )(where, keeps, ancestor, *pieces, *extra)
 
 
 def sum_kernel(where, mine_ref, handed_ref, own_ref, sent_ref):
     step = pl.program_id(0)
-    summed = mine_ref[0] + handed_ref[0]
+    summed = mine_ref[0, 0] + handed_ref[0, 0]
 
     @pl.when(step == 0)
     def _():
@@ -174,8 +151,8 @@
 
 
 def chip_sum(where, mine, handed):
-    chips, depth, width = mine.shape
-    taken = pl.BlockSpec((1, depth, width), lambda i, where: (where[2] ^ i, 0, 0))
+    chips, depth, width = mine.shape[1:]
+    taken = pl.BlockSpec((1, 1, depth, width), lambda i, where: (0, where[2] ^ i, 0, 0))
     return pl.pallas_call(
         sum_kernel,
         grid_spec=pltpu.PrefetchScalarGridSpec(
@@ -191,7 +168,7 @@
             jax.ShapeDtypeStruct((depth, width), F32),
             jax.ShapeDtypeStruct((chips - 1, depth, width), F32),
         ],
-        compiler_params=pltpu.CompilerParams(vmem_limit_bytes=24 * 1024 * 1024),
+        compiler_params=pltpu.CompilerParams(vmem_limit_bytes=14 * 1024 * 1024),
         cost_estimate=LITTLE,
     )(where, mine, handed)
 
@@ -232,7 +209,7 @@
     return total
 
 
-def small_kernel(where, keeps, sums, rows, couple, ends, out_ref):
+def small_kernel(where, keeps, sums, rows, couple, ends, stay_ref, give_ref):
     start, inner = ((0,), (0,)), ((1,), (0,))
     c_zero, c_one, c_two = couple[0], couple[1], couple[2]
     width = c_zero.shape[0]
@@ -277,12 +254,20 @@
         - turned(c_one, cross_first)
         - turned(c_two, cross_second)
     )
-    part = out_ref.shape[3]
+    part = stay_ref.shape[2]
     blocks = (diag_one, diag_two, diag_three, cross_two, cross_first, cross_second)
     for index, value in enumerate(blocks):
         value = value.T
         for place in range(width // part):
-            out_ref[place % 2, place // 2, index] = value[place * part : (place + 1) * part, :]
+            strip = value[place * part : (place + 1) * part, :]
+
+            @pl.when(where[1] == place % 2)
+            def _():
+                stay_ref[place // 2, index] = strip
+
+            @pl.when(where[1] != place % 2)
+            def _():
+                give_ref[place // 2, index] = strip
 
 
 def small_parts(where, keeps, sums, rows, couplings, ends, cols):
@@ -292,16 +277,16 @@
     return pl.pallas_call(
         small_kernel,
         in_specs=[scalars] * 2 + [whole] * 4,
-        out_specs=whole,
-        out_shape=jax.ShapeDtypeStruct((2, cols // 2, 6, width // cols, width), F32),
-        compiler_params=pltpu.CompilerParams(vmem_limit_bytes=24 * 1024 * 1024),
+        out_specs=[whole] * 2,
+        out_shape=[jax.ShapeDtypeStruct((cols // 2, 6, width // cols, width), F32)] * 2,
+        compiler_params=pltpu.CompilerParams(vmem_limit_bytes=16 * 1024 * 1024),
         cost_estimate=LITTLE,
     )(where, keeps, sums, rows, couplings, ends)
 
 
-def tile_scatter(split, rows, cols):
-    row, core, chip = lax.axis_index("row"), lax.axis_index("col") % 2, lax.axis_index("col") // 2
-    held = take(split, core) + sibling(take(split, 1 - core), cols)
+def tile_scatter(stay, give, rows, cols):
+    row, chip = lax.axis_index("row"), lax.axis_index("col") // 2
+    held = stay + sibling(give, cols)
     arrived = [to_chip(take(held, chip ^ step), step, cols) for step in range(1, cols // 2)]
     held = functools.reduce(jnp.add, arrived, take(held, chip))
     bit = rows // 2
@@ -336,7 +321,6 @@
     others = [chip, col_id * ancestor.shape[1], device * slab_rows]
     turned_row = row_id ^ swap_of(col_id // (cols // rows), rows)
     where = jnp.stack([turned_row, core] + others).astype(jnp.int32)
-    other_where = jnp.stack([turned_row, 1 - core] + others).astype(jnp.int32)
     keep_two = piece_keep(list_two, device * slab_rows, slab_rows, block_width)
     keep_three = piece_keep(list_three, device * slab_rows, slab_rows, block_width)
     blocks = jnp.arange(ancestor.shape[0] * rows // block_width, dtype=jnp.int32)
@@ -346,17 +330,16 @@
 
     own_rows = join([panel_one, panel_two, panel_three])
     early, late = spread(own_rows, rows, cols)
-    shared = (keeps, ancestor)
-    theirs, mine = multiply(other_where, *shared, early, block_width, 2)
-    (theirs,) = multiply(other_where, *shared, late, block_width, 1, theirs)
+    sums = multiply(where, keeps, ancestor, early, block_width, (0, 1))
+    theirs = multiply(where, keeps, ancestor, late, block_width, (0,), sums)
     handed = sibling(theirs, cols)
     turn = after(where, theirs)
-    (mine,) = multiply(turn, *shared, late, block_width, 1, mine)
+    mine = multiply(turn, keeps, ancestor, late, block_width, (1,), sums)
     own, sent = chip_sum(where, mine, handed)
     payloads = [sent[step].astype(F16) for step in range(cols // 2 - 1)]
     total = collect(own, hand_over(payloads, cols))
     parts = small_parts(where, keeps, total, own_rows, couplings, diag_terms, cols)
-    own_tile = tile_scatter(parts, rows, cols)
+    own_tile = tile_scatter(*parts, rows, cols)
     sum_one = total[:, :block_width]
     sum_two = total[:, block_width : 2 * block_width]
     sum_three = total[:, 2 * block_width :]

time: 190 us -> 181 us (0.953)
  local copies, waits for them, and re-layouts: 8.15 us -> 1.76 us
  Pallas kernels: 48.1 us -> 45 us
  other arithmetic: 5.9 us -> 3.03 us
  waiting for transfers between devices: 76.3 us -> 78.9 us
    unnamed x16 -> x12, local copies, waits for them, and re-layouts: 5.45 us -> 1.03 us
    ppermute x4, waiting for transfers between devices: 22.4 us -> 25.8 us  [spread_step(): return lax.ppermute(own, ('row', 'col'), pairs)]
    pallas_call x1, Pallas kernels: 4.49 us -> 1.65 us  [chip_sum(): pl.pallas_call(sum_kernel, grid_spec=pltpu.PrefetchScalarGridSpec(num_sca...]
    pallas_call x3, Pallas kernels: 38.6 us -> 36.3 us  [multiply(): pl.pallas_call(functools.partial(multiply_kernel, depth=slab_rows, span=s...]
    pallas_call x1, Pallas kernels: 2.95 us -> 5.01 us  [small_parts(): pl.pallas_call(small_kernel, in_specs=[scalars] * 2 + [whole] * 4, out_sp...]
  transfers between devices with their start and end apart: 14 -> 14, of which waited for: 9 -> 10; matrix products, arithmetic and copies ran while one was open for 2% -> 2% of each run, Pallas kernels for 14% -> 15%
where the time goes in v4:
time: 181 us
  waiting for transfers between devices  78.9 us (44%)
  starting transfers between devices  48.9 us (27%)
  Pallas kernels  45 us (25%)
  other arithmetic  3.03 us (2%)
  matrix products  1.97 us (1%)
    ppermute x6, waiting for transfers between devices, to_chip(): return lax.ppermute(value, 'col', [(c, c ^ 2 * step) for c in range(cols)])  42.2 us
    ppermute x4, starting transfers between devices, spread_step(): return lax.ppermute(own, ('row', 'col'), pairs)  38.9 us
    pallas_call x3, Pallas kernels, multiply(): pl.pallas_call(functools.partial(multiply_kernel, depth=slab_rows, span=s...  36.3 us
    ppermute x4, waiting for transfers between devices, spread_step(): return lax.ppermute(own, ('row', 'col'), pairs)  25.8 us
    ppermute x2, waiting for transfers between devices, tile_scatter(): held = mine + lax.ppermute(theirs, 'row', pairs)  8.75 us
    ppermute x6, starting transfers between devices, to_chip(): return lax.ppermute(value, 'col', [(c, c ^ 2 * step) for c in range(cols)])  8.1 us
    pallas_call x1, Pallas kernels, small_parts(): pl.pallas_call(small_kernel, in_specs=[scalars] * 2 + [whole] * 4, out_sp...  5.01 us
  transfers between devices with their start and end apart: 14, of which 10 were waited for; matrix products, arithmetic and copies ran while one was open for 2% of the time, Pallas kernels for 15%

profile of v4, /device:TPU:0, one launch (start us, length us, event | category | flops | bytes accessed | tf_op | source)
XLA Modules:
  0.0 180.5 jit_solution(17259635747548092706)
XLA Ops:
  0.7 2.1 %shard_map.111.rows = bf16[512,768]{1,0:T(8,128)(2,1)} custom-call(bf16[512,256]{1,0:T(8,128)(2,1)} %refs_0_.1, bf16[512,256]{1,0:T(8,128)(2,1)} %refs_1_.1, bf16[512,256]{1,0:T(8,128)(2,1)} %refs_2_.1), custom_call_target="tpu_custom_call" | custom-call | flops 1 | bytes 1 | tf_op jit(solution)/shard_map/pallas_call | solution.py:68
  2.7 1.8 collective-permute-start
  4.5 7.6 %collective-permute-start.1 = (bf16[512,768]{1,0:T(8,128)(2,1)}, bf16[512,768]{1,0:T(8,128)(2,1)S(1)}, u32[]{:S(2)}, u32[]{:S(2)}) collective-permute-start(bf16[512,768]{1,0:T(8,128)(2,1)} %shard_map.111.rows), channel_id=1, source_target_pairs={{0,8},{1,0},{2,24},{3,16},{4,9},{5,1},{6,25},{7,17},{8,26},{9,18},... | collective-permute-start | bytes 2359304 | tf_op jit(solution)/shard_map/ppermute | solution.py:40
  12.1 13.2 %collective-permute-done.1.refs_1_ = bf16[512,768]{1,0:T(8,128)(2,1)S(1)} collective-permute-done((bf16[512,768]{1,0:T(8,128)(2,1)}, bf16[512,768]{1,0:T(8,128)(2,1)S(1)}, u32[]{:S(2)}, u32[]{:S(2)}) %collective-permute-start.1) | collective-permute-done | bytes 786464 | tf_op jit(solution)/shard_map/ppermute | solution.py:40
  25.3 24.5 %collective-permute-start.2 = (bf16[512,768]{1,0:T(8,128)(2,1)}, bf16[512,768]{1,0:T(8,128)(2,1)S(1)}, u32[]{:S(2)}, u32[]{:S(2)}) collective-permute-start(bf16[512,768]{1,0:T(8,128)(2,1)} %shard_map.111.rows), channel_id=1, source_target_pairs={{0,16},{1,24},{2,0},{3,8},{4,17},{5,25},{6,1},{7,9},{8,2},{9,10},{... | collective-permute-start | bytes 2359304 | tf_op jit(solution)/shard_map/ppermute | solution.py:40
  49.8 5.1 %collective-permute-start.3 = (bf16[512,768]{1,0:T(8,128)(2,1)}, bf16[512,768]{1,0:T(8,128)(2,1)S(1)}, u32[]{:S(2)}, u32[]{:S(2)}) collective-permute-start(bf16[512,768]{1,0:T(8,128)(2,1)} %shard_map.111.rows), channel_id=1, source_target_pairs={{0,24},{1,16},{2,8},{3,0},{4,25},{5,17},{6,9},{7,1},{8,10},{9,2},{... | collective-permute-start | bytes 2359304 | tf_op jit(solution)/shard_map/ppermute | solution.py:40
  55.3 17.0 %shard_map.112.refs_2_ = f32[2,4,512,768]{3,2,1,0:T(8,128)S(1)} custom-call(s32[5]{0:T(128)S(1)} %stack.32.where, s32[3,64]{1,0:T(4,128)S(1)} %add_convert_fusion.keeps, f32[4096,2048]{1,0:T(8,128)} %s_ref.5, bf16[512,768]{1,0:T(8,128)(2,1)S(1)} %collective-permute-done.refs_0_, bf16[512,768]{1,0:T(8,128)(2,1)S(1)} %collective-permute-done.1.refs_1_), custom_call_target="tpu_custom_call" | custom-call | flops 1 | bytes 1 | tf_op jit(solution)/shard_map/pallas_call | solution.py:116
  72.3 12.5 %collective-permute-done.3.refs_1_ = bf16[512,768]{1,0:T(8,128)(2,1)S(1)} collective-permute-done((bf16[512,768]{1,0:T(8,128)(2,1)}, bf16[512,768]{1,0:T(8,128)(2,1)S(1)}, u32[]{:S(2)}, u32[]{:S(2)}) %collective-permute-start.3) | collective-permute-done | bytes 786464 | tf_op jit(solution)/shard_map/ppermute | solution.py:40
  84.9 9.7 %shard_map.113 = f32[1,4,512,768]{3,2,1,0:T(8,128)S(1)} custom-call(s32[5]{0:T(128)S(1)} %stack.32.where, s32[3,64]{1,0:T(4,128)S(1)} %add_convert_fusion.keeps, f32[4096,2048]{1,0:T(8,128)} %s_ref.5, bf16[512,768]{1,0:T(8,128)(2,1)S(1)} %collective-permute-done.2.refs_0_, bf16[512,768]{1,0:T(8,128)(2,1)S(1)} %collective-permute-done.3.refs_1_, ...), custom_call_target="tpu_custom_call" | custom-call | flops 1 | bytes 1 | tf_op jit(solution)/shard_map/pallas_call | solution.py:116
  94.7 9.7 %shard_map.114.mine_ref = f32[1,4,512,768]{3,2,1,0:T(8,128)S(1)} custom-call(s32[5]{0:T(128)S(1)} %stack.32.where, s32[3,64]{1,0:T(4,128)S(1)} %add_convert_fusion.keeps, f32[4096,2048]{1,0:T(8,128)} %s_ref.5, bf16[512,768]{1,0:T(8,128)(2,1)S(1)} %collective-permute-done.2.refs_0_, bf16[512,768]{1,0:T(8,128)(2,1)S(1)} %collective-permute-done.3.refs_1_, ...), custom_call_target="tpu_custom_call" | custom-call | flops 1 | bytes 1 | tf_op jit(solution)/shard_map/pallas_call | solution.py:116
  104.8 1.6 shard_map.115
  107.2 3.9 %collective-permute-start.7 = (f16[512,768]{1,0:T(8,128)(2,1)S(1)}, f16[512,768]{1,0:T(8,128)(2,1)S(1)}, u32[]{:S(2)}, u32[]{:S(2)}) collective-permute-start(f16[512,768]{1,0:T(8,128)(2,1)S(1)} %get-tuple-element.17), channel_id=1, source_target_pairs={{0,6},{1,7},{2,4},{3,5},{4,2},{5,3},{6,0},{7,1},{8,14},{9,15},{10,... | collective-permute-start | bytes 2359304 | tf_op jit(solution)/shard_map/ppermute | solution.py:181
  111.8 17.7 %collective-permute-done.7 = f16[512,768]{1,0:T(8,128)(2,1)S(1)} collective-permute-done((f16[512,768]{1,0:T(8,128)(2,1)S(1)}, f16[512,768]{1,0:T(8,128)(2,1)S(1)}, u32[]{:S(2)}, u32[]{:S(2)}) %collective-permute-start.7) | collective-permute-done | bytes 786464 | tf_op jit(solution)/shard_map/ppermute | solution.py:181
  129.5 16.3 %collective-permute-done.6 = f16[512,768]{1,0:T(8,128)(2,1)S(1)} collective-permute-done((f16[512,768]{1,0:T(8,128)(2,1)S(1)}, f16[512,768]{1,0:T(8,128)(2,1)S(1)}, u32[]{:S(2)}, u32[]{:S(2)}) %collective-permute-start.6) | collective-permute-done | bytes 786464 | tf_op jit(solution)/shard_map/ppermute | solution.py:181
  147.3 5.0 %shard_map.116 = (f32[4,6,32,256]{3,2,1,0:T(8,128)S(1)}, f32[4,6,32,256]{3,2,1,0:T(8,128)}) custom-call(s32[5]{0:T(128)S(1)} %stack.32.where, s32[3,64]{1,0:T(4,128)S(1)} %add_convert_fusion.keeps, f32[512,768]{1,0:T(8,128)S(1)} %multiply_add_fusion.sums, bf16[512,768]{1,0:T(8,128)(2,1)S(1)} %copy-done, bf16[3,256,256]{2,1,0:T(8,128)(2,1)S(1)} %copy-done.1, ...), custom_call_target="tpu_custom_call" | custom-call | flops 1 | bytes 1 | tf_op jit(solution)/shard_map/pallas_call | solution.py:277
  153.0 1.8 collective-permute-done.8
  155.0 1.9 %collective-permute-start.11 = (f32[6,32,256]{2,1,0:T(8,128)S(1)}, f32[6,32,256]{2,1,0:T(8,128)S(1)}, u32[]{:S(2)}, u32[]{:S(2)}) collective-permute-start(f32[6,32,256]{2,1,0:T(8,128)S(1)} %get-tuple-element.20), channel_id=1, source_target_pairs={{0,6},{1,7},{2,4},{3,5},{4,2},{5,3},{6,0},{7,1},{8,14},{9,15},{10,... | collective-permute-start | bytes 589832 | tf_op jit(solution)/shard_map/ppermute | solution.py:181
  156.9 1.4 collective-permute-start.10
  158.9 4.8 %collective-permute-done.11 = f32[6,32,256]{2,1,0:T(8,128)S(1)} collective-permute-done((f32[6,32,256]{2,1,0:T(8,128)S(1)}, f32[6,32,256]{2,1,0:T(8,128)S(1)}, u32[]{:S(2)}, u32[]{:S(2)}) %collective-permute-start.11) | collective-permute-done | bytes 196640 | tf_op jit(solution)/shard_map/ppermute | solution.py:181
  163.8 3.4 %collective-permute-done.10 = f32[6,32,256]{2,1,0:T(8,128)S(1)} collective-permute-done((f32[6,32,256]{2,1,0:T(8,128)S(1)}, f32[6,32,256]{2,1,0:T(8,128)S(1)}, u32[]{:S(2)}, u32[]{:S(2)}) %collective-permute-start.10) | collective-permute-done | bytes 196640 | tf_op jit(solution)/shard_map/ppermute | solution.py:181
  167.2 1.6 collective-permute-start.12
  168.8 1.2 fusion.1
  170.0 5.0 %collective-permute-done.12 = f32[6,32,128]{2,1,0:T(8,128)S(1)} collective-permute-done((f32[6,32,128]{2,1,0:T(8,128)S(1)}, f32[6,32,128]{2,1,0:T(8,128)S(1)}, u32[]{:S(2)}, u32[]{:S(2)}) %collective-permute-start.12) | collective-permute-done | bytes 98336 | tf_op jit(solution)/shard_map/ppermute | solution.py:299
  176.0 3.8 %collective-permute-done.13 = f32[6,32,64]{2,1,0:T(8,128)S(1)} collective-permute-done((f32[6,32,64]{2,1,0:T(8,128)S(1)}, f32[6,32,64]{2,1,0:T(8,128)S(1)}, u32[]{:S(2)}, u32[]{:S(2)}) %collective-permute-start.13) | collective-permute-done | bytes 49184 | tf_op jit(solution)/shard_map/ppermute | solution.py:299
  (46 shorter events, 7.1 us)
Async XLA Ops:
  0.6 54.4 %copy-start.4 = (s32[60]{0:T(128)S(1)}, s32[60]{0:T(128)}, u32[]{:S(2)}) copy-start(s32[60]{0:T(128)} %param.14) | copy-start | bytes 724
  0.6 54.5 %copy-start.5 = (s32[56]{0:T(128)S(1)}, s32[56]{0:T(128)}, u32[]{:S(2)}) copy-start(s32[56]{0:T(128)} %param.15) | copy-start | bytes 676
  2.7 9.3 %collective-permute-start = (bf16[512,768]{1,0:T(8,128)(2,1)}, bf16[512,768]{1,0:T(8,128)(2,1)S(1)}, u32[]{:S(2)}, u32[]{:S(2)}) collective-permute-start(bf16[512,768]{1,0:T(8,128)(2,1)} %shard_map.111.rows), channel_id=1, source_target_pairs={{0,0},{1,8},{2,16},{3,24},{4,1},{5,9},{6,17},{7,25},{8,18},{9,26},... | collective-permute-start | bytes 2359304 | tf_op jit(solution)/shard_map/ppermute | solution.py:40
  4.5 20.8 %collective-permute-start.1 = (bf16[512,768]{1,0:T(8,128)(2,1)}, bf16[512,768]{1,0:T(8,128)(2,1)S(1)}, u32[]{:S(2)}, u32[]{:S(2)}) collective-permute-start(bf16[512,768]{1,0:T(8,128)(2,1)} %shard_map.111.rows), channel_id=1, source_target_pairs={{0,8},{1,0},{2,24},{3,16},{4,9},{5,1},{6,25},{7,17},{8,26},{9,18},... | collective-permute-start | bytes 2359304 | tf_op jit(solution)/shard_map/ppermute | solution.py:40
  25.3 47.0 %collective-permute-start.2 = (bf16[512,768]{1,0:T(8,128)(2,1)}, bf16[512,768]{1,0:T(8,128)(2,1)S(1)}, u32[]{:S(2)}, u32[]{:S(2)}) collective-permute-start(bf16[512,768]{1,0:T(8,128)(2,1)} %shard_map.111.rows), channel_id=1, source_target_pairs={{0,16},{1,24},{2,0},{3,8},{4,17},{5,25},{6,1},{7,9},{8,2},{9,10},{... | collective-permute-start | bytes 2359304 | tf_op jit(solution)/shard_map/ppermute | solution.py:40
  49.8 35.0 %collective-permute-start.3 = (bf16[512,768]{1,0:T(8,128)(2,1)}, bf16[512,768]{1,0:T(8,128)(2,1)S(1)}, u32[]{:S(2)}, u32[]{:S(2)}) collective-permute-start(bf16[512,768]{1,0:T(8,128)(2,1)} %shard_map.111.rows), channel_id=1, source_target_pairs={{0,24},{1,16},{2,8},{3,0},{4,25},{5,17},{6,9},{7,1},{8,10},{9,2},{... | collective-permute-start | bytes 2359304 | tf_op jit(solution)/shard_map/ppermute | solution.py:40
  94.5 10.2 %collective-permute-start.4 = (f32[1,4,512,768]{3,2,1,0:T(8,128)S(1)}, f32[1,4,512,768]{3,2,1,0:T(8,128)S(1)}, u32[]{:S(2)}, u32[]{:S(2)}) collective-permute-start(f32[1,4,512,768]{3,2,1,0:T(8,128)S(1)} %shard_map.113), channel_id=1, source_target_pairs={{0,1},{1,0},{2,3},{3,2},{4,5},{5,4},{6,7},{7,6},{8,9},{9,8},{10,11... | collective-permute-start | bytes 18874376 | tf_op jit(solution)/shard_map/ppermute | solution.py:177
  107.2 22.3 %collective-permute-start.7 = (f16[512,768]{1,0:T(8,128)(2,1)S(1)}, f16[512,768]{1,0:T(8,128)(2,1)S(1)}, u32[]{:S(2)}, u32[]{:S(2)}) collective-permute-start(f16[512,768]{1,0:T(8,128)(2,1)S(1)} %get-tuple-element.17), channel_id=1, source_target_pairs={{0,6},{1,7},{2,4},{3,5},{4,2},{5,3},{6,0},{7,1},{8,14},{9,15},{10,... | collective-permute-start | bytes 2359304 | tf_op jit(solution)/shard_map/ppermute | solution.py:181
  111.1 34.7 %collective-permute-start.6 = (f16[512,768]{1,0:T(8,128)(2,1)S(1)}, f16[512,768]{1,0:T(8,128)(2,1)S(1)}, u32[]{:S(2)}, u32[]{:S(2)}) collective-permute-start(f16[512,768]{1,0:T(8,128)(2,1)S(1)} %get-tuple-element.18), channel_id=1, source_target_pairs={{0,4},{1,5},{2,6},{3,7},{4,0},{5,1},{6,2},{7,3},{8,12},{9,13},{10,... | collective-permute-start | bytes 2359304 | tf_op jit(solution)/shard_map/ppermute | solution.py:181
  111.1 34.7 %collective-permute-start.5 = (f16[512,768]{1,0:T(8,128)(2,1)S(1)}, f16[512,768]{1,0:T(8,128)(2,1)S(1)}, u32[]{:S(2)}, u32[]{:S(2)}) collective-permute-start(f16[512,768]{1,0:T(8,128)(2,1)S(1)} %get-tuple-element.16), channel_id=1, source_target_pairs={{0,2},{1,3},{2,0},{3,1},{4,6},{5,7},{6,4},{7,5},{8,10},{9,11},{10,... | collective-permute-start | bytes 2359304 | tf_op jit(solution)/shard_map/ppermute | solution.py:181
  145.8 1.1 copy-start
  145.8 1.2 copy-start.1
  145.8 1.5 copy-start.2
  152.3 2.5 %collective-permute-start.8 = (f32[4,6,32,256]{3,2,1,0:T(8,128)}, f32[4,6,32,256]{3,2,1,0:T(8,128)S(1)}, u32[]{:S(2)}, u32[]{:S(2)}) collective-permute-start(f32[4,6,32,256]{3,2,1,0:T(8,128)} %get-tuple-element.15), channel_id=1, source_target_pairs={{0,1},{1,0},{2,3},{3,2},{4,5},{5,4},{6,7},{7,6},{8,9},{9,8},{10,11... | collective-permute-start | bytes 2359304 | tf_op jit(solution)/shard_map/ppermute | solution.py:177
  153.0 5.5 %copy-start.3 = (f32[512,256]{1,0:T(8,128)}, f32[512,256]{1,0:T(8,128)S(1)}, u32[]{:S(2)}) copy-start(f32[512,256]{1,0:T(8,128)S(1)} %fusion.3) | copy-start | bytes 1572868
  155.0 8.8 %collective-permute-start.11 = (f32[6,32,256]{2,1,0:T(8,128)S(1)}, f32[6,32,256]{2,1,0:T(8,128)S(1)}, u32[]{:S(2)}, u32[]{:S(2)}) collective-permute-start(f32[6,32,256]{2,1,0:T(8,128)S(1)} %get-tuple-element.20), channel_id=1, source_target_pairs={{0,6},{1,7},{2,4},{3,5},{4,2},{5,3},{6,0},{7,1},{8,14},{9,15},{10,... | collective-permute-start | bytes 589832 | tf_op jit(solution)/shard_map/ppermute | solution.py:181
  156.9 10.3 %collective-permute-start.10 = (f32[6,32,256]{2,1,0:T(8,128)S(1)}, f32[6,32,256]{2,1,0:T(8,128)S(1)}, u32[]{:S(2)}, u32[]{:S(2)}) collective-permute-start(f32[6,32,256]{2,1,0:T(8,128)S(1)} %get-tuple-element.21), channel_id=1, source_target_pairs={{0,4},{1,5},{2,6},{3,7},{4,0},{5,1},{6,2},{7,3},{8,12},{9,13},{10,... | collective-permute-start | bytes 589832 | tf_op jit(solution)/shard_map/ppermute | solution.py:181
  158.3 8.8 %collective-permute-start.9 = (f32[6,32,256]{2,1,0:T(8,128)S(1)}, f32[6,32,256]{2,1,0:T(8,128)S(1)}, u32[]{:S(2)}, u32[]{:S(2)}) collective-permute-start(f32[6,32,256]{2,1,0:T(8,128)S(1)} %get-tuple-element.19), channel_id=1, source_target_pairs={{0,2},{1,3},{2,0},{3,1},{4,6},{5,7},{6,4},{7,5},{8,10},{9,11},{10,... | collective-permute-start | bytes 589832 | tf_op jit(solution)/shard_map/ppermute | solution.py:181
  167.2 7.8 %collective-permute-start.12 = (f32[6,32,128]{2,1,0:T(8,128)S(1)}, f32[6,32,128]{2,1,0:T(8,128)S(1)}, u32[]{:S(2)}, u32[]{:S(2)}) collective-permute-start(f32[6,32,128]{2,1,0:T(8,128)S(1)} %constant_dynamic-slice_fusion.1), channel_id=1, source_target_pairs={{0,16},{8,24},{16,0},{24,8},{1,17},{9,25},{17,1},{25,9},{2,18},{10... | collective-permute-start | bytes 294920 | tf_op jit(solution)/shard_map/ppermute | solution.py:299
  175.1 4.7 %collective-permute-start.13 = (f32[6,32,64]{2,1,0:T(8,128)S(1)}, f32[6,32,64]{2,1,0:T(8,128)S(1)}, u32[]{:S(2)}, u32[]{:S(2)}) collective-permute-start(f32[6,32,64]{2,1,0:T(8,128)S(1)} %constant_dynamic-slice_fusion), channel_id=1, source_target_pairs={{0,8},{8,0},{16,24},{24,16},{1,9},{9,1},{17,25},{25,17},{2,10},{10... | collective-permute-start | bytes 147464 | tf_op jit(solution)/shard_map/ppermute | solution.py:299

commit v5 on v4

--- a/solution.py
+++ b/solution.py
@@ -10,7 +10,10 @@
 F32 = jnp.float32
 BF16 = jnp.bfloat16
 F16 = jnp.float16
-SCALE = 32.0
+TOP = 2.0**15
+FLOOR = 2.0**-14
+SUBLANES = 8
+TAIL = 16
 LITTLE = pl.CostEstimate(flops=1, bytes_accessed=1, transcendentals=0)
 
 
@@ -140,19 +143,25 @@
 def sum_kernel(where, mine_ref, handed_ref, own_ref, sent_ref):
     step = pl.program_id(0)
     summed = mine_ref[0, 0] + handed_ref[0, 0]
+    depth, width = summed.shape
 
     @pl.when(step == 0)
     def _():
-        own_ref[...] = summed
+        own_ref[:depth, :] = summed
+        own_ref[depth:, :] = jnp.zeros((TAIL, width), F32)
 
     @pl.when(step > 0)
     def _():
-        sent_ref[0] = summed * SCALE
+        most = jnp.max(jnp.abs(summed), axis=(0, 1), keepdims=True)
+        unit = jnp.maximum(most, FLOOR).astype(BF16).astype(F32)
+        sent_ref[0, :depth, :] = summed * (TOP / unit)
+        sent_ref[0, depth:, :] = jnp.broadcast_to(unit, (TAIL, width))
 
 
 def chip_sum(where, mine, handed):
     chips, depth, width = mine.shape[1:]
     taken = pl.BlockSpec((1, 1, depth, width), lambda i, where: (0, where[2] ^ i, 0, 0))
+    longer = depth + TAIL
     return pl.pallas_call(
         sum_kernel,
         grid_spec=pltpu.PrefetchScalarGridSpec(
@@ -160,15 +169,15 @@
             grid=(chips,),
             in_specs=[taken, taken],
             out_specs=[
-                pl.BlockSpec((depth, width), lambda *at: (0, 0)),
-                pl.BlockSpec((1, depth, width), lambda i, *at: (jnp.maximum(i - 1, 0), 0, 0)),
+                pl.BlockSpec((longer, width), lambda *at: (0, 0)),
+                pl.BlockSpec((1, longer, width), lambda i, *at: (jnp.maximum(i - 1, 0), 0, 0)),
             ],
         ),
         out_shape=[
-            jax.ShapeDtypeStruct((depth, width), F32),
-            jax.ShapeDtypeStruct((chips - 1, depth, width), F32),
+            jax.ShapeDtypeStruct((longer, width), F32),
+            jax.ShapeDtypeStruct((chips - 1, longer, width), F32),
         ],
-        compiler_params=pltpu.CompilerParams(vmem_limit_bytes=14 * 1024 * 1024),
+        compiler_params=pltpu.CompilerParams(vmem_limit_bytes=15 * 1024 * 1024),
         cost_estimate=LITTLE,
     )(where, mine, handed)
 
@@ -203,10 +212,13 @@
 
 
 def collect(own, arrived):
-    total = own
+    longer, width = own.shape
+    groups = (longer // SUBLANES, SUBLANES, width)
+    total = own.reshape(groups)
     for payload in arrived:
-        total = total + payload.astype(F32) * (1.0 / SCALE)
-    return total
+        unit = payload[longer - TAIL :].astype(F32)[:SUBLANES]
+        total = total + payload.astype(F32).reshape(groups) * (unit * (1.0 / TOP))[None]
+    return total.reshape(longer, width)
 
 
 def small_kernel(where, keeps, sums, rows, couple, ends, stay_ref, give_ref):
@@ -340,9 +352,9 @@
     total = collect(own, hand_over(payloads, cols))
     parts = small_parts(where, keeps, total, own_rows, couplings, diag_terms, cols)
     own_tile = tile_scatter(*parts, rows, cols)
-    sum_one = total[:, :block_width]
-    sum_two = total[:, block_width : 2 * block_width]
-    sum_three = total[:, 2 * block_width :]
+    sum_one = total[:slab_rows, :block_width]
+    sum_two = total[:slab_rows, block_width : 2 * block_width]
+    sum_three = total[:slab_rows, 2 * block_width :]
     inverse_one = -sum_one
     coupled = couplings.astype(F32)
     inverse_two = -(sum_two - product(sum_one, coupled[0])) * keep_two

time: 181 us -> 184 us (1.017)
  no operation moved by 1% of the time
where the time goes in v5:
time: 184 us
  waiting for transfers between devices  80.1 us (44%)
  starting transfers between devices  48.9 us (27%)
  Pallas kernels  45.7 us (25%)
  other arithmetic  4.32 us (2%)
  matrix products  1.97 us (1%)
    ppermute x6, waiting for transfers between devices, to_chip(): return lax.ppermute(value, 'col', [(c, c ^ 2 * step) for c in range(cols)])  43.3 us
    ppermute x4, starting transfers between devices, spread_step(): return lax.ppermute(own, ('row', 'col'), pairs)  38.9 us
    pallas_call x3, Pallas kernels, multiply(): pl.pallas_call(functools.partial(multiply_kernel, depth=slab_rows, span=s...  36.3 us
    ppermute x4, waiting for transfers between devices, spread_step(): return lax.ppermute(own, ('row', 'col'), pairs)  25.8 us
    ppermute x2, waiting for transfers between devices, tile_scatter(): held = mine + lax.ppermute(theirs, 'row', pairs)  8.76 us
    ppermute x6, starting transfers between devices, to_chip(): return lax.ppermute(value, 'col', [(c, c ^ 2 * step) for c in range(cols)])  8.1 us
    pallas_call x1, Pallas kernels, small_parts(): pl.pallas_call(small_kernel, in_specs=[scalars] * 2 + [whole] * 4, out_sp...  5.01 us
  transfers between devices with their start and end apart: 14, of which 10 were waited for; matrix products, arithmetic and copies ran while one was open for 2% of the time, Pallas kernels for 15%

profile of v5, /device:TPU:0, one launch (start us, length us, event | category | flops | bytes accessed | tf_op | source)
XLA Modules:
  0.0 183.6 jit_solution(7958918027601996166)
XLA Ops:
  0.7 2.1 %shard_map.111.rows = bf16[512,768]{1,0:T(8,128)(2,1)} custom-call(bf16[512,256]{1,0:T(8,128)(2,1)} %refs_0_.1, bf16[512,256]{1,0:T(8,128)(2,1)} %refs_1_.1, bf16[512,256]{1,0:T(8,128)(2,1)} %refs_2_.1), custom_call_target="tpu_custom_call" | custom-call | flops 1 | bytes 1 | tf_op jit(solution)/shard_map/pallas_call | solution.py:71
  2.7 1.8 collective-permute-start
  4.5 7.6 %collective-permute-start.1 = (bf16[512,768]{1,0:T(8,128)(2,1)}, bf16[512,768]{1,0:T(8,128)(2,1)S(1)}, u32[]{:S(2)}, u32[]{:S(2)}) collective-permute-start(bf16[512,768]{1,0:T(8,128)(2,1)} %shard_map.111.rows), channel_id=1, source_target_pairs={{0,8},{1,0},{2,24},{3,16},{4,9},{5,1},{6,25},{7,17},{8,26},{9,18},... | collective-permute-start | bytes 2359304 | tf_op jit(solution)/shard_map/ppermute | solution.py:43
  12.1 13.2 %collective-permute-done.1.refs_1_ = bf16[512,768]{1,0:T(8,128)(2,1)S(1)} collective-permute-done((bf16[512,768]{1,0:T(8,128)(2,1)}, bf16[512,768]{1,0:T(8,128)(2,1)S(1)}, u32[]{:S(2)}, u32[]{:S(2)}) %collective-permute-start.1) | collective-permute-done | bytes 786464 | tf_op jit(solution)/shard_map/ppermute | solution.py:43
  25.3 24.5 %collective-permute-start.2 = (bf16[512,768]{1,0:T(8,128)(2,1)}, bf16[512,768]{1,0:T(8,128)(2,1)S(1)}, u32[]{:S(2)}, u32[]{:S(2)}) collective-permute-start(bf16[512,768]{1,0:T(8,128)(2,1)} %shard_map.111.rows), channel_id=1, source_target_pairs={{0,16},{1,24},{2,0},{3,8},{4,17},{5,25},{6,1},{7,9},{8,2},{9,10},{... | collective-permute-start | bytes 2359304 | tf_op jit(solution)/shard_map/ppermute | solution.py:43
  49.8 5.1 %collective-permute-start.3 = (bf16[512,768]{1,0:T(8,128)(2,1)}, bf16[512,768]{1,0:T(8,128)(2,1)S(1)}, u32[]{:S(2)}, u32[]{:S(2)}) collective-permute-start(bf16[512,768]{1,0:T(8,128)(2,1)} %shard_map.111.rows), channel_id=1, source_target_pairs={{0,24},{1,16},{2,8},{3,0},{4,25},{5,17},{6,9},{7,1},{8,10},{9,2},{... | collective-permute-start | bytes 2359304 | tf_op jit(solution)/shard_map/ppermute | solution.py:43
  55.3 17.0 %shard_map.112.refs_2_ = f32[2,4,512,768]{3,2,1,0:T(8,128)S(1)} custom-call(s32[5]{0:T(128)S(1)} %stack.32.where, s32[3,64]{1,0:T(4,128)S(1)} %add_convert_fusion.keeps, f32[4096,2048]{1,0:T(8,128)} %s_ref.5, bf16[512,768]{1,0:T(8,128)(2,1)S(1)} %collective-permute-done.refs_0_, bf16[512,768]{1,0:T(8,128)(2,1)S(1)} %collective-permute-done.1.refs_1_), custom_call_target="tpu_custom_call" | custom-call | flops 1 | bytes 1 | tf_op jit(solution)/shard_map/pallas_call | solution.py:119
  72.3 12.5 %collective-permute-done.3.refs_1_ = bf16[512,768]{1,0:T(8,128)(2,1)S(1)} collective-permute-done((bf16[512,768]{1,0:T(8,128)(2,1)}, bf16[512,768]{1,0:T(8,128)(2,1)S(1)}, u32[]{:S(2)}, u32[]{:S(2)}) %collective-permute-start.3) | collective-permute-done | bytes 786464 | tf_op jit(solution)/shard_map/ppermute | solution.py:43
  84.9 9.7 %shard_map.113 = f32[1,4,512,768]{3,2,1,0:T(8,128)S(1)} custom-call(s32[5]{0:T(128)S(1)} %stack.32.where, s32[3,64]{1,0:T(4,128)S(1)} %add_convert_fusion.keeps, f32[4096,2048]{1,0:T(8,128)} %s_ref.5, bf16[512,768]{1,0:T(8,128)(2,1)S(1)} %collective-permute-done.2.refs_0_, bf16[512,768]{1,0:T(8,128)(2,1)S(1)} %collective-permute-done.3.refs_1_, ...), custom_call_target="tpu_custom_call" | custom-call | flops 1 | bytes 1 | tf_op jit(solution)/shard_map/pallas_call | solution.py:119
  94.7 9.7 %shard_map.114.mine_ref = f32[1,4,512,768]{3,2,1,0:T(8,128)S(1)} custom-call(s32[5]{0:T(128)S(1)} %stack.32.where, s32[3,64]{1,0:T(4,128)S(1)} %add_convert_fusion.keeps, f32[4096,2048]{1,0:T(8,128)} %s_ref.5, bf16[512,768]{1,0:T(8,128)(2,1)S(1)} %collective-permute-done.2.refs_0_, bf16[512,768]{1,0:T(8,128)(2,1)S(1)} %collective-permute-done.3.refs_1_, ...), custom_call_target="tpu_custom_call" | custom-call | flops 1 | bytes 1 | tf_op jit(solution)/shard_map/pallas_call | solution.py:119
  104.8 2.3 %shard_map.115 = (f32[528,768]{1,0:T(8,128)S(1)}, f32[3,528,768]{2,1,0:T(8,128)S(1)}) custom-call(s32[5]{0:T(128)S(1)} %stack.32.where, f32[1,4,512,768]{3,2,1,0:T(8,128)S(1)} %shard_map.114.mine_ref, f32[1,4,512,768]{3,2,1,0:T(8,128)S(1)} %collective-permute-done.4.handed_ref), custom_call_target="tpu_custom_call" | custom-call | flops 1 | bytes 1 | tf_op jit(solution)/shard_map/pallas_call | solution.py:165
  107.9 3.9 %collective-permute-start.7 = (f16[528,768]{1,0:T(8,128)(2,1)S(1)}, f16[528,768]{1,0:T(8,128)(2,1)S(1)}, u32[]{:S(2)}, u32[]{:S(2)}) collective-permute-start(f16[528,768]{1,0:T(8,128)(2,1)S(1)} %get-tuple-element.17), channel_id=1, source_target_pairs={{0,6},{1,7},{2,4},{3,5},{4,2},{5,3},{6,0},{7,1},{8,14},{9,15},{10,... | collective-permute-start | bytes 2433032 | tf_op jit(solution)/shard_map/ppermute | solution.py:190
  112.5 18.3 %collective-permute-done.7 = f16[528,768]{1,0:T(8,128)(2,1)S(1)} collective-permute-done((f16[528,768]{1,0:T(8,128)(2,1)S(1)}, f16[528,768]{1,0:T(8,128)(2,1)S(1)}, u32[]{:S(2)}, u32[]{:S(2)}) %collective-permute-start.7) | collective-permute-done | bytes 811040 | tf_op jit(solution)/shard_map/ppermute | solution.py:190
  130.7 16.8 %collective-permute-done.6 = f16[528,768]{1,0:T(8,128)(2,1)S(1)} collective-permute-done((f16[528,768]{1,0:T(8,128)(2,1)S(1)}, f16[528,768]{1,0:T(8,128)(2,1)S(1)}, u32[]{:S(2)}, u32[]{:S(2)}) %collective-permute-start.6) | collective-permute-done | bytes 811040 | tf_op jit(solution)/shard_map/ppermute | solution.py:190
  149.1 5.0 %shard_map.116 = (f32[4,6,32,256]{3,2,1,0:T(8,128)S(1)}, f32[4,6,32,256]{3,2,1,0:T(8,128)}) custom-call(s32[5]{0:T(128)S(1)} %stack.32.where, s32[3,64]{1,0:T(4,128)S(1)} %add_convert_fusion.keeps, f32[528,768]{1,0:T(8,128)S(1)} %fusion.sums, bf16[512,768]{1,0:T(8,128)(2,1)S(1)} %copy-done, bf16[3,256,256]{2,1,0:T(8,128)(2,1)S(1)} %copy-done.1, ...), custom_call_target="tpu_custom_call" | custom-call | flops 1 | bytes 1 | tf_op jit(solution)/shard_map/pallas_call | solution.py:289
  154.8 1.9 %collective-permute-done.8 = f32[4,6,32,256]{3,2,1,0:T(8,128)} collective-permute-done((f32[4,6,32,256]{3,2,1,0:T(8,128)}, f32[4,6,32,256]{3,2,1,0:T(8,128)}, u32[]{:S(2)}, u32[]{:S(2)}) %collective-permute-start.8) | collective-permute-done | bytes 786464 | tf_op jit(solution)/shard_map/ppermute | solution.py:186
  156.7 1.3 add.99
  158.1 1.9 %collective-permute-start.11 = (f32[6,32,256]{2,1,0:T(8,128)S(1)}, f32[6,32,256]{2,1,0:T(8,128)S(1)}, u32[]{:S(2)}, u32[]{:S(2)}) collective-permute-start(f32[6,32,256]{2,1,0:T(8,128)S(1)} %get-tuple-element.20), channel_id=1, source_target_pairs={{0,6},{1,7},{2,4},{3,5},{4,2},{5,3},{6,0},{7,1},{8,14},{9,15},{10,... | collective-permute-start | bytes 589832 | tf_op jit(solution)/shard_map/ppermute | solution.py:190
  159.9 1.4 collective-permute-start.10
  162.0 4.8 %collective-permute-done.11 = f32[6,32,256]{2,1,0:T(8,128)S(1)} collective-permute-done((f32[6,32,256]{2,1,0:T(8,128)S(1)}, f32[6,32,256]{2,1,0:T(8,128)S(1)}, u32[]{:S(2)}, u32[]{:S(2)}) %collective-permute-start.11) | collective-permute-done | bytes 196640 | tf_op jit(solution)/shard_map/ppermute | solution.py:190
  166.8 3.4 %collective-permute-done.10 = f32[6,32,256]{2,1,0:T(8,128)S(1)} collective-permute-done((f32[6,32,256]{2,1,0:T(8,128)S(1)}, f32[6,32,256]{2,1,0:T(8,128)S(1)}, u32[]{:S(2)}, u32[]{:S(2)}) %collective-permute-start.10) | collective-permute-done | bytes 196640 | tf_op jit(solution)/shard_map/ppermute | solution.py:190
  170.3 1.6 collective-permute-start.12
  173.1 5.0 %collective-permute-done.12 = f32[6,32,128]{2,1,0:T(8,128)S(1)} collective-permute-done((f32[6,32,128]{2,1,0:T(8,128)S(1)}, f32[6,32,128]{2,1,0:T(8,128)S(1)}, u32[]{:S(2)}, u32[]{:S(2)}) %collective-permute-start.12) | collective-permute-done | bytes 98336 | tf_op jit(solution)/shard_map/ppermute | solution.py:311
  179.1 3.8 %collective-permute-done.13 = f32[6,32,64]{2,1,0:T(8,128)S(1)} collective-permute-done((f32[6,32,64]{2,1,0:T(8,128)S(1)}, f32[6,32,64]{2,1,0:T(8,128)S(1)}, u32[]{:S(2)}, u32[]{:S(2)}) %collective-permute-start.13) | collective-permute-done | bytes 49184 | tf_op jit(solution)/shard_map/ppermute | solution.py:311
  (49 shorter events, 8.2 us)
Async XLA Ops:
  0.6 54.4 %copy-start.4 = (s32[60]{0:T(128)S(1)}, s32[60]{0:T(128)}, u32[]{:S(2)}) copy-start(s32[60]{0:T(128)} %param.14) | copy-start | bytes 724
  0.6 54.5 %copy-start.5 = (s32[56]{0:T(128)S(1)}, s32[56]{0:T(128)}, u32[]{:S(2)}) copy-start(s32[56]{0:T(128)} %param.15) | copy-start | bytes 676
  2.7 9.3 %collective-permute-start = (bf16[512,768]{1,0:T(8,128)(2,1)}, bf16[512,768]{1,0:T(8,128)(2,1)S(1)}, u32[]{:S(2)}, u32[]{:S(2)}) collective-permute-start(bf16[512,768]{1,0:T(8,128)(2,1)} %shard_map.111.rows), channel_id=1, source_target_pairs={{0,0},{1,8},{2,16},{3,24},{4,1},{5,9},{6,17},{7,25},{8,18},{9,26},... | collective-permute-start | bytes 2359304 | tf_op jit(solution)/shard_map/ppermute | solution.py:43
  4.5 20.8 %collective-permute-start.1 = (bf16[512,768]{1,0:T(8,128)(2,1)}, bf16[512,768]{1,0:T(8,128)(2,1)S(1)}, u32[]{:S(2)}, u32[]{:S(2)}) collective-permute-start(bf16[512,768]{1,0:T(8,128)(2,1)} %shard_map.111.rows), channel_id=1, source_target_pairs={{0,8},{1,0},{2,24},{3,16},{4,9},{5,1},{6,25},{7,17},{8,26},{9,18},... | collective-permute-start | bytes 2359304 | tf_op jit(solution)/shard_map/ppermute | solution.py:43
  25.3 47.0 %collective-permute-start.2 = (bf16[512,768]{1,0:T(8,128)(2,1)}, bf16[512,768]{1,0:T(8,128)(2,1)S(1)}, u32[]{:S(2)}, u32[]{:S(2)}) collective-permute-start(bf16[512,768]{1,0:T(8,128)(2,1)} %shard_map.111.rows), channel_id=1, source_target_pairs={{0,16},{1,24},{2,0},{3,8},{4,17},{5,25},{6,1},{7,9},{8,2},{9,10},{... | collective-permute-start | bytes 2359304 | tf_op jit(solution)/shard_map/ppermute | solution.py:43
  49.8 35.0 %collective-permute-start.3 = (bf16[512,768]{1,0:T(8,128)(2,1)}, bf16[512,768]{1,0:T(8,128)(2,1)S(1)}, u32[]{:S(2)}, u32[]{:S(2)}) collective-permute-start(bf16[512,768]{1,0:T(8,128)(2,1)} %shard_map.111.rows), channel_id=1, source_target_pairs={{0,24},{1,16},{2,8},{3,0},{4,25},{5,17},{6,9},{7,1},{8,10},{9,2},{... | collective-permute-start | bytes 2359304 | tf_op jit(solution)/shard_map/ppermute | solution.py:43
  94.5 10.2 %collective-permute-start.4 = (f32[1,4,512,768]{3,2,1,0:T(8,128)S(1)}, f32[1,4,512,768]{3,2,1,0:T(8,128)S(1)}, u32[]{:S(2)}, u32[]{:S(2)}) collective-permute-start(f32[1,4,512,768]{3,2,1,0:T(8,128)S(1)} %shard_map.113), channel_id=1, source_target_pairs={{0,1},{1,0},{2,3},{3,2},{4,5},{5,4},{6,7},{7,6},{8,9},{9,8},{10,11... | collective-permute-start | bytes 18874376 | tf_op jit(solution)/shard_map/ppermute | solution.py:186
  107.9 22.8 %collective-permute-start.7 = (f16[528,768]{1,0:T(8,128)(2,1)S(1)}, f16[528,768]{1,0:T(8,128)(2,1)S(1)}, u32[]{:S(2)}, u32[]{:S(2)}) collective-permute-start(f16[528,768]{1,0:T(8,128)(2,1)S(1)} %get-tuple-element.17), channel_id=1, source_target_pairs={{0,6},{1,7},{2,4},{3,5},{4,2},{5,3},{6,0},{7,1},{8,14},{9,15},{10,... | collective-permute-start | bytes 2433032 | tf_op jit(solution)/shard_map/ppermute | solution.py:190
  111.8 35.7 %collective-permute-start.6 = (f16[528,768]{1,0:T(8,128)(2,1)S(1)}, f16[528,768]{1,0:T(8,128)(2,1)S(1)}, u32[]{:S(2)}, u32[]{:S(2)}) collective-permute-start(f16[528,768]{1,0:T(8,128)(2,1)S(1)} %get-tuple-element.18), channel_id=1, source_target_pairs={{0,4},{1,5},{2,6},{3,7},{4,0},{5,1},{6,2},{7,3},{8,12},{9,13},{10,... | collective-permute-start | bytes 2433032 | tf_op jit(solution)/shard_map/ppermute | solution.py:190
  111.8 35.8 %collective-permute-start.5 = (f16[528,768]{1,0:T(8,128)(2,1)S(1)}, f16[528,768]{1,0:T(8,128)(2,1)S(1)}, u32[]{:S(2)}, u32[]{:S(2)}) collective-permute-start(f16[528,768]{1,0:T(8,128)(2,1)S(1)} %get-tuple-element.16), channel_id=1, source_target_pairs={{0,2},{1,3},{2,0},{3,1},{4,6},{5,7},{6,4},{7,5},{8,10},{9,11},{10,... | collective-permute-start | bytes 2433032 | tf_op jit(solution)/shard_map/ppermute | solution.py:190
  147.6 1.1 copy-start
  147.6 1.2 copy-start.1
  147.6 1.5 copy-start.2
  154.1 2.6 %collective-permute-start.8 = (f32[4,6,32,256]{3,2,1,0:T(8,128)}, f32[4,6,32,256]{3,2,1,0:T(8,128)}, u32[]{:S(2)}, u32[]{:S(2)}) collective-permute-start(f32[4,6,32,256]{3,2,1,0:T(8,128)} %get-tuple-element.15), channel_id=1, source_target_pairs={{0,1},{1,0},{2,3},{3,2},{4,5},{5,4},{6,7},{7,6},{8,9},{9,8},{10,11... | collective-permute-start | bytes 2359304 | tf_op jit(solution)/shard_map/ppermute | solution.py:186
  154.8 6.8 %copy-start.3 = (f32[512,256]{1,0:T(8,128)}, f32[512,256]{1,0:T(8,128)S(1)}, u32[]{:S(2)}) copy-start(f32[512,256]{1,0:T(8,128)S(1)} %fusion.6) | copy-start | bytes 1572868
  158.1 8.8 %collective-permute-start.11 = (f32[6,32,256]{2,1,0:T(8,128)S(1)}, f32[6,32,256]{2,1,0:T(8,128)S(1)}, u32[]{:S(2)}, u32[]{:S(2)}) collective-permute-start(f32[6,32,256]{2,1,0:T(8,128)S(1)} %get-tuple-element.20), channel_id=1, source_target_pairs={{0,6},{1,7},{2,4},{3,5},{4,2},{5,3},{6,0},{7,1},{8,14},{9,15},{10,... | collective-permute-start | bytes 589832 | tf_op jit(solution)/shard_map/ppermute | solution.py:190
  159.9 10.3 %collective-permute-start.10 = (f32[6,32,256]{2,1,0:T(8,128)S(1)}, f32[6,32,256]{2,1,0:T(8,128)S(1)}, u32[]{:S(2)}, u32[]{:S(2)}) collective-permute-start(f32[6,32,256]{2,1,0:T(8,128)S(1)} %get-tuple-element.21), channel_id=1, source_target_pairs={{0,4},{1,5},{2,6},{3,7},{4,0},{5,1},{6,2},{7,3},{8,12},{9,13},{10,... | collective-permute-start | bytes 589832 | tf_op jit(solution)/shard_map/ppermute | solution.py:190
  161.3 8.9 %collective-permute-start.9 = (f32[6,32,256]{2,1,0:T(8,128)S(1)}, f32[6,32,256]{2,1,0:T(8,128)S(1)}, u32[]{:S(2)}, u32[]{:S(2)}) collective-permute-start(f32[6,32,256]{2,1,0:T(8,128)S(1)} %get-tuple-element.19), channel_id=1, source_target_pairs={{0,2},{1,3},{2,0},{3,1},{4,6},{5,7},{6,4},{7,5},{8,10},{9,11},{10,... | collective-permute-start | bytes 589832 | tf_op jit(solution)/shard_map/ppermute | solution.py:190
  170.3 7.8 %collective-permute-start.12 = (f32[6,32,128]{2,1,0:T(8,128)S(1)}, f32[6,32,128]{2,1,0:T(8,128)S(1)}, u32[]{:S(2)}, u32[]{:S(2)}) collective-permute-start(f32[6,32,128]{2,1,0:T(8,128)S(1)} %constant_dynamic-slice_fusion.1), channel_id=1, source_target_pairs={{0,16},{8,24},{16,0},{24,8},{1,17},{9,25},{17,1},{25,9},{2,18},{10... | collective-permute-start | bytes 294920 | tf_op jit(solution)/shard_map/ppermute | solution.py:311
  178.2 4.7 %collective-permute-start.13 = (f32[6,32,64]{2,1,0:T(8,128)S(1)}, f32[6,32,64]{2,1,0:T(8,128)S(1)}, u32[]{:S(2)}, u32[]{:S(2)}) collective-permute-start(f32[6,32,64]{2,1,0:T(8,128)S(1)} %constant_dynamic-slice_fusion), channel_id=1, source_target_pairs={{0,8},{8,0},{16,24},{24,16},{1,9},{9,1},{17,25},{25,17},{2,10},{10... | collective-permute-start | bytes 147464 | tf_op jit(solution)/shard_map/ppermute | solution.py:311

commit v6 on v5

--- a/solution.py
+++ b/solution.py
@@ -10,8 +10,8 @@
 F32 = jnp.float32
 BF16 = jnp.bfloat16
 F16 = jnp.float16
-TOP = 2.0**15
-FLOOR = 2.0**-14
+TOP_POWER = 15.0
+FLOOR = 2.0**-110
 SUBLANES = 8
 TAIL = 16
 LITTLE = pl.CostEstimate(flops=1, bytes_accessed=1, transcendentals=0)
@@ -153,9 +153,9 @@
     @pl.when(step > 0)
     def _():
         most = jnp.max(jnp.abs(summed), axis=(0, 1), keepdims=True)
-        unit = jnp.maximum(most, FLOOR).astype(BF16).astype(F32)
-        sent_ref[0, :depth, :] = summed * (TOP / unit)
-        sent_ref[0, depth:, :] = jnp.broadcast_to(unit, (TAIL, width))
+        power = jnp.ceil(jnp.log2(jnp.maximum(most, FLOOR)))
+        sent_ref[0, :depth, :] = summed * jnp.exp2(TOP_POWER - power)
+        sent_ref[0, depth:, :] = jnp.broadcast_to(power, (TAIL, width))
 
 
 def chip_sum(where, mine, handed):
@@ -216,8 +216,8 @@
     groups = (longer // SUBLANES, SUBLANES, width)
     total = own.reshape(groups)
     for payload in arrived:
-        unit = payload[longer - TAIL :].astype(F32)[:SUBLANES]
-        total = total + payload.astype(F32).reshape(groups) * (unit * (1.0 / TOP))[None]
+        unit = jnp.exp2(payload[longer - TAIL :].astype(F32)[:SUBLANES] - TOP_POWER)
+        total = total + payload.astype(F32).reshape(groups) * unit[None]
     return total.reshape(longer, width)
 
 

time: 184 us -> 184 us (level)
  no operation moved by 1% of the time
where the time goes in v6:
time: 184 us
  waiting for transfers between devices  80.1 us (44%)
  starting transfers between devices  48.9 us (27%)
  Pallas kernels  45.7 us (25%)
  other arithmetic  4.35 us (2%)
  matrix products  1.97 us (1%)
    ppermute x6, waiting for transfers between devices, to_chip(): return lax.ppermute(value, 'col', [(c, c ^ 2 * step) for c in range(cols)])  43.3 us
    ppermute x4, starting transfers between devices, spread_step(): return lax.ppermute(own, ('row', 'col'), pairs)  38.9 us
    pallas_call x3, Pallas kernels, multiply(): pl.pallas_call(functools.partial(multiply_kernel, depth=slab_rows, span=s...  36.3 us
    ppermute x4, waiting for transfers between devices, spread_step(): return lax.ppermute(own, ('row', 'col'), pairs)  25.8 us
    ppermute x2, waiting for transfers between devices, tile_scatter(): held = mine + lax.ppermute(theirs, 'row', pairs)  8.77 us
    ppermute x6, starting transfers between devices, to_chip(): return lax.ppermute(value, 'col', [(c, c ^ 2 * step) for c in range(cols)])  8.1 us
    pallas_call x1, Pallas kernels, small_parts(): pl.pallas_call(small_kernel, in_specs=[scalars] * 2 + [whole] * 4, out_sp...  5.01 us
  transfers between devices with their start and end apart: 14, of which 10 were waited for; matrix products, arithmetic and copies ran while one was open for 2% of the time, Pallas kernels for 15%

profile of v6, /device:TPU:0, one launch (start us, length us, event | category | flops | bytes accessed | tf_op | source)
XLA Modules:
  0.0 183.6 jit_solution(7475632669500547284)
XLA Ops:
  0.7 2.1 %shard_map.111.rows = bf16[512,768]{1,0:T(8,128)(2,1)} custom-call(bf16[512,256]{1,0:T(8,128)(2,1)} %refs_0_.1, bf16[512,256]{1,0:T(8,128)(2,1)} %refs_1_.1, bf16[512,256]{1,0:T(8,128)(2,1)} %refs_2_.1), custom_call_target="tpu_custom_call" | custom-call | flops 1 | bytes 1 | tf_op jit(solution)/shard_map/pallas_call | solution.py:71
  2.7 1.8 collective-permute-start
  4.5 7.6 %collective-permute-start.1 = (bf16[512,768]{1,0:T(8,128)(2,1)}, bf16[512,768]{1,0:T(8,128)(2,1)S(1)}, u32[]{:S(2)}, u32[]{:S(2)}) collective-permute-start(bf16[512,768]{1,0:T(8,128)(2,1)} %shard_map.111.rows), channel_id=1, source_target_pairs={{0,8},{1,0},{2,24},{3,16},{4,9},{5,1},{6,25},{7,17},{8,26},{9,18},... | collective-permute-start | bytes 2359304 | tf_op jit(solution)/shard_map/ppermute | solution.py:43
  12.1 13.2 %collective-permute-done.1.refs_1_ = bf16[512,768]{1,0:T(8,128)(2,1)S(1)} collective-permute-done((bf16[512,768]{1,0:T(8,128)(2,1)}, bf16[512,768]{1,0:T(8,128)(2,1)S(1)}, u32[]{:S(2)}, u32[]{:S(2)}) %collective-permute-start.1) | collective-permute-done | bytes 786464 | tf_op jit(solution)/shard_map/ppermute | solution.py:43
  25.3 24.5 %collective-permute-start.2 = (bf16[512,768]{1,0:T(8,128)(2,1)}, bf16[512,768]{1,0:T(8,128)(2,1)S(1)}, u32[]{:S(2)}, u32[]{:S(2)}) collective-permute-start(bf16[512,768]{1,0:T(8,128)(2,1)} %shard_map.111.rows), channel_id=1, source_target_pairs={{0,16},{1,24},{2,0},{3,8},{4,17},{5,25},{6,1},{7,9},{8,2},{9,10},{... | collective-permute-start | bytes 2359304 | tf_op jit(solution)/shard_map/ppermute | solution.py:43
  49.8 5.1 %collective-permute-start.3 = (bf16[512,768]{1,0:T(8,128)(2,1)}, bf16[512,768]{1,0:T(8,128)(2,1)S(1)}, u32[]{:S(2)}, u32[]{:S(2)}) collective-permute-start(bf16[512,768]{1,0:T(8,128)(2,1)} %shard_map.111.rows), channel_id=1, source_target_pairs={{0,24},{1,16},{2,8},{3,0},{4,25},{5,17},{6,9},{7,1},{8,10},{9,2},{... | collective-permute-start | bytes 2359304 | tf_op jit(solution)/shard_map/ppermute | solution.py:43
  55.3 17.0 %shard_map.112.refs_2_ = f32[2,4,512,768]{3,2,1,0:T(8,128)S(1)} custom-call(s32[5]{0:T(128)S(1)} %stack.32.where, s32[3,64]{1,0:T(4,128)S(1)} %add_convert_fusion.keeps, f32[4096,2048]{1,0:T(8,128)} %s_ref.5, bf16[512,768]{1,0:T(8,128)(2,1)S(1)} %collective-permute-done.refs_0_, bf16[512,768]{1,0:T(8,128)(2,1)S(1)} %collective-permute-done.1.refs_1_), custom_call_target="tpu_custom_call" | custom-call | flops 1 | bytes 1 | tf_op jit(solution)/shard_map/pallas_call | solution.py:119
  72.3 12.5 %collective-permute-done.3.refs_1_ = bf16[512,768]{1,0:T(8,128)(2,1)S(1)} collective-permute-done((bf16[512,768]{1,0:T(8,128)(2,1)}, bf16[512,768]{1,0:T(8,128)(2,1)S(1)}, u32[]{:S(2)}, u32[]{:S(2)}) %collective-permute-start.3) | collective-permute-done | bytes 786464 | tf_op jit(solution)/shard_map/ppermute | solution.py:43
  84.9 9.7 %shard_map.113 = f32[1,4,512,768]{3,2,1,0:T(8,128)S(1)} custom-call(s32[5]{0:T(128)S(1)} %stack.32.where, s32[3,64]{1,0:T(4,128)S(1)} %add_convert_fusion.keeps, f32[4096,2048]{1,0:T(8,128)} %s_ref.5, bf16[512,768]{1,0:T(8,128)(2,1)S(1)} %collective-permute-done.2.refs_0_, bf16[512,768]{1,0:T(8,128)(2,1)S(1)} %collective-permute-done.3.refs_1_, ...), custom_call_target="tpu_custom_call" | custom-call | flops 1 | bytes 1 | tf_op jit(solution)/shard_map/pallas_call | solution.py:119
  94.7 9.7 %shard_map.114.mine_ref = f32[1,4,512,768]{3,2,1,0:T(8,128)S(1)} custom-call(s32[5]{0:T(128)S(1)} %stack.32.where, s32[3,64]{1,0:T(4,128)S(1)} %add_convert_fusion.keeps, f32[4096,2048]{1,0:T(8,128)} %s_ref.5, bf16[512,768]{1,0:T(8,128)(2,1)S(1)} %collective-permute-done.2.refs_0_, bf16[512,768]{1,0:T(8,128)(2,1)S(1)} %collective-permute-done.3.refs_1_, ...), custom_call_target="tpu_custom_call" | custom-call | flops 1 | bytes 1 | tf_op jit(solution)/shard_map/pallas_call | solution.py:119
  104.8 2.3 %shard_map.115 = (f32[528,768]{1,0:T(8,128)S(1)}, f32[3,528,768]{2,1,0:T(8,128)S(1)}) custom-call(s32[5]{0:T(128)S(1)} %stack.32.where, f32[1,4,512,768]{3,2,1,0:T(8,128)S(1)} %shard_map.114.mine_ref, f32[1,4,512,768]{3,2,1,0:T(8,128)S(1)} %collective-permute-done.4.handed_ref), custom_call_target="tpu_custom_call" | custom-call | flops 1 | bytes 1 | tf_op jit(solution)/shard_map/pallas_call | solution.py:165
  107.9 3.9 %collective-permute-start.7 = (f16[528,768]{1,0:T(8,128)(2,1)S(1)}, f16[528,768]{1,0:T(8,128)(2,1)S(1)}, u32[]{:S(2)}, u32[]{:S(2)}) collective-permute-start(f16[528,768]{1,0:T(8,128)(2,1)S(1)} %get-tuple-element.17), channel_id=1, source_target_pairs={{0,6},{1,7},{2,4},{3,5},{4,2},{5,3},{6,0},{7,1},{8,14},{9,15},{10,... | collective-permute-start | bytes 2433032 | tf_op jit(solution)/shard_map/ppermute | solution.py:190
  112.5 18.3 %collective-permute-done.7 = f16[528,768]{1,0:T(8,128)(2,1)S(1)} collective-permute-done((f16[528,768]{1,0:T(8,128)(2,1)S(1)}, f16[528,768]{1,0:T(8,128)(2,1)S(1)}, u32[]{:S(2)}, u32[]{:S(2)}) %collective-permute-start.7) | collective-permute-done | bytes 811040 | tf_op jit(solution)/shard_map/ppermute | solution.py:190
  130.8 16.8 %collective-permute-done.6 = f16[528,768]{1,0:T(8,128)(2,1)S(1)} collective-permute-done((f16[528,768]{1,0:T(8,128)(2,1)S(1)}, f16[528,768]{1,0:T(8,128)(2,1)S(1)}, u32[]{:S(2)}, u32[]{:S(2)}) %collective-permute-start.6) | collective-permute-done | bytes 811040 | tf_op jit(solution)/shard_map/ppermute | solution.py:190
  149.1 5.0 %shard_map.116 = (f32[4,6,32,256]{3,2,1,0:T(8,128)S(1)}, f32[4,6,32,256]{3,2,1,0:T(8,128)}) custom-call(s32[5]{0:T(128)S(1)} %stack.32.where, s32[3,64]{1,0:T(4,128)S(1)} %add_convert_fusion.keeps, f32[528,768]{1,0:T(8,128)S(1)} %fusion.sums, bf16[512,768]{1,0:T(8,128)(2,1)S(1)} %copy-done, bf16[3,256,256]{2,1,0:T(8,128)(2,1)S(1)} %copy-done.1, ...), custom_call_target="tpu_custom_call" | custom-call | flops 1 | bytes 1 | tf_op jit(solution)/shard_map/pallas_call | solution.py:289
  154.8 1.9 %collective-permute-done.8 = f32[4,6,32,256]{3,2,1,0:T(8,128)} collective-permute-done((f32[4,6,32,256]{3,2,1,0:T(8,128)}, f32[4,6,32,256]{3,2,1,0:T(8,128)}, u32[]{:S(2)}, u32[]{:S(2)}) %collective-permute-start.8) | collective-permute-done | bytes 786464 | tf_op jit(solution)/shard_map/ppermute | solution.py:186
  156.8 1.3 add.102
  158.1 1.9 %collective-permute-start.11 = (f32[6,32,256]{2,1,0:T(8,128)S(1)}, f32[6,32,256]{2,1,0:T(8,128)S(1)}, u32[]{:S(2)}, u32[]{:S(2)}) collective-permute-start(f32[6,32,256]{2,1,0:T(8,128)S(1)} %get-tuple-element.20), channel_id=1, source_target_pairs={{0,6},{1,7},{2,4},{3,5},{4,2},{5,3},{6,0},{7,1},{8,14},{9,15},{10,... | collective-permute-start | bytes 589832 | tf_op jit(solution)/shard_map/ppermute | solution.py:190
  160.0 1.4 collective-permute-start.10
  162.1 4.8 %collective-permute-done.11 = f32[6,32,256]{2,1,0:T(8,128)S(1)} collective-permute-done((f32[6,32,256]{2,1,0:T(8,128)S(1)}, f32[6,32,256]{2,1,0:T(8,128)S(1)}, u32[]{:S(2)}, u32[]{:S(2)}) %collective-permute-start.11) | collective-permute-done | bytes 196640 | tf_op jit(solution)/shard_map/ppermute | solution.py:190
  166.9 3.4 %collective-permute-done.10 = f32[6,32,256]{2,1,0:T(8,128)S(1)} collective-permute-done((f32[6,32,256]{2,1,0:T(8,128)S(1)}, f32[6,32,256]{2,1,0:T(8,128)S(1)}, u32[]{:S(2)}, u32[]{:S(2)}) %collective-permute-start.10) | collective-permute-done | bytes 196640 | tf_op jit(solution)/shard_map/ppermute | solution.py:190
  170.3 1.6 collective-permute-start.12
  173.1 5.0 %collective-permute-done.12 = f32[6,32,128]{2,1,0:T(8,128)S(1)} collective-permute-done((f32[6,32,128]{2,1,0:T(8,128)S(1)}, f32[6,32,128]{2,1,0:T(8,128)S(1)}, u32[]{:S(2)}, u32[]{:S(2)}) %collective-permute-start.12) | collective-permute-done | bytes 98336 | tf_op jit(solution)/shard_map/ppermute | solution.py:311
  179.1 3.8 %collective-permute-done.13 = f32[6,32,64]{2,1,0:T(8,128)S(1)} collective-permute-done((f32[6,32,64]{2,1,0:T(8,128)S(1)}, f32[6,32,64]{2,1,0:T(8,128)S(1)}, u32[]{:S(2)}, u32[]{:S(2)}) %collective-permute-start.13) | collective-permute-done | bytes 49184 | tf_op jit(solution)/shard_map/ppermute | solution.py:311
  (49 shorter events, 8.3 us)
Async XLA Ops:
  0.6 54.4 %copy-start.4 = (s32[60]{0:T(128)S(1)}, s32[60]{0:T(128)}, u32[]{:S(2)}) copy-start(s32[60]{0:T(128)} %param.14) | copy-start | bytes 724
  0.6 54.5 %copy-start.5 = (s32[56]{0:T(128)S(1)}, s32[56]{0:T(128)}, u32[]{:S(2)}) copy-start(s32[56]{0:T(128)} %param.15) | copy-start | bytes 676
  2.7 9.3 %collective-permute-start = (bf16[512,768]{1,0:T(8,128)(2,1)}, bf16[512,768]{1,0:T(8,128)(2,1)S(1)}, u32[]{:S(2)}, u32[]{:S(2)}) collective-permute-start(bf16[512,768]{1,0:T(8,128)(2,1)} %shard_map.111.rows), channel_id=1, source_target_pairs={{0,0},{1,8},{2,16},{3,24},{4,1},{5,9},{6,17},{7,25},{8,18},{9,26},... | collective-permute-start | bytes 2359304 | tf_op jit(solution)/shard_map/ppermute | solution.py:43
  4.5 20.8 %collective-permute-start.1 = (bf16[512,768]{1,0:T(8,128)(2,1)}, bf16[512,768]{1,0:T(8,128)(2,1)S(1)}, u32[]{:S(2)}, u32[]{:S(2)}) collective-permute-start(bf16[512,768]{1,0:T(8,128)(2,1)} %shard_map.111.rows), channel_id=1, source_target_pairs={{0,8},{1,0},{2,24},{3,16},{4,9},{5,1},{6,25},{7,17},{8,26},{9,18},... | collective-permute-start | bytes 2359304 | tf_op jit(solution)/shard_map/ppermute | solution.py:43
  25.3 47.0 %collective-permute-start.2 = (bf16[512,768]{1,0:T(8,128)(2,1)}, bf16[512,768]{1,0:T(8,128)(2,1)S(1)}, u32[]{:S(2)}, u32[]{:S(2)}) collective-permute-start(bf16[512,768]{1,0:T(8,128)(2,1)} %shard_map.111.rows), channel_id=1, source_target_pairs={{0,16},{1,24},{2,0},{3,8},{4,17},{5,25},{6,1},{7,9},{8,2},{9,10},{... | collective-permute-start | bytes 2359304 | tf_op jit(solution)/shard_map/ppermute | solution.py:43
  49.8 35.0 %collective-permute-start.3 = (bf16[512,768]{1,0:T(8,128)(2,1)}, bf16[512,768]{1,0:T(8,128)(2,1)S(1)}, u32[]{:S(2)}, u32[]{:S(2)}) collective-permute-start(bf16[512,768]{1,0:T(8,128)(2,1)} %shard_map.111.rows), channel_id=1, source_target_pairs={{0,24},{1,16},{2,8},{3,0},{4,25},{5,17},{6,9},{7,1},{8,10},{9,2},{... | collective-permute-start | bytes 2359304 | tf_op jit(solution)/shard_map/ppermute | solution.py:43
  94.5 10.2 %collective-permute-start.4 = (f32[1,4,512,768]{3,2,1,0:T(8,128)S(1)}, f32[1,4,512,768]{3,2,1,0:T(8,128)S(1)}, u32[]{:S(2)}, u32[]{:S(2)}) collective-permute-start(f32[1,4,512,768]{3,2,1,0:T(8,128)S(1)} %shard_map.113), channel_id=1, source_target_pairs={{0,1},{1,0},{2,3},{3,2},{4,5},{5,4},{6,7},{7,6},{8,9},{9,8},{10,11... | collective-permute-start | bytes 18874376 | tf_op jit(solution)/shard_map/ppermute | solution.py:186
  107.9 22.8 %collective-permute-start.7 = (f16[528,768]{1,0:T(8,128)(2,1)S(1)}, f16[528,768]{1,0:T(8,128)(2,1)S(1)}, u32[]{:S(2)}, u32[]{:S(2)}) collective-permute-start(f16[528,768]{1,0:T(8,128)(2,1)S(1)} %get-tuple-element.17), channel_id=1, source_target_pairs={{0,6},{1,7},{2,4},{3,5},{4,2},{5,3},{6,0},{7,1},{8,14},{9,15},{10,... | collective-permute-start | bytes 2433032 | tf_op jit(solution)/shard_map/ppermute | solution.py:190
  111.8 35.7 %collective-permute-start.6 = (f16[528,768]{1,0:T(8,128)(2,1)S(1)}, f16[528,768]{1,0:T(8,128)(2,1)S(1)}, u32[]{:S(2)}, u32[]{:S(2)}) collective-permute-start(f16[528,768]{1,0:T(8,128)(2,1)S(1)} %get-tuple-element.18), channel_id=1, source_target_pairs={{0,4},{1,5},{2,6},{3,7},{4,0},{5,1},{6,2},{7,3},{8,12},{9,13},{10,... | collective-permute-start | bytes 2433032 | tf_op jit(solution)/shard_map/ppermute | solution.py:190
  111.8 35.8 %collective-permute-start.5 = (f16[528,768]{1,0:T(8,128)(2,1)S(1)}, f16[528,768]{1,0:T(8,128)(2,1)S(1)}, u32[]{:S(2)}, u32[]{:S(2)}) collective-permute-start(f16[528,768]{1,0:T(8,128)(2,1)S(1)} %get-tuple-element.16), channel_id=1, source_target_pairs={{0,2},{1,3},{2,0},{3,1},{4,6},{5,7},{6,4},{7,5},{8,10},{9,11},{10,... | collective-permute-start | bytes 2433032 | tf_op jit(solution)/shard_map/ppermute | solution.py:190
  147.6 1.1 copy-start
  147.7 1.2 copy-start.1
  147.7 1.5 copy-start.2
  154.2 2.6 %collective-permute-start.8 = (f32[4,6,32,256]{3,2,1,0:T(8,128)}, f32[4,6,32,256]{3,2,1,0:T(8,128)}, u32[]{:S(2)}, u32[]{:S(2)}) collective-permute-start(f32[4,6,32,256]{3,2,1,0:T(8,128)} %get-tuple-element.15), channel_id=1, source_target_pairs={{0,1},{1,0},{2,3},{3,2},{4,5},{5,4},{6,7},{7,6},{8,9},{9,8},{10,11... | collective-permute-start | bytes 2359304 | tf_op jit(solution)/shard_map/ppermute | solution.py:186
  154.8 6.8 %copy-start.3 = (f32[512,256]{1,0:T(8,128)}, f32[512,256]{1,0:T(8,128)S(1)}, u32[]{:S(2)}) copy-start(f32[512,256]{1,0:T(8,128)S(1)} %fusion.6) | copy-start | bytes 1572868
  158.1 8.8 %collective-permute-start.11 = (f32[6,32,256]{2,1,0:T(8,128)S(1)}, f32[6,32,256]{2,1,0:T(8,128)S(1)}, u32[]{:S(2)}, u32[]{:S(2)}) collective-permute-start(f32[6,32,256]{2,1,0:T(8,128)S(1)} %get-tuple-element.20), channel_id=1, source_target_pairs={{0,6},{1,7},{2,4},{3,5},{4,2},{5,3},{6,0},{7,1},{8,14},{9,15},{10,... | collective-permute-start | bytes 589832 | tf_op jit(solution)/shard_map/ppermute | solution.py:190
  160.0 10.3 %collective-permute-start.10 = (f32[6,32,256]{2,1,0:T(8,128)S(1)}, f32[6,32,256]{2,1,0:T(8,128)S(1)}, u32[]{:S(2)}, u32[]{:S(2)}) collective-permute-start(f32[6,32,256]{2,1,0:T(8,128)S(1)} %get-tuple-element.21), channel_id=1, source_target_pairs={{0,4},{1,5},{2,6},{3,7},{4,0},{5,1},{6,2},{7,3},{8,12},{9,13},{10,... | collective-permute-start | bytes 589832 | tf_op jit(solution)/shard_map/ppermute | solution.py:190
  161.4 8.9 %collective-permute-start.9 = (f32[6,32,256]{2,1,0:T(8,128)S(1)}, f32[6,32,256]{2,1,0:T(8,128)S(1)}, u32[]{:S(2)}, u32[]{:S(2)}) collective-permute-start(f32[6,32,256]{2,1,0:T(8,128)S(1)} %get-tuple-element.19), channel_id=1, source_target_pairs={{0,2},{1,3},{2,0},{3,1},{4,6},{5,7},{6,4},{7,5},{8,10},{9,11},{10,... | collective-permute-start | bytes 589832 | tf_op jit(solution)/shard_map/ppermute | solution.py:190
  170.3 7.8 %collective-permute-start.12 = (f32[6,32,128]{2,1,0:T(8,128)S(1)}, f32[6,32,128]{2,1,0:T(8,128)S(1)}, u32[]{:S(2)}, u32[]{:S(2)}) collective-permute-start(f32[6,32,128]{2,1,0:T(8,128)S(1)} %constant_dynamic-slice_fusion.1), channel_id=1, source_target_pairs={{0,16},{8,24},{16,0},{24,8},{1,17},{9,25},{17,1},{25,9},{2,18},{10... | collective-permute-start | bytes 294920 | tf_op jit(solution)/shard_map/ppermute | solution.py:311
  178.2 4.7 %collective-permute-start.13 = (f32[6,32,64]{2,1,0:T(8,128)S(1)}, f32[6,32,64]{2,1,0:T(8,128)S(1)}, u32[]{:S(2)}, u32[]{:S(2)}) collective-permute-start(f32[6,32,64]{2,1,0:T(8,128)S(1)} %constant_dynamic-slice_fusion), channel_id=1, source_target_pairs={{0,8},{8,0},{16,24},{24,16},{1,9},{9,1},{17,25},{25,17},{2,10},{10... | collective-permute-start | bytes 147464 | tf_op jit(solution)/shard_map/ppermute | solution.py:311

commit v7 on v6

--- a/solution.py
+++ b/solution.py
@@ -301,16 +301,16 @@
     held = stay + sibling(give, cols)
     arrived = [to_chip(take(held, chip ^ step), step, cols) for step in range(1, cols // 2)]
     held = functools.reduce(jnp.add, arrived, take(held, chip))
-    bit = rows // 2
-    while bit:
-        size = held.shape[2] // 2
-        side = row // bit % 2
-        mine = lax.dynamic_slice_in_dim(held, side * size, size, 2)
-        theirs = lax.dynamic_slice_in_dim(held, (1 - side) * size, size, 2)
-        pairs = [(r, r ^ bit) for r in range(rows)]
-        held = mine + lax.ppermute(theirs, "row", pairs)
-        bit //= 2
-    return jnp.swapaxes(held, 1, 2)
+    size = held.shape[2] // rows
+
+    def rows_of(plane):
+        return lax.dynamic_slice_in_dim(held, plane * size, size, 2)
+
+    total = rows_of(row)
+    for step in range(1, rows):
+        pairs = [(r, r ^ step) for r in range(rows)]
+        total = total + lax.ppermute(rows_of(row ^ step), "row", pairs)
+    return jnp.swapaxes(total, 1, 2)
 
 
 def body(

time: 184 us -> 184 us (level)
  waiting for transfers between devices: 80.1 us -> 77 us
  starting transfers between devices: 48.9 us -> 51.7 us
    ppermute x2 -> x3, starting transfers between devices: 1.66 us -> 4.45 us  [tile_scatter(): total = total + lax.ppermute(rows_of(row ^ step), 'row', pairs)]
    ppermute x2 -> x3, waiting for transfers between devices: 8.77 us -> 6.9 us  [tile_scatter(): total = total + lax.ppermute(rows_of(row ^ step), 'row', pairs)]
  transfers between devices with their start and end apart: 14 -> 15, of which waited for: 10 -> 10; matrix products, arithmetic and copies ran while one was open for 2% -> 2% of each run, Pallas kernels for 15% -> 15%
where the time goes in v7:
time: 184 us; the launch traced here: 183 us
  waiting for transfers between devices  77 us (42%)
  starting transfers between devices  51.7 us (28%)
  Pallas kernels  45.8 us (25%)
  other arithmetic  4.33 us (2%)
  matrix products  1.95 us (1%)
    ppermute x6, waiting for transfers between devices, to_chip(): return lax.ppermute(value, 'col', [(c, c ^ 2 * step) for c in range(cols)])  42.5 us
    ppermute x4, starting transfers between devices, spread_step(): return lax.ppermute(own, ('row', 'col'), pairs)  38.9 us
    pallas_call x3, Pallas kernels, multiply(): pl.pallas_call(functools.partial(multiply_kernel, depth=slab_rows, span=s...  36.3 us
    ppermute x4, waiting for transfers between devices, spread_step(): return lax.ppermute(own, ('row', 'col'), pairs)  25.8 us
    ppermute x6, starting transfers between devices, to_chip(): return lax.ppermute(value, 'col', [(c, c ^ 2 * step) for c in range(cols)])  8.1 us
    ppermute x3, waiting for transfers between devices, tile_scatter(): total = total + lax.ppermute(rows_of(row ^ step), 'row', pairs)  6.9 us
    pallas_call x1, Pallas kernels, small_parts(): pl.pallas_call(small_kernel, in_specs=[scalars] * 2 + [whole] * 4, out_sp...  5.04 us
    ppermute x3, starting transfers between devices, tile_scatter(): total = total + lax.ppermute(rows_of(row ^ step), 'row', pairs)  4.45 us
  transfers between devices with their start and end apart: 15, of which 10 were waited for; matrix products, arithmetic and copies ran while one was open for 2% of the time, Pallas kernels for 15%

profile of v7, /device:TPU:0, one launch (start us, length us, event | category | flops | bytes accessed | tf_op | source)
XLA Modules:
  0.0 183.4 jit_solution(6976849797232403314)
XLA Ops:
  0.7 2.1 %shard_map.111.rows = bf16[512,768]{1,0:T(8,128)(2,1)} custom-call(bf16[512,256]{1,0:T(8,128)(2,1)} %refs_0_.1, bf16[512,256]{1,0:T(8,128)(2,1)} %refs_1_.1, bf16[512,256]{1,0:T(8,128)(2,1)} %refs_2_.1), custom_call_target="tpu_custom_call" | custom-call | flops 1 | bytes 1 | tf_op jit(solution)/shard_map/pallas_call | solution.py:71
  2.7 1.8 collective-permute-start
  4.5 7.6 %collective-permute-start.1 = (bf16[512,768]{1,0:T(8,128)(2,1)}, bf16[512,768]{1,0:T(8,128)(2,1)S(1)}, u32[]{:S(2)}, u32[]{:S(2)}) collective-permute-start(bf16[512,768]{1,0:T(8,128)(2,1)} %shard_map.111.rows), channel_id=1, source_target_pairs={{0,8},{1,0},{2,24},{3,16},{4,9},{5,1},{6,25},{7,17},{8,26},{9,18},... | collective-permute-start | bytes 2359304 | tf_op jit(solution)/shard_map/ppermute | solution.py:43
  12.1 13.2 %collective-permute-done.1.refs_1_ = bf16[512,768]{1,0:T(8,128)(2,1)S(1)} collective-permute-done((bf16[512,768]{1,0:T(8,128)(2,1)}, bf16[512,768]{1,0:T(8,128)(2,1)S(1)}, u32[]{:S(2)}, u32[]{:S(2)}) %collective-permute-start.1) | collective-permute-done | bytes 786464 | tf_op jit(solution)/shard_map/ppermute | solution.py:43
  25.3 24.5 %collective-permute-start.2 = (bf16[512,768]{1,0:T(8,128)(2,1)}, bf16[512,768]{1,0:T(8,128)(2,1)S(1)}, u32[]{:S(2)}, u32[]{:S(2)}) collective-permute-start(bf16[512,768]{1,0:T(8,128)(2,1)} %shard_map.111.rows), channel_id=1, source_target_pairs={{0,16},{1,24},{2,0},{3,8},{4,17},{5,25},{6,1},{7,9},{8,2},{9,10},{... | collective-permute-start | bytes 2359304 | tf_op jit(solution)/shard_map/ppermute | solution.py:43
  49.8 5.1 %collective-permute-start.3 = (bf16[512,768]{1,0:T(8,128)(2,1)}, bf16[512,768]{1,0:T(8,128)(2,1)S(1)}, u32[]{:S(2)}, u32[]{:S(2)}) collective-permute-start(bf16[512,768]{1,0:T(8,128)(2,1)} %shard_map.111.rows), channel_id=1, source_target_pairs={{0,24},{1,16},{2,8},{3,0},{4,25},{5,17},{6,9},{7,1},{8,10},{9,2},{... | collective-permute-start | bytes 2359304 | tf_op jit(solution)/shard_map/ppermute | solution.py:43
  55.4 17.0 %shard_map.112.refs_2_ = f32[2,4,512,768]{3,2,1,0:T(8,128)S(1)} custom-call(s32[5]{0:T(128)S(1)} %stack.32.where, s32[3,64]{1,0:T(4,128)S(1)} %add_convert_fusion.keeps, f32[4096,2048]{1,0:T(8,128)} %s_ref.5, bf16[512,768]{1,0:T(8,128)(2,1)S(1)} %collective-permute-done.refs_0_, bf16[512,768]{1,0:T(8,128)(2,1)S(1)} %collective-permute-done.1.refs_1_), custom_call_target="tpu_custom_call" | custom-call | flops 1 | bytes 1 | tf_op jit(solution)/shard_map/pallas_call | solution.py:119
  72.3 12.5 %collective-permute-done.3.refs_1_ = bf16[512,768]{1,0:T(8,128)(2,1)S(1)} collective-permute-done((bf16[512,768]{1,0:T(8,128)(2,1)}, bf16[512,768]{1,0:T(8,128)(2,1)S(1)}, u32[]{:S(2)}, u32[]{:S(2)}) %collective-permute-start.3) | collective-permute-done | bytes 786464 | tf_op jit(solution)/shard_map/ppermute | solution.py:43
  84.9 9.7 %shard_map.113 = f32[1,4,512,768]{3,2,1,0:T(8,128)S(1)} custom-call(s32[5]{0:T(128)S(1)} %stack.32.where, s32[3,64]{1,0:T(4,128)S(1)} %add_convert_fusion.keeps, f32[4096,2048]{1,0:T(8,128)} %s_ref.5, bf16[512,768]{1,0:T(8,128)(2,1)S(1)} %collective-permute-done.2.refs_0_, bf16[512,768]{1,0:T(8,128)(2,1)S(1)} %collective-permute-done.3.refs_1_, ...), custom_call_target="tpu_custom_call" | custom-call | flops 1 | bytes 1 | tf_op jit(solution)/shard_map/pallas_call | solution.py:119
  94.7 9.7 %shard_map.114.mine_ref = f32[1,4,512,768]{3,2,1,0:T(8,128)S(1)} custom-call(s32[5]{0:T(128)S(1)} %stack.32.where, s32[3,64]{1,0:T(4,128)S(1)} %add_convert_fusion.keeps, f32[4096,2048]{1,0:T(8,128)} %s_ref.5, bf16[512,768]{1,0:T(8,128)(2,1)S(1)} %collective-permute-done.2.refs_0_, bf16[512,768]{1,0:T(8,128)(2,1)S(1)} %collective-permute-done.3.refs_1_, ...), custom_call_target="tpu_custom_call" | custom-call | flops 1 | bytes 1 | tf_op jit(solution)/shard_map/pallas_call | solution.py:119
  104.8 2.3 %shard_map.115 = (f32[528,768]{1,0:T(8,128)S(1)}, f32[3,528,768]{2,1,0:T(8,128)S(1)}) custom-call(s32[5]{0:T(128)S(1)} %stack.32.where, f32[1,4,512,768]{3,2,1,0:T(8,128)S(1)} %shard_map.114.mine_ref, f32[1,4,512,768]{3,2,1,0:T(8,128)S(1)} %collective-permute-done.4.handed_ref), custom_call_target="tpu_custom_call" | custom-call | flops 1 | bytes 1 | tf_op jit(solution)/shard_map/pallas_call | solution.py:165
  108.0 3.9 %collective-permute-start.7 = (f16[528,768]{1,0:T(8,128)(2,1)S(1)}, f16[528,768]{1,0:T(8,128)(2,1)S(1)}, u32[]{:S(2)}, u32[]{:S(2)}) collective-permute-start(f16[528,768]{1,0:T(8,128)(2,1)S(1)} %get-tuple-element.17), channel_id=1, source_target_pairs={{0,6},{1,7},{2,4},{3,5},{4,2},{5,3},{6,0},{7,1},{8,14},{9,15},{10,... | collective-permute-start | bytes 2433032 | tf_op jit(solution)/shard_map/ppermute | solution.py:190
  112.5 18.3 %collective-permute-done.7 = f16[528,768]{1,0:T(8,128)(2,1)S(1)} collective-permute-done((f16[528,768]{1,0:T(8,128)(2,1)S(1)}, f16[528,768]{1,0:T(8,128)(2,1)S(1)}, u32[]{:S(2)}, u32[]{:S(2)}) %collective-permute-start.7) | collective-permute-done | bytes 811040 | tf_op jit(solution)/shard_map/ppermute | solution.py:190
  130.8 16.8 %collective-permute-done.6 = f16[528,768]{1,0:T(8,128)(2,1)S(1)} collective-permute-done((f16[528,768]{1,0:T(8,128)(2,1)S(1)}, f16[528,768]{1,0:T(8,128)(2,1)S(1)}, u32[]{:S(2)}, u32[]{:S(2)}) %collective-permute-start.6) | collective-permute-done | bytes 811040 | tf_op jit(solution)/shard_map/ppermute | solution.py:190
  149.2 5.0 %shard_map.116 = (f32[4,6,32,256]{3,2,1,0:T(8,128)S(1)}, f32[4,6,32,256]{3,2,1,0:T(8,128)}) custom-call(s32[5]{0:T(128)S(1)} %stack.32.where, s32[3,64]{1,0:T(4,128)S(1)} %add_convert_fusion.keeps, f32[528,768]{1,0:T(8,128)S(1)} %fusion.sums, bf16[512,768]{1,0:T(8,128)(2,1)S(1)} %copy-done, bf16[3,256,256]{2,1,0:T(8,128)(2,1)S(1)} %copy-done.1, ...), custom_call_target="tpu_custom_call" | custom-call | flops 1 | bytes 1 | tf_op jit(solution)/shard_map/pallas_call | solution.py:289
  155.3 1.5 collective-permute-done.8
  158.2 1.9 %collective-permute-start.11 = (f32[6,32,256]{2,1,0:T(8,128)S(1)}, f32[6,32,256]{2,1,0:T(8,128)S(1)}, u32[]{:S(2)}, u32[]{:S(2)}) collective-permute-start(f32[6,32,256]{2,1,0:T(8,128)S(1)} %get-tuple-element.20), channel_id=1, source_target_pairs={{0,6},{1,7},{2,4},{3,5},{4,2},{5,3},{6,0},{7,1},{8,14},{9,15},{10,... | collective-permute-start | bytes 589832 | tf_op jit(solution)/shard_map/ppermute | solution.py:190
  160.0 1.4 collective-permute-start.10
  162.9 4.0 %collective-permute-done.11 = f32[6,32,256]{2,1,0:T(8,128)S(1)} collective-permute-done((f32[6,32,256]{2,1,0:T(8,128)S(1)}, f32[6,32,256]{2,1,0:T(8,128)S(1)}, u32[]{:S(2)}, u32[]{:S(2)}) %collective-permute-start.11) | collective-permute-done | bytes 196640 | tf_op jit(solution)/shard_map/ppermute | solution.py:190
  166.9 3.4 %collective-permute-done.10 = f32[6,32,256]{2,1,0:T(8,128)S(1)} collective-permute-done((f32[6,32,256]{2,1,0:T(8,128)S(1)}, f32[6,32,256]{2,1,0:T(8,128)S(1)}, u32[]{:S(2)}, u32[]{:S(2)}) %collective-permute-start.10) | collective-permute-done | bytes 196640 | tf_op jit(solution)/shard_map/ppermute | solution.py:190
  170.5 2.5 %collective-permute-start.14 = (f32[6,32,64]{2,1,0:T(8,128)S(1)}, f32[6,32,64]{2,1,0:T(8,128)S(1)}, u32[]{:S(2)}, u32[]{:S(2)}) collective-permute-start(f32[6,32,64]{2,1,0:T(8,128)S(1)} %get-tuple-element.23), channel_id=1, source_target_pairs={{0,24},{8,16},{16,8},{24,0},{1,25},{9,17},{17,9},{25,1},{2,26},{10... | collective-permute-start | bytes 147464 | tf_op jit(solution)/shard_map/ppermute | solution.py:312
  173.7 1.3 collective-permute-start.12
  175.8 2.3 %collective-permute-done.14 = f32[6,32,64]{2,1,0:T(8,128)S(1)} collective-permute-done((f32[6,32,64]{2,1,0:T(8,128)S(1)}, f32[6,32,64]{2,1,0:T(8,128)S(1)}, u32[]{:S(2)}, u32[]{:S(2)}) %collective-permute-start.14) | collective-permute-done | bytes 49184 | tf_op jit(solution)/shard_map/ppermute | solution.py:312
  178.1 4.6 %collective-permute-done.13 = f32[6,32,64]{2,1,0:T(8,128)S(1)} collective-permute-done((f32[6,32,64]{2,1,0:T(8,128)S(1)}, f32[6,32,64]{2,1,0:T(8,128)S(1)}, u32[]{:S(2)}, u32[]{:S(2)}) %collective-permute-start.13) | collective-permute-done | bytes 49184 | tf_op jit(solution)/shard_map/ppermute | solution.py:312
  (49 shorter events, 10.1 us)
Async XLA Ops:
  0.6 54.4 %copy-start.4 = (s32[60]{0:T(128)S(1)}, s32[60]{0:T(128)}, u32[]{:S(2)}) copy-start(s32[60]{0:T(128)} %param.14) | copy-start | bytes 724
  0.6 54.5 %copy-start.5 = (s32[56]{0:T(128)S(1)}, s32[56]{0:T(128)}, u32[]{:S(2)}) copy-start(s32[56]{0:T(128)} %param.15) | copy-start | bytes 676
  2.7 9.3 %collective-permute-start = (bf16[512,768]{1,0:T(8,128)(2,1)}, bf16[512,768]{1,0:T(8,128)(2,1)S(1)}, u32[]{:S(2)}, u32[]{:S(2)}) collective-permute-start(bf16[512,768]{1,0:T(8,128)(2,1)} %shard_map.111.rows), channel_id=1, source_target_pairs={{0,0},{1,8},{2,16},{3,24},{4,1},{5,9},{6,17},{7,25},{8,18},{9,26},... | collective-permute-start | bytes 2359304 | tf_op jit(solution)/shard_map/ppermute | solution.py:43
  4.5 20.8 %collective-permute-start.1 = (bf16[512,768]{1,0:T(8,128)(2,1)}, bf16[512,768]{1,0:T(8,128)(2,1)S(1)}, u32[]{:S(2)}, u32[]{:S(2)}) collective-permute-start(bf16[512,768]{1,0:T(8,128)(2,1)} %shard_map.111.rows), channel_id=1, source_target_pairs={{0,8},{1,0},{2,24},{3,16},{4,9},{5,1},{6,25},{7,17},{8,26},{9,18},... | collective-permute-start | bytes 2359304 | tf_op jit(solution)/shard_map/ppermute | solution.py:43
  25.3 47.0 %collective-permute-start.2 = (bf16[512,768]{1,0:T(8,128)(2,1)}, bf16[512,768]{1,0:T(8,128)(2,1)S(1)}, u32[]{:S(2)}, u32[]{:S(2)}) collective-permute-start(bf16[512,768]{1,0:T(8,128)(2,1)} %shard_map.111.rows), channel_id=1, source_target_pairs={{0,16},{1,24},{2,0},{3,8},{4,17},{5,25},{6,1},{7,9},{8,2},{9,10},{... | collective-permute-start | bytes 2359304 | tf_op jit(solution)/shard_map/ppermute | solution.py:43
  49.8 35.0 %collective-permute-start.3 = (bf16[512,768]{1,0:T(8,128)(2,1)}, bf16[512,768]{1,0:T(8,128)(2,1)S(1)}, u32[]{:S(2)}, u32[]{:S(2)}) collective-permute-start(bf16[512,768]{1,0:T(8,128)(2,1)} %shard_map.111.rows), channel_id=1, source_target_pairs={{0,24},{1,16},{2,8},{3,0},{4,25},{5,17},{6,9},{7,1},{8,10},{9,2},{... | collective-permute-start | bytes 2359304 | tf_op jit(solution)/shard_map/ppermute | solution.py:43
  94.6 10.2 %collective-permute-start.4 = (f32[1,4,512,768]{3,2,1,0:T(8,128)S(1)}, f32[1,4,512,768]{3,2,1,0:T(8,128)S(1)}, u32[]{:S(2)}, u32[]{:S(2)}) collective-permute-start(f32[1,4,512,768]{3,2,1,0:T(8,128)S(1)} %shard_map.113), channel_id=1, source_target_pairs={{0,1},{1,0},{2,3},{3,2},{4,5},{5,4},{6,7},{7,6},{8,9},{9,8},{10,11... | collective-permute-start | bytes 18874376 | tf_op jit(solution)/shard_map/ppermute | solution.py:186
  108.0 22.8 %collective-permute-start.7 = (f16[528,768]{1,0:T(8,128)(2,1)S(1)}, f16[528,768]{1,0:T(8,128)(2,1)S(1)}, u32[]{:S(2)}, u32[]{:S(2)}) collective-permute-start(f16[528,768]{1,0:T(8,128)(2,1)S(1)} %get-tuple-element.17), channel_id=1, source_target_pairs={{0,6},{1,7},{2,4},{3,5},{4,2},{5,3},{6,0},{7,1},{8,14},{9,15},{10,... | collective-permute-start | bytes 2433032 | tf_op jit(solution)/shard_map/ppermute | solution.py:190
  111.9 35.7 %collective-permute-start.6 = (f16[528,768]{1,0:T(8,128)(2,1)S(1)}, f16[528,768]{1,0:T(8,128)(2,1)S(1)}, u32[]{:S(2)}, u32[]{:S(2)}) collective-permute-start(f16[528,768]{1,0:T(8,128)(2,1)S(1)} %get-tuple-element.18), channel_id=1, source_target_pairs={{0,4},{1,5},{2,6},{3,7},{4,0},{5,1},{6,2},{7,3},{8,12},{9,13},{10,... | collective-permute-start | bytes 2433032 | tf_op jit(solution)/shard_map/ppermute | solution.py:190
  111.9 35.8 %collective-permute-start.5 = (f16[528,768]{1,0:T(8,128)(2,1)S(1)}, f16[528,768]{1,0:T(8,128)(2,1)S(1)}, u32[]{:S(2)}, u32[]{:S(2)}) collective-permute-start(f16[528,768]{1,0:T(8,128)(2,1)S(1)} %get-tuple-element.16), channel_id=1, source_target_pairs={{0,2},{1,3},{2,0},{3,1},{4,6},{5,7},{6,4},{7,5},{8,10},{9,11},{10,... | collective-permute-start | bytes 2433032 | tf_op jit(solution)/shard_map/ppermute | solution.py:190
  147.7 1.1 copy-start
  147.7 1.2 copy-start.1
  147.7 1.5 copy-start.2
  154.2 2.6 %collective-permute-start.8 = (f32[4,6,32,256]{3,2,1,0:T(8,128)}, f32[4,6,32,256]{3,2,1,0:T(8,128)}, u32[]{:S(2)}, u32[]{:S(2)}) collective-permute-start(f32[4,6,32,256]{3,2,1,0:T(8,128)} %get-tuple-element.15), channel_id=1, source_target_pairs={{0,1},{1,0},{2,3},{3,2},{4,5},{5,4},{6,7},{7,6},{8,9},{9,8},{10,11... | collective-permute-start | bytes 2359304 | tf_op jit(solution)/shard_map/ppermute | solution.py:186
  154.9 3.2 %copy-start.3 = (f32[512,256]{1,0:T(8,128)}, f32[512,256]{1,0:T(8,128)S(1)}, u32[]{:S(2)}) copy-start(f32[512,256]{1,0:T(8,128)S(1)} %fusion.6) | copy-start | bytes 1572868
  158.2 8.8 %collective-permute-start.11 = (f32[6,32,256]{2,1,0:T(8,128)S(1)}, f32[6,32,256]{2,1,0:T(8,128)S(1)}, u32[]{:S(2)}, u32[]{:S(2)}) collective-permute-start(f32[6,32,256]{2,1,0:T(8,128)S(1)} %get-tuple-element.20), channel_id=1, source_target_pairs={{0,6},{1,7},{2,4},{3,5},{4,2},{5,3},{6,0},{7,1},{8,14},{9,15},{10,... | collective-permute-start | bytes 589832 | tf_op jit(solution)/shard_map/ppermute | solution.py:190
  160.0 10.3 %collective-permute-start.10 = (f32[6,32,256]{2,1,0:T(8,128)S(1)}, f32[6,32,256]{2,1,0:T(8,128)S(1)}, u32[]{:S(2)}, u32[]{:S(2)}) collective-permute-start(f32[6,32,256]{2,1,0:T(8,128)S(1)} %get-tuple-element.21), channel_id=1, source_target_pairs={{0,4},{1,5},{2,6},{3,7},{4,0},{5,1},{6,2},{7,3},{8,12},{9,13},{10,... | collective-permute-start | bytes 589832 | tf_op jit(solution)/shard_map/ppermute | solution.py:190
  161.4 8.9 %collective-permute-start.9 = (f32[6,32,256]{2,1,0:T(8,128)S(1)}, f32[6,32,256]{2,1,0:T(8,128)S(1)}, u32[]{:S(2)}, u32[]{:S(2)}) collective-permute-start(f32[6,32,256]{2,1,0:T(8,128)S(1)} %get-tuple-element.19), channel_id=1, source_target_pairs={{0,2},{1,3},{2,0},{3,1},{4,6},{5,7},{6,4},{7,5},{8,10},{9,11},{10,... | collective-permute-start | bytes 589832 | tf_op jit(solution)/shard_map/ppermute | solution.py:190
  170.5 7.6 %collective-permute-start.14 = (f32[6,32,64]{2,1,0:T(8,128)S(1)}, f32[6,32,64]{2,1,0:T(8,128)S(1)}, u32[]{:S(2)}, u32[]{:S(2)}) collective-permute-start(f32[6,32,64]{2,1,0:T(8,128)S(1)} %get-tuple-element.23), channel_id=1, source_target_pairs={{0,24},{8,16},{16,8},{24,0},{1,25},{9,17},{17,9},{25,1},{2,26},{10... | collective-permute-start | bytes 147464 | tf_op jit(solution)/shard_map/ppermute | solution.py:312
  173.1 9.6 %collective-permute-start.13 = (f32[6,32,64]{2,1,0:T(8,128)S(1)}, f32[6,32,64]{2,1,0:T(8,128)S(1)}, u32[]{:S(2)}, u32[]{:S(2)}) collective-permute-start(f32[6,32,64]{2,1,0:T(8,128)S(1)} %get-tuple-element.24), channel_id=1, source_target_pairs={{0,16},{8,24},{16,0},{24,8},{1,17},{9,25},{17,1},{25,9},{2,18},{10... | collective-permute-start | bytes 147464 | tf_op jit(solution)/shard_map/ppermute | solution.py:312
  173.7 9.0 %collective-permute-start.12 = (f32[6,32,64]{2,1,0:T(8,128)S(1)}, f32[6,32,64]{2,1,0:T(8,128)S(1)}, u32[]{:S(2)}, u32[]{:S(2)}) collective-permute-start(f32[6,32,64]{2,1,0:T(8,128)S(1)} %get-tuple-element.22), channel_id=1, source_target_pairs={{0,8},{8,0},{16,24},{24,16},{1,9},{9,1},{17,25},{25,17},{2,10},{10... | collective-permute-start | bytes 147464 | tf_op jit(solution)/shard_map/ppermute | solution.py:312

commit v8 on v6

--- a/solution.py
+++ b/solution.py
@@ -298,9 +298,10 @@
 
 def tile_scatter(stay, give, rows, cols):
     row, chip = lax.axis_index("row"), lax.axis_index("col") // 2
-    held = stay + sibling(give, cols)
-    arrived = [to_chip(take(held, chip ^ step), step, cols) for step in range(1, cols // 2)]
-    held = functools.reduce(jnp.add, arrived, take(held, chip))
+    handed = sibling(give, cols)
+    sums = [take(stay, chip ^ step) + take(handed, chip ^ step) for step in range(cols // 2)]
+    arrived = [to_chip(part, step, cols) for step, part in enumerate(sums) if step]
+    held = functools.reduce(jnp.add, arrived, sums[0])
     bit = rows // 2
     while bit:
         size = held.shape[2] // 2

time: 184 us -> 185 us (level)
  transfers between devices with their start and end apart: 14 -> 14, of which waited for: 10 -> 10; matrix products, arithmetic and copies ran while one was open for 2% -> 2% of each run, Pallas kernels for 15% -> 14%
where the time goes in v8:
time: 185 us; the launch traced here: 184 us
  waiting for transfers between devices  80.1 us (43%)
  starting transfers between devices  48.9 us (26%)
  Pallas kernels  45.7 us (25%)
  other arithmetic  5.23 us (3%)
  matrix products  1.97 us (1%)
    ppermute x6, waiting for transfers between devices, to_chip(): return lax.ppermute(value, 'col', [(c, c ^ 2 * step) for c in range(cols)])  43.3 us
    ppermute x4, starting transfers between devices, spread_step(): return lax.ppermute(own, ('row', 'col'), pairs)  38.9 us
    pallas_call x3, Pallas kernels, multiply(): pl.pallas_call(functools.partial(multiply_kernel, depth=slab_rows, span=s...  36.3 us
    ppermute x4, waiting for transfers between devices, spread_step(): return lax.ppermute(own, ('row', 'col'), pairs)  25.8 us
    ppermute x2, waiting for transfers between devices, tile_scatter(): held = mine + lax.ppermute(theirs, 'row', pairs)  8.76 us
    ppermute x6, starting transfers between devices, to_chip(): return lax.ppermute(value, 'col', [(c, c ^ 2 * step) for c in range(cols)])  8.1 us
    pallas_call x1, Pallas kernels, small_parts(): pl.pallas_call(small_kernel, in_specs=[scalars] * 2 + [whole] * 4, out_sp...  5.01 us
  transfers between devices with their start and end apart: 14, of which 10 were waited for; matrix products, arithmetic and copies ran while one was open for 2% of the time, Pallas kernels for 14%

profile of v8, /device:TPU:0, one launch (start us, length us, event | category | flops | bytes accessed | tf_op | source)
XLA Modules:
  0.0 184.5 jit_solution(10560043982725885075)
XLA Ops:
  0.7 2.1 %shard_map.111.rows = bf16[512,768]{1,0:T(8,128)(2,1)} custom-call(bf16[512,256]{1,0:T(8,128)(2,1)} %refs_0_.1, bf16[512,256]{1,0:T(8,128)(2,1)} %refs_1_.1, bf16[512,256]{1,0:T(8,128)(2,1)} %refs_2_.1), custom_call_target="tpu_custom_call" | custom-call | flops 1 | bytes 1 | tf_op jit(solution)/shard_map/pallas_call | solution.py:71
  2.7 1.8 collective-permute-start
  4.5 7.6 %collective-permute-start.1 = (bf16[512,768]{1,0:T(8,128)(2,1)}, bf16[512,768]{1,0:T(8,128)(2,1)S(1)}, u32[]{:S(2)}, u32[]{:S(2)}) collective-permute-start(bf16[512,768]{1,0:T(8,128)(2,1)} %shard_map.111.rows), channel_id=1, source_target_pairs={{0,8},{1,0},{2,24},{3,16},{4,9},{5,1},{6,25},{7,17},{8,26},{9,18},... | collective-permute-start | bytes 2359304 | tf_op jit(solution)/shard_map/ppermute | solution.py:43
  12.1 13.2 %collective-permute-done.1.refs_1_ = bf16[512,768]{1,0:T(8,128)(2,1)S(1)} collective-permute-done((bf16[512,768]{1,0:T(8,128)(2,1)}, bf16[512,768]{1,0:T(8,128)(2,1)S(1)}, u32[]{:S(2)}, u32[]{:S(2)}) %collective-permute-start.1) | collective-permute-done | bytes 786464 | tf_op jit(solution)/shard_map/ppermute | solution.py:43
  25.3 24.5 %collective-permute-start.2 = (bf16[512,768]{1,0:T(8,128)(2,1)}, bf16[512,768]{1,0:T(8,128)(2,1)S(1)}, u32[]{:S(2)}, u32[]{:S(2)}) collective-permute-start(bf16[512,768]{1,0:T(8,128)(2,1)} %shard_map.111.rows), channel_id=1, source_target_pairs={{0,16},{1,24},{2,0},{3,8},{4,17},{5,25},{6,1},{7,9},{8,2},{9,10},{... | collective-permute-start | bytes 2359304 | tf_op jit(solution)/shard_map/ppermute | solution.py:43
  49.8 5.1 %collective-permute-start.3 = (bf16[512,768]{1,0:T(8,128)(2,1)}, bf16[512,768]{1,0:T(8,128)(2,1)S(1)}, u32[]{:S(2)}, u32[]{:S(2)}) collective-permute-start(bf16[512,768]{1,0:T(8,128)(2,1)} %shard_map.111.rows), channel_id=1, source_target_pairs={{0,24},{1,16},{2,8},{3,0},{4,25},{5,17},{6,9},{7,1},{8,10},{9,2},{... | collective-permute-start | bytes 2359304 | tf_op jit(solution)/shard_map/ppermute | solution.py:43
  55.3 17.0 %shard_map.112.refs_2_ = f32[2,4,512,768]{3,2,1,0:T(8,128)S(1)} custom-call(s32[5]{0:T(128)S(1)} %stack.32.where, s32[3,64]{1,0:T(4,128)S(1)} %add_convert_fusion.keeps, f32[4096,2048]{1,0:T(8,128)} %s_ref.5, bf16[512,768]{1,0:T(8,128)(2,1)S(1)} %collective-permute-done.refs_0_, bf16[512,768]{1,0:T(8,128)(2,1)S(1)} %collective-permute-done.1.refs_1_), custom_call_target="tpu_custom_call" | custom-call | flops 1 | bytes 1 | tf_op jit(solution)/shard_map/pallas_call | solution.py:119
  72.3 12.5 %collective-permute-done.3.refs_1_ = bf16[512,768]{1,0:T(8,128)(2,1)S(1)} collective-permute-done((bf16[512,768]{1,0:T(8,128)(2,1)}, bf16[512,768]{1,0:T(8,128)(2,1)S(1)}, u32[]{:S(2)}, u32[]{:S(2)}) %collective-permute-start.3) | collective-permute-done | bytes 786464 | tf_op jit(solution)/shard_map/ppermute | solution.py:43
  84.9 9.7 %shard_map.113 = f32[1,4,512,768]{3,2,1,0:T(8,128)S(1)} custom-call(s32[5]{0:T(128)S(1)} %stack.32.where, s32[3,64]{1,0:T(4,128)S(1)} %add_convert_fusion.keeps, f32[4096,2048]{1,0:T(8,128)} %s_ref.5, bf16[512,768]{1,0:T(8,128)(2,1)S(1)} %collective-permute-done.2.refs_0_, bf16[512,768]{1,0:T(8,128)(2,1)S(1)} %collective-permute-done.3.refs_1_, ...), custom_call_target="tpu_custom_call" | custom-call | flops 1 | bytes 1 | tf_op jit(solution)/shard_map/pallas_call | solution.py:119
  94.7 9.7 %shard_map.114.mine_ref = f32[1,4,512,768]{3,2,1,0:T(8,128)S(1)} custom-call(s32[5]{0:T(128)S(1)} %stack.32.where, s32[3,64]{1,0:T(4,128)S(1)} %add_convert_fusion.keeps, f32[4096,2048]{1,0:T(8,128)} %s_ref.5, bf16[512,768]{1,0:T(8,128)(2,1)S(1)} %collective-permute-done.2.refs_0_, bf16[512,768]{1,0:T(8,128)(2,1)S(1)} %collective-permute-done.3.refs_1_, ...), custom_call_target="tpu_custom_call" | custom-call | flops 1 | bytes 1 | tf_op jit(solution)/shard_map/pallas_call | solution.py:119
  104.8 2.3 %shard_map.115 = (f32[528,768]{1,0:T(8,128)S(1)}, f32[3,528,768]{2,1,0:T(8,128)S(1)}) custom-call(s32[5]{0:T(128)S(1)} %stack.32.where, f32[1,4,512,768]{3,2,1,0:T(8,128)S(1)} %shard_map.114.mine_ref, f32[1,4,512,768]{3,2,1,0:T(8,128)S(1)} %collective-permute-done.4.handed_ref), custom_call_target="tpu_custom_call" | custom-call | flops 1 | bytes 1 | tf_op jit(solution)/shard_map/pallas_call | solution.py:165
  107.9 3.9 %collective-permute-start.7 = (f16[528,768]{1,0:T(8,128)(2,1)S(1)}, f16[528,768]{1,0:T(8,128)(2,1)S(1)}, u32[]{:S(2)}, u32[]{:S(2)}) collective-permute-start(f16[528,768]{1,0:T(8,128)(2,1)S(1)} %get-tuple-element.17), channel_id=1, source_target_pairs={{0,6},{1,7},{2,4},{3,5},{4,2},{5,3},{6,0},{7,1},{8,14},{9,15},{10,... | collective-permute-start | bytes 2433032 | tf_op jit(solution)/shard_map/ppermute | solution.py:190
  112.5 18.3 %collective-permute-done.7 = f16[528,768]{1,0:T(8,128)(2,1)S(1)} collective-permute-done((f16[528,768]{1,0:T(8,128)(2,1)S(1)}, f16[528,768]{1,0:T(8,128)(2,1)S(1)}, u32[]{:S(2)}, u32[]{:S(2)}) %collective-permute-start.7) | collective-permute-done | bytes 811040 | tf_op jit(solution)/shard_map/ppermute | solution.py:190
  130.8 16.8 %collective-permute-done.6 = f16[528,768]{1,0:T(8,128)(2,1)S(1)} collective-permute-done((f16[528,768]{1,0:T(8,128)(2,1)S(1)}, f16[528,768]{1,0:T(8,128)(2,1)S(1)}, u32[]{:S(2)}, u32[]{:S(2)}) %collective-permute-start.6) | collective-permute-done | bytes 811040 | tf_op jit(solution)/shard_map/ppermute | solution.py:190
  149.1 5.0 %shard_map.116 = (f32[4,6,32,256]{3,2,1,0:T(8,128)S(1)}, f32[4,6,32,256]{3,2,1,0:T(8,128)}) custom-call(s32[5]{0:T(128)S(1)} %stack.32.where, s32[3,64]{1,0:T(4,128)S(1)} %add_convert_fusion.keeps, f32[528,768]{1,0:T(8,128)S(1)} %fusion.sums, bf16[512,768]{1,0:T(8,128)(2,1)S(1)} %copy-done, bf16[3,256,256]{2,1,0:T(8,128)(2,1)S(1)} %copy-done.1, ...), custom_call_target="tpu_custom_call" | custom-call | flops 1 | bytes 1 | tf_op jit(solution)/shard_map/pallas_call | solution.py:289
  154.8 1.9 %collective-permute-done.8 = f32[4,6,32,256]{3,2,1,0:T(8,128)} collective-permute-done((f32[4,6,32,256]{3,2,1,0:T(8,128)}, f32[4,6,32,256]{3,2,1,0:T(8,128)}, u32[]{:S(2)}, u32[]{:S(2)}) %collective-permute-start.8) | collective-permute-done | bytes 786464 | tf_op jit(solution)/shard_map/ppermute | solution.py:186
  158.0 1.9 %collective-permute-start.11 = (f32[6,32,256]{2,1,0:T(8,128)S(1)}, f32[6,32,256]{2,1,0:T(8,128)S(1)}, u32[]{:S(2)}, u32[]{:S(2)}) collective-permute-start(f32[6,32,256]{2,1,0:T(8,128)S(1)} %get-tuple-element.20), channel_id=1, source_target_pairs={{0,6},{1,7},{2,4},{3,5},{4,2},{5,3},{6,0},{7,1},{8,14},{9,15},{10,... | collective-permute-start | bytes 589832 | tf_op jit(solution)/shard_map/ppermute | solution.py:190
  159.9 1.4 collective-permute-start.10
  161.9 4.8 %collective-permute-done.11 = f32[6,32,256]{2,1,0:T(8,128)S(1)} collective-permute-done((f32[6,32,256]{2,1,0:T(8,128)S(1)}, f32[6,32,256]{2,1,0:T(8,128)S(1)}, u32[]{:S(2)}, u32[]{:S(2)}) %collective-permute-start.11) | collective-permute-done | bytes 196640 | tf_op jit(solution)/shard_map/ppermute | solution.py:190
  166.7 3.4 %collective-permute-done.10 = f32[6,32,256]{2,1,0:T(8,128)S(1)} collective-permute-done((f32[6,32,256]{2,1,0:T(8,128)S(1)}, f32[6,32,256]{2,1,0:T(8,128)S(1)}, u32[]{:S(2)}, u32[]{:S(2)}) %collective-permute-start.10) | collective-permute-done | bytes 196640 | tf_op jit(solution)/shard_map/ppermute | solution.py:190
  171.1 1.6 collective-permute-start.12
  172.7 1.2 fusion.4
  173.9 5.0 %collective-permute-done.12 = f32[6,32,128]{2,1,0:T(8,128)S(1)} collective-permute-done((f32[6,32,128]{2,1,0:T(8,128)S(1)}, f32[6,32,128]{2,1,0:T(8,128)S(1)}, u32[]{:S(2)}, u32[]{:S(2)}) %collective-permute-start.12) | collective-permute-done | bytes 98336 | tf_op jit(solution)/shard_map/ppermute | solution.py:312
  180.0 3.8 %collective-permute-done.13 = f32[6,32,64]{2,1,0:T(8,128)S(1)} collective-permute-done((f32[6,32,64]{2,1,0:T(8,128)S(1)}, f32[6,32,64]{2,1,0:T(8,128)S(1)}, u32[]{:S(2)}, u32[]{:S(2)}) %collective-permute-start.13) | collective-permute-done | bytes 49184 | tf_op jit(solution)/shard_map/ppermute | solution.py:312
  (48 shorter events, 9.1 us)
Async XLA Ops:
  0.6 54.4 %copy-start.4 = (s32[60]{0:T(128)S(1)}, s32[60]{0:T(128)}, u32[]{:S(2)}) copy-start(s32[60]{0:T(128)} %param.14) | copy-start | bytes 724
  0.6 54.5 %copy-start.5 = (s32[56]{0:T(128)S(1)}, s32[56]{0:T(128)}, u32[]{:S(2)}) copy-start(s32[56]{0:T(128)} %param.15) | copy-start | bytes 676
  2.7 9.3 %collective-permute-start = (bf16[512,768]{1,0:T(8,128)(2,1)}, bf16[512,768]{1,0:T(8,128)(2,1)S(1)}, u32[]{:S(2)}, u32[]{:S(2)}) collective-permute-start(bf16[512,768]{1,0:T(8,128)(2,1)} %shard_map.111.rows), channel_id=1, source_target_pairs={{0,0},{1,8},{2,16},{3,24},{4,1},{5,9},{6,17},{7,25},{8,18},{9,26},... | collective-permute-start | bytes 2359304 | tf_op jit(solution)/shard_map/ppermute | solution.py:43
  4.5 20.8 %collective-permute-start.1 = (bf16[512,768]{1,0:T(8,128)(2,1)}, bf16[512,768]{1,0:T(8,128)(2,1)S(1)}, u32[]{:S(2)}, u32[]{:S(2)}) collective-permute-start(bf16[512,768]{1,0:T(8,128)(2,1)} %shard_map.111.rows), channel_id=1, source_target_pairs={{0,8},{1,0},{2,24},{3,16},{4,9},{5,1},{6,25},{7,17},{8,26},{9,18},... | collective-permute-start | bytes 2359304 | tf_op jit(solution)/shard_map/ppermute | solution.py:43
  25.3 47.0 %collective-permute-start.2 = (bf16[512,768]{1,0:T(8,128)(2,1)}, bf16[512,768]{1,0:T(8,128)(2,1)S(1)}, u32[]{:S(2)}, u32[]{:S(2)}) collective-permute-start(bf16[512,768]{1,0:T(8,128)(2,1)} %shard_map.111.rows), channel_id=1, source_target_pairs={{0,16},{1,24},{2,0},{3,8},{4,17},{5,25},{6,1},{7,9},{8,2},{9,10},{... | collective-permute-start | bytes 2359304 | tf_op jit(solution)/shard_map/ppermute | solution.py:43
  49.8 35.0 %collective-permute-start.3 = (bf16[512,768]{1,0:T(8,128)(2,1)}, bf16[512,768]{1,0:T(8,128)(2,1)S(1)}, u32[]{:S(2)}, u32[]{:S(2)}) collective-permute-start(bf16[512,768]{1,0:T(8,128)(2,1)} %shard_map.111.rows), channel_id=1, source_target_pairs={{0,24},{1,16},{2,8},{3,0},{4,25},{5,17},{6,9},{7,1},{8,10},{9,2},{... | collective-permute-start | bytes 2359304 | tf_op jit(solution)/shard_map/ppermute | solution.py:43
  94.5 10.2 %collective-permute-start.4 = (f32[1,4,512,768]{3,2,1,0:T(8,128)S(1)}, f32[1,4,512,768]{3,2,1,0:T(8,128)S(1)}, u32[]{:S(2)}, u32[]{:S(2)}) collective-permute-start(f32[1,4,512,768]{3,2,1,0:T(8,128)S(1)} %shard_map.113), channel_id=1, source_target_pairs={{0,1},{1,0},{2,3},{3,2},{4,5},{5,4},{6,7},{7,6},{8,9},{9,8},{10,11... | collective-permute-start | bytes 18874376 | tf_op jit(solution)/shard_map/ppermute | solution.py:186
  107.9 22.8 %collective-permute-start.7 = (f16[528,768]{1,0:T(8,128)(2,1)S(1)}, f16[528,768]{1,0:T(8,128)(2,1)S(1)}, u32[]{:S(2)}, u32[]{:S(2)}) collective-permute-start(f16[528,768]{1,0:T(8,128)(2,1)S(1)} %get-tuple-element.17), channel_id=1, source_target_pairs={{0,6},{1,7},{2,4},{3,5},{4,2},{5,3},{6,0},{7,1},{8,14},{9,15},{10,... | collective-permute-start | bytes 2433032 | tf_op jit(solution)/shard_map/ppermute | solution.py:190
  111.8 35.7 %collective-permute-start.6 = (f16[528,768]{1,0:T(8,128)(2,1)S(1)}, f16[528,768]{1,0:T(8,128)(2,1)S(1)}, u32[]{:S(2)}, u32[]{:S(2)}) collective-permute-start(f16[528,768]{1,0:T(8,128)(2,1)S(1)} %get-tuple-element.18), channel_id=1, source_target_pairs={{0,4},{1,5},{2,6},{3,7},{4,0},{5,1},{6,2},{7,3},{8,12},{9,13},{10,... | collective-permute-start | bytes 2433032 | tf_op jit(solution)/shard_map/ppermute | solution.py:190
  111.8 35.8 %collective-permute-start.5 = (f16[528,768]{1,0:T(8,128)(2,1)S(1)}, f16[528,768]{1,0:T(8,128)(2,1)S(1)}, u32[]{:S(2)}, u32[]{:S(2)}) collective-permute-start(f16[528,768]{1,0:T(8,128)(2,1)S(1)} %get-tuple-element.16), channel_id=1, source_target_pairs={{0,2},{1,3},{2,0},{3,1},{4,6},{5,7},{6,4},{7,5},{8,10},{9,11},{10,... | collective-permute-start | bytes 2433032 | tf_op jit(solution)/shard_map/ppermute | solution.py:190
  147.6 1.1 copy-start
  147.7 1.2 copy-start.1
  147.7 1.5 copy-start.2
  154.1 2.6 %collective-permute-start.8 = (f32[4,6,32,256]{3,2,1,0:T(8,128)}, f32[4,6,32,256]{3,2,1,0:T(8,128)}, u32[]{:S(2)}, u32[]{:S(2)}) collective-permute-start(f32[4,6,32,256]{3,2,1,0:T(8,128)} %get-tuple-element.15), channel_id=1, source_target_pairs={{0,1},{1,0},{2,3},{3,2},{4,5},{5,4},{6,7},{7,6},{8,9},{9,8},{10,11... | collective-permute-start | bytes 2359304 | tf_op jit(solution)/shard_map/ppermute | solution.py:186
  154.8 16.3 %copy-start.3 = (f32[512,256]{1,0:T(8,128)}, f32[512,256]{1,0:T(8,128)S(1)}, u32[]{:S(2)}) copy-start(f32[512,256]{1,0:T(8,128)S(1)} %fusion.6) | copy-start | bytes 1572868
  158.0 8.8 %collective-permute-start.11 = (f32[6,32,256]{2,1,0:T(8,128)S(1)}, f32[6,32,256]{2,1,0:T(8,128)S(1)}, u32[]{:S(2)}, u32[]{:S(2)}) collective-permute-start(f32[6,32,256]{2,1,0:T(8,128)S(1)} %get-tuple-element.20), channel_id=1, source_target_pairs={{0,6},{1,7},{2,4},{3,5},{4,2},{5,3},{6,0},{7,1},{8,14},{9,15},{10,... | collective-permute-start | bytes 589832 | tf_op jit(solution)/shard_map/ppermute | solution.py:190
  159.9 10.2 %collective-permute-start.10 = (f32[6,32,256]{2,1,0:T(8,128)S(1)}, f32[6,32,256]{2,1,0:T(8,128)S(1)}, u32[]{:S(2)}, u32[]{:S(2)}) collective-permute-start(f32[6,32,256]{2,1,0:T(8,128)S(1)} %get-tuple-element.21), channel_id=1, source_target_pairs={{0,4},{1,5},{2,6},{3,7},{4,0},{5,1},{6,2},{7,3},{8,12},{9,13},{10,... | collective-permute-start | bytes 589832 | tf_op jit(solution)/shard_map/ppermute | solution.py:190
  161.3 8.9 %collective-permute-start.9 = (f32[6,32,256]{2,1,0:T(8,128)S(1)}, f32[6,32,256]{2,1,0:T(8,128)S(1)}, u32[]{:S(2)}, u32[]{:S(2)}) collective-permute-start(f32[6,32,256]{2,1,0:T(8,128)S(1)} %get-tuple-element.19), channel_id=1, source_target_pairs={{0,2},{1,3},{2,0},{3,1},{4,6},{5,7},{6,4},{7,5},{8,10},{9,11},{10,... | collective-permute-start | bytes 589832 | tf_op jit(solution)/shard_map/ppermute | solution.py:190
  171.1 7.8 %collective-permute-start.12 = (f32[6,32,128]{2,1,0:T(8,128)S(1)}, f32[6,32,128]{2,1,0:T(8,128)S(1)}, u32[]{:S(2)}, u32[]{:S(2)}) collective-permute-start(f32[6,32,128]{2,1,0:T(8,128)S(1)} %constant_dynamic-slice_fusion), channel_id=1, source_target_pairs={{0,16},{8,24},{16,0},{24,8},{1,17},{9,25},{17,1},{25,9},{2,18},{10... | collective-permute-start | bytes 294920 | tf_op jit(solution)/shard_map/ppermute | solution.py:312
  179.0 4.7 %collective-permute-start.13 = (f32[6,32,64]{2,1,0:T(8,128)S(1)}, f32[6,32,64]{2,1,0:T(8,128)S(1)}, u32[]{:S(2)}, u32[]{:S(2)}) collective-permute-start(f32[6,32,64]{2,1,0:T(8,128)S(1)} %constant_dynamic-slice_fusion.1), channel_id=1, source_target_pairs={{0,8},{8,0},{16,24},{24,16},{1,9},{9,1},{17,25},{25,17},{2,10},{10... | collective-permute-start | bytes 147464 | tf_op jit(solution)/shard_map/ppermute | solution.py:312
